TPU v7x, 32 devices: a whole 2x2x4 slice. The times are simulated.
32 devices in a mesh: parts: 2 (over x), ep: 16 (over z, y, core).
Axes of the slice: x: 2, y: 2, z: 4, core: 2. Of those that a mesh axis runs over, the one named last changes fastest.
Arguments:
- tokens: bfloat16 [1, 256, 7168], P(None, ('parts', 'ep')), parts along dimension 1, may hold values from -6 to 6
- expert_ids: int32 [1, 256, 2], P(None, ('parts', 'ep')), parts along dimension 1, may hold values from 0 to 7, all different within a row; in each aligned block of 8 rows (0 to 7, 8 to 15, ..., all dimensions but the last counted through in order) at most 4 rows name the same one
- gate_weights: float32 [1, 256, 2], P(None, ('parts', 'ep')), parts along dimension 1, may hold values from 0.2 to 1
- w_gate: bfloat16 [16, 7168, 512], P('ep'), may hold values from -0.0625 to 0.0625
- scale_gate: bfloat16 [16, 56, 512], P('ep'), may hold values from 0.5 to 2
- w_up: bfloat16 [16, 7168, 512], P('ep'), may hold values from -0.0625 to 0.0625
- scale_up: bfloat16 [16, 56, 512], P('ep'), may hold values from 0.5 to 2
- w_down: bfloat16 [16, 512, 7168], P('ep'), may hold values from -0.1875 to 0.1875
- scale_down: bfloat16 [16, 4, 7168], P('ep'), may hold values from 0.5 to 2
- outlier_cols: int32 [8, 128], replicated, may hold values from 0 to 7167
- outlier_gate: bfloat16 [16, 128, 512], P('ep'), may hold values from -0.5 to 0.5
- outlier_up: bfloat16 [16, 128, 512], P('ep'), may hold values from -0.5 to 0.5
- shared_gate: bfloat16 [16, 7168, 512], P('ep'), as said below
- shared_up: bfloat16 [16, 7168, 512], P('ep'), as said below
- shared_down: bfloat16 [16, 512, 7168], P('ep'), as said below
Outputs:
- mixed: bfloat16 [1, 256, 7168], P(None, ('parts', 'ep')), parts along dimension 1
There are 2 independent parts, one for each index of `parts`. A program takes and returns all parts, laid end to end along the dimension named above; an argument that names none is the same for every part. Nothing has to cross between parts.
Inputs may be any that keep to these rules, and one draw needn't show every extreme that they name: `expert_ids`: each row names 2 different experts; among the rows of one device in one step no expert is named by more than 4 rows, and in some device's rows some expert is named exactly 4 times. `outlier_cols`: feature indices; an expert may repeat one. `shared_gate`: slices s and s + 2 are equal. `shared_up`: slices s and s + 2 are equal. `shared_down`: slices s and s + 2 are equal.
All inputs are finite; a program needn't handle non-finite values.
Results may differ from a plain program's by a relative error of at most 0.007.
Values may be sent and summed in bfloat16 or wider, within the bound.
No kernel may reach another device: no remote copies, remote signals or barrier semaphores. Data moves between devices by JAX's collectives and lax.ppermute only.
A program may use at most 192 MiB of HBM per device.

v0:
```python
import jax
import jax.numpy as jnp
from jax import lax
from jax.sharding import PartitionSpec as P

FF = 1024
TOPK = 2


def partner(block, axis, apart):
    count = lax.axis_size(axis)
    route = []
    for low in range(count):
        high = low | 1 << apart
        if high != low and high < count:
            route += [(low, high), (high, low)]
    return lax.ppermute(block, axis, route)


def dequant(codes, scales):
    height, breadth = codes.shape
    blocks = scales.shape[0]
    scaled = (
        codes.astype(jnp.float32).reshape(blocks, height // blocks, breadth)
        * scales.astype(jnp.float32)[:, None, :]
    )
    return scaled.reshape(height, breadth).astype(jnp.bfloat16)


def split_inputs(inputs, columns):
    width = inputs.shape[-1]
    hits = jnp.any(jnp.arange(width, dtype=jnp.int32)[None, :] == columns[:, None], axis=0)
    masked = jnp.where(hits[None, :], jnp.zeros((), inputs.dtype), inputs)
    picked = jnp.take(inputs, columns, axis=1)
    return (masked, picked)


def expert_rows(flat, weights):
    gate_matrix, up_matrix, down_matrix, extra_gate, extra_up, columns = weights
    masked, picked = split_inputs(flat, columns)
    gate_val = jnp.dot(masked, gate_matrix, preferred_element_type=jnp.float32) + jnp.dot(
        picked, extra_gate, preferred_element_type=jnp.float32
    )
    up_val = jnp.dot(masked, up_matrix, preferred_element_type=jnp.float32) + jnp.dot(
        picked, extra_up, preferred_element_type=jnp.float32
    )
    hidden = (jax.nn.silu(gate_val) * up_val).astype(jnp.bfloat16)
    return jnp.dot(hidden, down_matrix, preferred_element_type=jnp.float32)


def shared_rows(flat, gate_matrix, up_matrix, down_matrix):
    gate_val = jnp.dot(flat, gate_matrix, preferred_element_type=jnp.float32)
    up_val = jnp.dot(flat, up_matrix, preferred_element_type=jnp.float32)
    hidden = (jax.nn.silu(gate_val) * up_val).astype(jnp.bfloat16)
    return jnp.dot(hidden, down_matrix, preferred_element_type=jnp.float32)


def make_slots(keys, key_count, capacity, current, weights):
    row_count, top = weights.shape
    key_range = jnp.arange(key_count, dtype=jnp.int32)
    onehot = (keys[:, None] == key_range[None, :]).astype(jnp.int32)
    before = jnp.cumsum(onehot, axis=0) - onehot
    position = jnp.sum(before * onehot, axis=1)
    slot_index = keys * capacity + position
    slot_range = jnp.arange(key_count * capacity, dtype=jnp.int32)
    matches = (slot_range[:, None] == slot_index[None, :]).reshape(
        key_count * capacity, row_count, top
    )
    chooser = jnp.any(matches, axis=2).astype(jnp.bfloat16)
    outbound = jnp.dot(chooser, current, preferred_element_type=jnp.float32).astype(jnp.bfloat16)
    combine_weights = jnp.sum(jnp.where(matches, weights[None], 0.0), axis=2).T
    return (outbound, combine_weights)


def on_device(
    tokens,
    expert_ids,
    gate_weights,
    w_gate,
    scale_gate,
    w_up,
    scale_up,
    w_down,
    scale_down,
    outlier_cols,
    outlier_gate,
    outlier_up,
    shared_gate,
    shared_up,
    shared_down,
):
    devices = lax.axis_size("ep")
    device = lax.axis_index("ep")
    hidden_units = w_gate.shape[2]
    group_size = FF // hidden_units
    experts = devices // group_size
    group_bits = group_size.bit_length() - 1
    row_count = tokens.shape[1]
    feature_count = tokens.shape[2]
    capacity = max(2, row_count * TOPK * 2 // experts)
    home_group = device // group_size
    home_weights = (
        dequant(w_gate[0], scale_gate[0]),
        dequant(w_up[0], scale_up[0]),
        dequant(w_down[0], scale_down[0]),
        outlier_gate[0],
        outlier_up[0],
        lax.dynamic_index_in_dim(outlier_cols, home_group, 0, keepdims=False),
    )
    shared_gate_local, shared_up_local, shared_down_local = (
        shared_gate[0],
        shared_up[0],
        shared_down[0],
    )
    current = tokens[0]
    routed_ids = expert_ids[0].reshape(row_count * TOPK)
    weights = gate_weights[0]
    gathered = current[None]
    for bit_index in range(group_bits):
        incoming = partner(gathered, "ep", bit_index)
        lower_half = device >> bit_index & 1 == 0
        gathered = jnp.where(
            lower_half,
            jnp.concatenate([gathered, incoming], axis=0),
            jnp.concatenate([incoming, gathered], axis=0),
        )
    shared_part = shared_rows(
        gathered.reshape(-1, feature_count), shared_gate_local, shared_up_local, shared_down_local
    ).reshape(group_size, row_count, feature_count)
    for bit_index in reversed(range(group_bits)):
        halves = shared_part.reshape(2, shared_part.shape[0] // 2, row_count, feature_count)
        lower_half = device >> bit_index & 1 == 0
        retained = jnp.where(lower_half, halves[0], halves[1])
        outgoing = jnp.where(lower_half, halves[1], halves[0])
        shared_part = retained + partner(outgoing.astype(jnp.bfloat16), "ep", bit_index).astype(
            outgoing.dtype
        )
    shared_out = shared_part[0]
    outbound, combine_weights = make_slots(routed_ids, experts, capacity, current, weights)
    spread = jnp.broadcast_to(
        outbound.reshape(experts, 1, 1, capacity, feature_count),
        (experts, group_size, 1, capacity, feature_count),
    ).reshape(devices, 1, capacity, feature_count)
    arrived_rows = lax.all_to_all(spread, "ep", split_axis=0, concat_axis=0, tiled=True)
    partial_value = (
        expert_rows(arrived_rows.reshape(-1, feature_count), home_weights)
        .reshape(arrived_rows.shape)
        .astype(jnp.bfloat16)
    )
    slot_total = partial_value.shape[1] * partial_value.shape[2]
    returned = lax.all_to_all(partial_value, "ep", split_axis=0, concat_axis=0, tiled=True)
    outputs = jnp.sum(
        returned.astype(jnp.float32).reshape(experts, group_size, slot_total, feature_count), axis=1
    )
    routed = jnp.dot(
        combine_weights,
        outputs.reshape(experts * slot_total, feature_count),
        precision=lax.Precision.HIGHEST,
        preferred_element_type=jnp.float32,
    )
    results = [(routed + shared_out).astype(jnp.bfloat16)]
    return jnp.stack(results, axis=0)


def solution(mesh):
    placed = (
        P(None, ("parts", "ep"), None),
        P(None, ("parts", "ep"), None),
        P(None, ("parts", "ep"), None),
        P("ep", None, None),
        P("ep", None, None),
        P("ep", None, None),
        P("ep", None, None),
        P("ep", None, None),
        P("ep", None, None),
        P(),
        P("ep", None, None),
        P("ep", None, None),
        P("ep", None, None),
        P("ep", None, None),
        P("ep", None, None),
    )
    return jax.shard_map(
        on_device,
        mesh=mesh,
        in_specs=placed,
        out_specs=P(None, ("parts", "ep"), None),
        check_vma=False,
    )
```

profile of v0, /device:TPU:0, one launch (start us, length us, event | category | flops | bytes accessed | tf_op | source)
XLA Modules:
  0.0 90.1 jit_solution(14484175358385053079)
XLA Ops:
  0.0 0.5 collective-permute-start
  0.5 0.8 copy.45
  1.8 0.7 bitcast_add_fusion.2
  2.5 1.2 %convolution_convert_fusion.1 = bf16[32,7168]{1,0:T(8,128)(2,1)S(1)} fusion(pred[32,8]{0,1:T(8,128)(4,1)S(1)} %fusion.41, bf16[1,8,7168]{2,1,0:T(8,128)(2,1)} %param.15), kind=kOutput, calls=%fused_computation.9 | convolution fusion | flops 3899392 | bytes 573696 | tf_op jit(solution)/shard_map/dot_general | solution.py:70
  3.9 1.2 %broadcast_in_dim.60 = bf16[8,2,4,7168]{3,2,1,0:T(4,128)(2,1)} broadcast(bf16[8,4,7168]{2,1,0:T(4,128)(2,1)S(1)} %broadcast_in_dim.59), dimensions={0,2,3} | broadcast | bytes 1376256 | tf_op jit(solution)/shard_map/broadcast_in_dim | solution.py:140
  5.1 7.0 %all-to-all-start = ((bf16[16,1,4,7168]{3,2,1,0:T(4,128)(2,1)}), bf16[16,1,4,7168]{3,2,1,0:T(4,128)(2,1)S(1)}, u32[]{:S(2)}, u32[]{:S(2)}) async-start(bf16[16,1,4,7168]{3,2,1,0:T(4,128)(2,1)} %bitcast.4), calls=%async_computation | async-start | bytes 1835008 | tf_op jit(solution)/shard_map/all_to_all | solution.py:144
  12.2 0.7 fusion.42
  12.9 0.7 compare_and_fusion
  13.6 0.6 fusion.10
  14.2 0.8 bitcast_convert_fusion.2
  15.0 1.0 %bitcast_convert_fusion.1 = f32[56,512]{1,0:T(8,128)S(1)} fusion(bf16[1,56,512]{2,1,0:T(8,128)(2,1)} %param.21), kind=kLoop, calls=%fused_computation.41 | loop fusion | flops 28672 | bytes 172032 | tf_op jit(solution)/shard_map/convert_element_type | solution.py:25
  16.0 1.1 %bitcast_convert_fusion = f32[4,7168]{1,0:T(4,128)S(1)} fusion(bf16[1,4,7168]{2,1,0:T(4,128)(2,1)} %param.23), kind=kLoop, calls=%fused_computation.40 | loop fusion | flops 28672 | bytes 172032 | tf_op jit(solution)/shard_map/convert_element_type | solution.py:25
  17.1 8.8 %fusion.2 = bf16[56,128,512]{2,1,0:T(8,128)(2,1)} fusion(bf16[56,128,512]{2,1,0:T(8,128)(2,1)} %bitcast.95, f32[56,512]{1,0:T(8,128)S(1)} %bitcast_convert_fusion.2), kind=kLoop, calls=%fused_computation.6 | loop fusion | flops 11010048 | bytes 14794752 | tf_op jit(solution)/shard_map/convert_element_type | solution.py:27
  25.9 4.7 %fusion = bf16[4,128,7168]{2,1,0:T(8,128)(2,1)} fusion(bf16[4,128,7168]{2,1,0:T(8,128)(2,1)S(1)} %bitcast.98, f32[4,7168]{1,0:T(4,128)S(1)} %bitcast_convert_fusion), kind=kLoop, calls=%fused_computation.2 | loop fusion | flops 11010048 | bytes 14794752 | tf_op jit(solution)/shard_map/convert_element_type | solution.py:27
  30.6 8.5 %fusion.1 = bf16[56,128,512]{2,1,0:T(8,128)(2,1)} fusion(bf16[56,128,512]{2,1,0:T(8,128)(2,1)} %bitcast.99, f32[56,512]{1,0:T(8,128)S(1)} %bitcast_convert_fusion.1), kind=kLoop, calls=%fused_computation.4 | loop fusion | flops 11010048 | bytes 14794752 | tf_op jit(solution)/shard_map/convert_element_type | solution.py:27
  39.2 4.2 %fusion.8 = f32[16,512]{1,0:T(8,128)S(1)} fusion(bf16[1,7168,512]{2,1,0:T(8,128)(2,1)} %param.27, bf16[1,8,7168]{2,1,0:T(8,128)(2,1)S(1)} %collective-permute-done, bf16[1,8,7168]{2,1,0:T(8,128)(2,1)S(1)} %copy-done.1, pred[]{:T(512)S(6)} %eq.59), kind=kOutput, calls=%fused_computation.14 | convolution fusion | flops 117784576 | bytes 7602177 | tf_op jit(solution)/shard_map/dot_general | solution.py:52
  43.6 1.7 %copy.47 = bf16[64,7168]{0,1:T(8,128)(2,1)} copy(bf16[64,7168]{1,0:T(8,128)(2,1)S(1)} %reshape.201) | data formatting | bytes 1835008 | tf_op jit(solution)/shard_map/reshape | solution.py:146
  45.3 0.4 broadcast_select_fusion
  45.9 2.4 %gather_fusion = bf16[128,64]{1,0:T(8,128)(2,1)S(1)} fusion(bf16[64,7168]{0,1:T(8,128)(2,1)} %copy.47, s32[1024]{0:T(1024)S(1)} %pad_clamp_fusion), kind=kCustom, calls=%fused_computation | custom fusion | bytes 33280 | tf_op jit(solution)/shard_map/jit(_take)/gather | solution.py:34
  48.6 0.3 fusion.23
  48.9 4.7 %convolution_add_fusion.1 = f32[64,512]{1,0:T(8,128)S(1)} fusion(f32[64,512]{1,0:T(8,128)S(1)} %fusion.25, bf16[64,7168]{1,0:T(8,128)(2,1)S(1)} %select_n.83, bf16[7168,512]{1,0:T(8,128)(2,1)} %bitcast.90), kind=kOutput, calls=%fused_computation.21 | convolution fusion | flops 469794816 | bytes 8519680 | tf_op jit(solution)/shard_map/dot_general | solution.py:41
  53.7 1.4 %fusion.12 = bf16[64,512]{1,0:T(8,128)(2,1)S(1)} fusion(f32[64,512]{1,0:T(8,128)S(1)} %fusion.23, bf16[64,7168]{1,0:T(8,128)(2,1)S(1)} %select_n.83, bf16[7168,512]{1,0:T(8,128)(2,1)S(1)} %bitcast.93, f32[64,512]{1,0:T(8,128)S(1)} %convolution_add_fusion.1), kind=kOutput, calls=%fused_computation.22 | convolution fusion | flops 469991424 | bytes 8585216 | tf_op jit(solution)/shard_map/dot_general | solution.py:44
  55.1 4.5 %fusion.3 = bf16[16,1,4,7168]{3,0,2,1:T(8,128)(2,1)S(1)} fusion(bf16[512,7168,1]{1,0,2:T(8,128)(2,1)} %bitcast.94, bf16[16,4,512]{2,1,0:T(4,128)(2,1)S(1)} %dot_general.37), kind=kOutput, calls=%fused_computation.8 | convolution fusion | flops 470220800 | bytes 8323072 | tf_op jit(solution)/shard_map/dot_general | solution.py:48
  59.6 1.6 %copy.49 = bf16[16,1,4,7168]{3,2,1,0:T(4,128)(2,1)} copy(bf16[16,1,4,7168]{3,0,2,1:T(8,128)(2,1)S(1)} %fusion.3) | data formatting | bytes 1835008 | tf_op jit(solution)/shard_map/convert_element_type | solution.py:148
  61.2 6.0 %all-to-all-start.1 = ((bf16[16,1,4,7168]{3,2,1,0:T(4,128)(2,1)}), bf16[16,1,4,7168]{3,2,1,0:T(4,128)(2,1)S(1)}, u32[]{:S(2)}, u32[]{:S(2)}) async-start(bf16[16,1,4,7168]{3,2,1,0:T(4,128)(2,1)} %copy.49), calls=%async_computation.1 | async-start | bytes 1835008 | tf_op jit(solution)/shard_map/all_to_all | solution.py:151
  67.2 7.3 %fusion.4 = f32[16,7168]{1,0:T(8,128)S(1)} fusion(bf16[1,512,7168]{2,1,0:T(8,128)(2,1)} %param.29, bf16[1,7168,512]{2,1,0:T(8,128)(2,1)} %param.28, bf16[1,8,7168]{2,1,0:T(8,128)(2,1)S(1)} %collective-permute-done, bf16[1,8,7168]{2,1,0:T(8,128)(2,1)S(1)} %copy-done.1, pred[]{:T(512)S(6)} %eq.59, f32[16,512]{1,0:T(8,128)S(1)} %fusion.8), kind=kOutput, calls=%fused_computation.10 | convolution fusion | flops 235274240 | bytes 15400961 | tf_op jit(solution)/shard_map/dot_general | solution.py:55
  74.5 0.5 collective-permute-start.1
  75.0 13.0 %all-to-all-done.1 = bf16[16,1,4,7168]{3,2,1,0:T(4,128)(2,1)S(1)} async-done(((bf16[16,1,4,7168]{3,2,1,0:T(4,128)(2,1)}), bf16[16,1,4,7168]{3,2,1,0:T(4,128)(2,1)S(1)}, u32[]{:S(2)}, u32[]{:S(2)}) %all-to-all-start.1) | async-done | bytes 917536 | tf_op jit(solution)/shard_map/all_to_all | solution.py:151
  88.0 0.5 convert_reduce_fusion
  88.6 0.3 reshape.204
  88.9 0.5 fusion.51
  89.4 0.7 fusion.28
  (36 shorter events, 1.7 us)
Async XLA Ops:
  0.0 48.3 %copy-start = (bf16[1,128,512]{2,1,0:T(8,128)(2,1)S(1)}, bf16[1,128,512]{2,1,0:T(8,128)(2,1)}, u32[]{:S(2)}) copy-start(bf16[1,128,512]{2,1,0:T(8,128)(2,1)} %param.25) | copy-start | bytes 393220
  0.0 39.2 %collective-permute-start = (bf16[1,8,7168]{2,1,0:T(8,128)(2,1)}, bf16[1,8,7168]{2,1,0:T(8,128)(2,1)S(1)}, u32[]{:S(2)}, u32[]{:S(2)}) collective-permute-start(bf16[1,8,7168]{2,1,0:T(8,128)(2,1)} %param.15), channel_id=1, source_target_pairs={{0,1},{1,0},{2,3},{3,2},{4,5},{5,4},{6,7},{7,6},{8,9},{9,8},{10,11... | collective-permute-start | bytes 344072 | tf_op jit(solution)/shard_map/ppermute | solution.py:17
  5.1 38.2 %all-to-all-start = ((bf16[16,1,4,7168]{3,2,1,0:T(4,128)(2,1)}), bf16[16,1,4,7168]{3,2,1,0:T(4,128)(2,1)S(1)}, u32[]{:S(2)}, u32[]{:S(2)}) async-start(bf16[16,1,4,7168]{3,2,1,0:T(4,128)(2,1)} %bitcast.4), calls=%async_computation | async-start | bytes 1835008 | tf_op jit(solution)/shard_map/all_to_all | solution.py:144
  15.0 10.9 %slice-start.2 = ((s8[7340032]{0:T(1024)(128)(4,1)}), s8[4194304]{0:T(1024)(128)(4,1)S(1)}, s32[]{:S(2)}) async-start(s8[7340032]{0:T(1024)(128)(4,1)} %bitcast.96), calls=%async_computation.4 | async-start | bytes 8388608
  17.1 8.8 %slice-start.3 = ((s8[7340032]{0:T(1024)(128)(4,1)}), s8[3145728]{0:T(1024)(128)(4,1)S(1)}, s32[]{:S(2)}) async-start(s8[7340032]{0:T(1024)(128)(4,1)} %bitcast.96), calls=%async_computation.5 | async-start | bytes 6291456
  30.6 8.6 %copy-start.3 = (f32[1,8,2]{1,2,0:T(2,128)S(1)}, f32[1,8,2]{1,2,0:T(2,128)}, u32[]{:S(2)}) copy-start(f32[1,8,2]{1,2,0:T(2,128)} %param.17) | copy-start | bytes 196
  30.6 8.6 %copy-start.1 = (bf16[1,8,7168]{2,1,0:T(8,128)(2,1)S(1)}, bf16[1,8,7168]{2,1,0:T(8,128)(2,1)}, u32[]{:S(2)}) copy-start(bf16[1,8,7168]{2,1,0:T(8,128)(2,1)} %param.15) | copy-start | bytes 344068
  39.2 9.4 %copy-start.2 = (bf16[1,128,512]{2,1,0:T(8,128)(2,1)S(1)}, bf16[1,128,512]{2,1,0:T(8,128)(2,1)}, u32[]{:S(2)}) copy-start(bf16[1,128,512]{2,1,0:T(8,128)(2,1)} %param.26) | copy-start | bytes 393220
  48.3 5.3 %slice-start = ((s8[7340032]{0:T(1024)(128)(4,1)}), s8[4194304]{0:T(1024)(128)(4,1)S(1)}, s32[]{:S(2)}) async-start(s8[7340032]{0:T(1024)(128)(4,1)} %bitcast.91), calls=%async_computation.2 | async-start | bytes 8388608
  48.8 4.9 %slice-start.1 = ((s8[7340032]{0:T(1024)(128)(4,1)}), s8[3145728]{0:T(1024)(128)(4,1)S(1)}, s32[]{:S(2)}) async-start(s8[7340032]{0:T(1024)(128)(4,1)} %bitcast.91), calls=%async_computation.3 | async-start | bytes 6291456
  61.2 26.8 %all-to-all-start.1 = ((bf16[16,1,4,7168]{3,2,1,0:T(4,128)(2,1)}), bf16[16,1,4,7168]{3,2,1,0:T(4,128)(2,1)S(1)}, u32[]{:S(2)}, u32[]{:S(2)}) async-start(bf16[16,1,4,7168]{3,2,1,0:T(4,128)(2,1)} %copy.49), calls=%async_computation.1 | async-start | bytes 1835008 | tf_op jit(solution)/shard_map/all_to_all | solution.py:151
  74.5 14.9 %collective-permute-start.1 = (bf16[1,8,7168]{2,1,0:T(8,128)(2,1)S(1)}, bf16[1,8,7168]{2,1,0:T(8,128)(2,1)S(1)}, u32[]{:S(2)}, u32[]{:S(2)}) collective-permute-start(bf16[1,8,7168]{2,1,0:T(8,128)(2,1)S(1)} %fusion.27), channel_id=1, source_target_pairs={{0,1},{1,0},{2,3},{3,2},{4,5},{5,4},{6,7},{7,6},{8,9},{9,8},{10,11... | collective-permute-start | bytes 344072 | tf_op jit(solution)/shard_map/ppermute | solution.py:17
where the time goes:
time: 91.2 us; the launch traced here: 90.1 us
  other arithmetic  29.7 us (33%)
  matrix products  24.3 us (27%)
  starting transfers between devices  14 us (15%)
  waiting for transfers between devices  13.1 us (14%)
  local copies, waits for them, and re-layouts  8.98 us (10%)
    convert_element_type x3, other arithmetic, dequant(): return scaled.reshape(height, breadth).astype(jnp.bfloat16)  22 us
    all_to_all x1, waiting for transfers between devices, on_device(): lax.all_to_all(partial_value, 'ep', split_axis=0, concat_axis=0, tiled=True)  13 us
    dot_general x1, matrix products, shared_rows(): return jnp.dot(hidden, down_matrix, preferred_element_type=jnp.float32)  7.26 us
    all_to_all x1, starting transfers between devices, on_device(): lax.all_to_all(spread, 'ep', split_axis=0, concat_axis=0, tiled=True)  7.05 us
    all_to_all x1, starting transfers between devices, on_device(): lax.all_to_all(partial_value, 'ep', split_axis=0, concat_axis=0, tiled=True)  5.99 us
    dot_general x1, matrix products, expert_rows(): jnp.dot(masked, gate_matrix, preferred_element_type=jnp.float32)  4.72 us
    dot_general x1, matrix products, expert_rows(): return jnp.dot(hidden, down_matrix, preferred_element_type=jnp.float32)  4.47 us
    dot_general x1, matrix products, shared_rows(): gate_val = jnp.dot(flat, gate_matrix, preferred_element_type=jnp.float32)  4.16 us
  transfers between devices with their start and end apart: 4, of which 1 were waited for; matrix products, arithmetic and copies ran while one was open for 49% of the time, Pallas kernels for 0%

commit v1 on v0

v1 whole, which is shorter than its diff:
```python
import functools

import jax
import jax.numpy as jnp
from jax import lax
from jax.experimental import pallas as pl
from jax.experimental.pallas import tpu as pltpu
from jax.sharding import PartitionSpec as P

FF = 1024
TOPK = 2
TILE = 16
BF16 = jnp.bfloat16
F32 = jnp.float32
VMEM = pl.BlockSpec(memory_space=pltpu.VMEM)
ANY = pl.BlockSpec(memory_space=pl.ANY)
SMEM = pl.BlockSpec(memory_space=pltpu.SMEM)


def params(mib):
    return pltpu.CompilerParams(vmem_limit_bytes=mib << 20)


def cost(flops, nbytes):
    return pl.CostEstimate(flops=int(flops), bytes_accessed=int(nbytes), transcendentals=0)


def matmul(left, right):
    return jnp.dot(left, right, preferred_element_type=F32)


def in_hbm(array):
    return pltpu.with_memory_space_constraint(array, pltpu.HBM)


def iota(shape, dim):
    return lax.broadcasted_iota(jnp.int32, shape, dim)


def slot_codes(ids_ref, home, rows, capacity):
    ids = [ids_ref[t, r] for r in range(rows) for t in range(TOPK)]
    codes = []
    for n, e in enumerate(ids):
        place = jnp.int32(0)
        for earlier in ids[:n]:
            place += (earlier == e).astype(jnp.int32)
        codes.append((e ^ home) * capacity + place)
    return codes


def by_row(values, position, rows, choice):
    out = jnp.zeros(position.shape, values[0].dtype)
    for r in range(rows):
        out = jnp.where(position == r, values[r * TOPK + choice], out)
    return out


def send_kernel(cap, order, ids_ref, home_ref, tokens_hbm, *refs):
    blocks, (tokens_ref, stacked, sem) = refs[:-3], refs[-3:]
    copy = pltpu.make_async_copy(tokens_hbm, tokens_ref, sem)
    copy.start()
    rows = tokens_ref.shape[0]
    parts = TILE // cap
    width = tokens_ref.shape[1] // parts
    codes = slot_codes(ids_ref, home_ref[0], rows, cap)
    shape = (len(blocks) * TILE, parts * rows)
    j, lane = iota(shape, 0), iota(shape, 1)
    code = j // TILE * cap + j % cap
    same = j % TILE // cap == lane // rows
    position = iota((1, parts * rows), 1) % rows
    hit = jnp.zeros(shape, F32)
    for t in range(TOPK):
        hit += jnp.where(same & (code == by_row(codes, position, rows, t)), 1.0, 0.0)
    copy.wait()
    for q in range(parts):
        stacked[q * rows : (q + 1) * rows, :] = tokens_ref[
            :, q * width : (q + 1) * width
        ].astype(F32)
    chosen = matmul(hit.astype(BF16), stacked[...].astype(BF16)).astype(BF16)
    for m, block in zip(order, blocks):
        block[...] = chosen[m * TILE : (m + 1) * TILE]


def sorted_blocks(order, refs):
    return [refs[order.index(m)] for m in range(len(order))]


def unpack_kernel(cap, order, *refs):
    blocks, out = sorted_blocks(order, refs[:-1]), refs[-1]
    count, parts = len(blocks), TILE // cap
    slots, width = count * cap, blocks[0].shape[1]
    shape = (parts * slots, count * TILE)
    i, j = iota(shape, 0), iota(shape, 1)
    source = i % slots // cap * TILE + i // slots * cap + i % cap
    arranged = matmul(
        jnp.where(source == j, 1.0, 0.0).astype(BF16),
        jnp.concatenate([b[...] for b in blocks], axis=0),
    ).astype(BF16)
    for q in range(parts):
        out[:, q * width : (q + 1) * width] = arranged[q * slots : (q + 1) * slots]


def pack_kernel(cap, order, mine_ref, other_ref, *blocks):
    count, parts = len(blocks), TILE // cap
    slots, width = count * cap, mine_ref.shape[1] // parts
    total = (mine_ref[...].astype(F32) + other_ref[...].astype(F32)).astype(BF16)
    shape = (count * TILE, parts * slots)
    j, i = iota(shape, 0), iota(shape, 1)
    source = j % TILE // cap * slots + j // TILE * cap + j % cap
    arranged = matmul(
        jnp.where(source == i, 1.0, 0.0).astype(BF16),
        jnp.concatenate([total[:, q * width : (q + 1) * width] for q in range(parts)], axis=0),
    ).astype(BF16)
    for m, block in zip(order, blocks):
        block[...] = arranged[m * TILE : (m + 1) * TILE]


def prepare_kernel(
    step, tall, wg, wu, wd, sg, su, sd, cols, gate, up, down, onehot, keep, gate_scale, up_scale, sems
):
    chunks = wg.shape[0] // step
    block = wg.shape[0] // sg.shape[0]
    heights = wd.shape[0] // tall

    def moved(k, source, target, start, size):
        here = pl.ds(start, size)
        return pltpu.make_async_copy(source.at[here], target.at[here], sems.at[k])

    gates = [moved(c, wg, gate, c * step, step) for c in range(chunks)]
    ups = [moved(chunks + c, wu, up, c * step, step) for c in range(chunks)]
    downs = [moved(2 * chunks + c, wd, down, c * tall, tall) for c in range(heights)]
    for c in range(chunks):
        gates[c].start()
        ups[c].start()
    for copy in downs:
        copy.start()

    gate_scale[...] = sg[...].astype(F32)
    up_scale[...] = su[...].astype(F32)
    outliers = cols.shape[1]
    for c in range(chunks):
        here = slice(c * step, (c + 1) * step)
        hot = jnp.where(iota((step, outliers), 0) + c * step == cols[...], 1.0, 0.0).astype(BF16)
        onehot[here, :] = hot
        count = lax.dot_general(
            jnp.ones((8, outliers), BF16), hot, (((1,), (1,)), ((), ())), preferred_element_type=F32
        )
        keep[:, here] = jnp.where(count == 0.0, 1.0, 0.0)

    for c in range(chunks):
        for copy, target, scale in ((gates[c], gate, gate_scale), (ups[c], up, up_scale)):
            copy.wait()

            @pl.loop(0, step // block)
            def _(b):
                n = c * (step // block) + b
                here = pl.ds(pl.multiple_of(n * block, block), block)
                factor = scale[pl.ds(n, 1), :].astype(BF16)
                target[here, :] = target[here, :] * jnp.broadcast_to(factor, (block, factor.shape[1]))

    unit = wd.shape[0] // sd.shape[0]
    for c in range(heights):
        downs[c].wait()
        n = c * tall // unit
        factor = sd[...].astype(F32)[n : n + 1, :].astype(BF16)

        @pl.loop(0, tall // TILE)
        def _(b):
            here = pl.ds(pl.multiple_of(c * tall + b * TILE, TILE), TILE)
            down[here, :] = down[here, :] * jnp.broadcast_to(factor, (TILE, factor.shape[1]))


def expert_kernel(chunk, wide, gate, up, down, onehot, keep, extra_gate, extra_up, *refs):
    count = (len(refs) - 4) // 2
    pieces, outs = refs[:count], refs[count : 2 * count]
    gate_acc, up_acc, picked, hidden_ref = refs[2 * count :]
    height = pieces[0].shape[0]
    gate_acc[...] = jnp.zeros_like(gate_acc)
    up_acc[...] = jnp.zeros_like(up_acc)
    picked[...] = jnp.zeros_like(picked)

    @pl.loop(0, gate.shape[0] // chunk)
    def _(i):
        here = pl.ds(pl.multiple_of(i * chunk, chunk), chunk)
        whole = jnp.concatenate([piece[:, here] for piece in pieces], axis=0)
        kept = keep[:, here][0:1].astype(BF16)
        masked = whole * jnp.broadcast_to(kept, whole.shape)
        picked[...] += matmul(whole, onehot[here, :])
        gate_acc[...] += matmul(masked, gate[here, :])
        up_acc[...] += matmul(masked, up[here, :])

    outliers = picked[...].astype(BF16)
    gate_val = gate_acc[...] + matmul(outliers, extra_gate[...])
    up_val = up_acc[...] + matmul(outliers, extra_up[...])
    hidden_ref[...] = (gate_val / (1.0 + jnp.exp(-gate_val)) * up_val).astype(BF16)

    @pl.loop(0, down.shape[1] // wide)
    def _(i):
        here = pl.ds(pl.multiple_of(i * wide, wide), wide)
        result = matmul(hidden_ref[...], down[:, here]).astype(BF16)
        for n, out in enumerate(outs):
            out[:, here] = result[n * height : (n + 1) * height]


def shared_kernel(step, tall, wide, wg, wu, wd, *refs):
    count = (len(refs) - 8) // 2
    pieces, outs = refs[:count], refs[count : 2 * count]
    gate, up, down, rows_ref, gate_acc, up_acc, hidden_ref, sems = refs[2 * count :]
    height = pieces[0].shape[0]
    chunks, heights = wg.shape[0] // step, wd.shape[0] // tall

    def moved(k, source, target, start, size):
        here = pl.ds(start, size)
        return pltpu.make_async_copy(source.at[here], target.at[here], sems.at[k])

    gates = [moved(c, wg, gate, c * step, step) for c in range(chunks)]
    ups = [moved(chunks + c, wu, up, c * step, step) for c in range(chunks)]
    downs = [moved(2 * chunks + c, wd, down, c * tall, tall) for c in range(heights)]
    for c in range(chunks):
        gates[c].start()
        ups[c].start()
    for copy in downs:
        copy.start()
    rows_ref[...] = jnp.concatenate([p[...].astype(F32) for p in pieces], axis=0).astype(BF16)
    gate_acc[...] = jnp.zeros_like(gate_acc)
    up_acc[...] = jnp.zeros_like(up_acc)
    for c in range(chunks):
        here = slice(c * step, (c + 1) * step)
        gates[c].wait()
        gate_acc[...] += matmul(rows_ref[:, here], gate[here, :])
        ups[c].wait()
        up_acc[...] += matmul(rows_ref[:, here], up[here, :])
    value = gate_acc[...]
    hidden_ref[...] = (value / (1.0 + jnp.exp(-value)) * up_acc[...]).astype(BF16)
    for copy in downs:
        copy.wait()

    @pl.loop(0, down.shape[1] // wide)
    def _(i):
        here = pl.ds(pl.multiple_of(i * wide, wide), wide)
        result = matmul(hidden_ref[...], down[:, here])
        for n, out in enumerate(outs):
            out[:, here] = result[n * height : (n + 1) * height].astype(out.dtype)


def combine_kernel(cap, order, ids_ref, home_ref, weights_ref, mine_ref, other_ref, *refs):
    blocks, out = sorted_blocks(order, refs[:-1]), refs[-1]
    rows = out.shape[0]
    parts = TILE // cap
    width = out.shape[1] // parts
    codes = slot_codes(ids_ref, home_ref[0], rows, cap)
    weights = [weights_ref[t, r] for r in range(rows) for t in range(TOPK)]
    shape = (parts * rows, len(blocks) * TILE)
    i, j = iota(shape, 0), iota(shape, 1)
    code = j // TILE * cap + j % cap
    same = j % TILE // cap == i // rows
    position = iota((parts * rows, 1), 0) % rows
    share = jnp.zeros(shape, F32)
    for t in range(TOPK):
        share += jnp.where(
            same & (code == by_row(codes, position, rows, t)),
            by_row(weights, position, rows, t),
            0.0,
        )
    high = share.astype(BF16)
    rest = share - high.astype(F32)
    middle = rest.astype(BF16)
    low = (rest - middle.astype(F32)).astype(BF16)
    arrived = jnp.concatenate([b[...] for b in blocks], axis=0)
    routed = matmul(high, arrived) + matmul(middle, arrived) + matmul(low, arrived)
    for q in range(parts):
        here = slice(q * width, (q + 1) * width)
        shared = mine_ref[:, here].astype(F32)
        for n in range(other_ref.shape[0] // rows):
            shared += other_ref[n * rows : (n + 1) * rows, here].astype(F32)
        out[:, here] = (routed[q * rows : (q + 1) * rows] + shared).astype(out.dtype)


def on_device(
    tokens,
    expert_ids,
    gate_weights,
    w_gate,
    scale_gate,
    w_up,
    scale_up,
    w_down,
    scale_down,
    outlier_cols,
    outlier_gate,
    outlier_up,
    shared_gate,
    shared_up,
    shared_down,
):
    devices = lax.axis_size("ep")
    device = lax.axis_index("ep")
    hid = w_gate.shape[2]
    group = FF // hid
    experts = devices // group
    bits = group.bit_length() - 1
    rows, width = tokens.shape[1], tokens.shape[2]
    cap = max(2, rows * TOPK * 2 // experts)
    home = device // group
    block = width // scale_gate.shape[1]
    part_width = width * cap // TILE
    slots = experts * cap

    def swap(array, mask):
        return lax.ppermute(array, "ep", [(d, d ^ mask) for d in range(devices)])

    def spread(pieces):
        for bit in range(bits):
            pieces = pieces + [swap(piece, 1 << bit) for piece in pieces]
        return pieces

    current, ids = tokens[0], expert_ids[0].T
    home_ref = home.astype(jnp.int32).reshape(1)
    send_block = jax.ShapeDtypeStruct((TILE, part_width), BF16)
    order = (0,) + tuple(sorted(range(1, experts), key=lambda m: (-m.bit_length(), m)))

    blocks = pl.pallas_call(
        functools.partial(send_kernel, cap, order),
        in_specs=[SMEM, SMEM, ANY],
        out_specs=[VMEM] * experts,
        out_shape=[send_block] * experts,
        scratch_shapes=[
            pltpu.VMEM((rows, width), BF16),
            pltpu.VMEM((TILE // cap * rows, part_width), F32),
            pltpu.SemaphoreType.DMA,
        ],
        compiler_params=params(8),
        cost_estimate=cost(1e8, 1e6),
        name="send",
    )(ids, home_ref, in_hbm(current))
    arrived = [blocks[0]] + [swap(block, m * group) for m, block in zip(order[1:], blocks[1:])]

    cols, _ = lax.optimization_barrier(
        (lax.dynamic_slice_in_dim(outlier_cols, home, 1, 0), blocks[0])
    )
    step, tall = 1024, hid // scale_down.shape[1]
    copies = 2 * (width // step) + hid // tall
    stored = jax.ShapeDtypeStruct((width, hid), BF16)
    prepared = pl.pallas_call(
        functools.partial(prepare_kernel, step, tall),
        in_specs=[ANY] * 3 + [VMEM] * 4,
        out_specs=[VMEM] * 5,
        out_shape=[
            stored,
            stored,
            jax.ShapeDtypeStruct((hid, width), BF16),
            jax.ShapeDtypeStruct((width, outlier_cols.shape[1]), BF16),
            jax.ShapeDtypeStruct((8, width), F32),
        ],
        scratch_shapes=[
            pltpu.VMEM(scale_gate.shape[1:], F32),
            pltpu.VMEM(scale_up.shape[1:], F32),
            pltpu.SemaphoreType.DMA((copies,)),
        ],
        compiler_params=params(12),
        cost_estimate=cost(1e9, 6 * hid * width),
        name="prepare",
    )(
        in_hbm(w_gate[0]),
        in_hbm(w_up[0]),
        in_hbm(w_down[0]),
        scale_gate[0],
        scale_up[0],
        scale_down[0],
        cols,
    )
    arrived, keep = lax.optimization_barrier((tuple(arrived), prepared[4]))
    prepared = list(prepared[:4]) + [keep]

    whole = jax.ShapeDtypeStruct((slots, width), BF16)
    taken = pl.pallas_call(
        functools.partial(unpack_kernel, cap, order),
        in_specs=[VMEM] * experts,
        out_specs=VMEM,
        out_shape=whole,
        compiler_params=params(16),
        cost_estimate=cost(1e8, 1e6),
        name="unpack",
    )(*arrived)
    pieces = spread([taken])

    partials = pl.pallas_call(
        functools.partial(expert_kernel, 1024, 1024),
        in_specs=[VMEM] * (7 + group),
        out_specs=[VMEM] * group,
        out_shape=[whole] * group,
        scratch_shapes=[
            pltpu.VMEM((group * slots, hid), F32),
            pltpu.VMEM((group * slots, hid), F32),
            pltpu.VMEM((group * slots, outlier_cols.shape[1]), F32),
            pltpu.VMEM((group * slots, hid), BF16),
        ],
        compiler_params=params(12),
        cost_estimate=cost(6 * group * slots * width * hid, 6 * hid * width),
        name="expert",
    )(*prepared, outlier_gate[0], outlier_up[0], *pieces)

    for bit in reversed(range(1, bits)):
        half = 1 << bit
        partials = [
            (mine.astype(F32) + swap(other, half).astype(F32)).astype(BF16)
            for mine, other in zip(partials[:half], partials[half:])
        ]
    returning = pl.pallas_call(
        functools.partial(pack_kernel, cap, order),
        in_specs=[VMEM] * 2,
        out_specs=[VMEM] * experts,
        out_shape=[send_block] * experts,
        compiler_params=params(16),
        cost_estimate=cost(1e8, 1e6),
        name="pack",
    )(partials[0], swap(partials[1], 1))
    returned = [returning[0]] + [swap(block, m * group) for m, block in zip(order[1:], returning[1:])]

    row_pieces = spread([current])
    row_pieces = list(lax.optimization_barrier((tuple(row_pieces), returning[0]))[0])
    shared = pl.pallas_call(
        functools.partial(shared_kernel, step, tall, 1024),
        in_specs=[ANY] * 3 + [VMEM] * group,
        out_specs=[VMEM] * group,
        out_shape=[jax.ShapeDtypeStruct((rows, width), F32)]
        + [jax.ShapeDtypeStruct((rows, width), BF16)] * (group - 1),
        scratch_shapes=[
            pltpu.VMEM((width, hid), BF16),
            pltpu.VMEM((width, hid), BF16),
            pltpu.VMEM((hid, width), BF16),
            pltpu.VMEM((group * rows, width), BF16),
            pltpu.VMEM((group * rows, hid), F32),
            pltpu.VMEM((group * rows, hid), F32),
            pltpu.VMEM((group * rows, hid), BF16),
            pltpu.SemaphoreType.DMA((copies,)),
        ],
        compiler_params=params(32),
        cost_estimate=cost(6 * group * rows * width * hid, 6 * hid * width),
        name="shared",
    )(in_hbm(shared_gate[0]), in_hbm(shared_up[0]), in_hbm(shared_down[0]), *row_pieces)
    others = [swap(shared[n], n) for n in range(1, group)]
    others = others[0] if group == 2 else jnp.concatenate(others, axis=0)

    out = pl.pallas_call(
        functools.partial(combine_kernel, cap, order),
        in_specs=[SMEM, SMEM, SMEM] + [VMEM] * (2 + experts),
        out_specs=VMEM,
        out_shape=jax.ShapeDtypeStruct((rows, width), BF16),
        compiler_params=params(16),
        cost_estimate=cost(1e8, 1e6),
        name="combine",
    )(ids, home_ref, gate_weights[0].T, shared[0], others, *returned)
    return out[None]


def solution(mesh):
    rows = P(None, ("parts", "ep"), None)
    held = P("ep", None, None)
    placed = (rows, rows, rows) + (held,) * 6 + (P(),) + (held,) * 5
    return jax.shard_map(
        on_device, mesh=mesh, in_specs=placed, out_specs=rows, check_vma=False
    )
```

time: 91.2 us -> 65.3 us (0.72)
  other arithmetic: 29.7 us -> 0 us
  Pallas kernels: 0 us -> 27.5 us
  matrix products: 24.3 us -> 0 us
  starting transfers between devices: 14 us -> 26.5 us
  local copies, waits for them, and re-layouts: 8.98 us -> 3.18 us
  waiting for transfers between devices: 13.1 us -> 7.63 us
    pallas_call x0 -> x7, Pallas kernels: none -> 27.5 us  [the longest x1 9.31 us: on_device(): pl.pallas_call(functools.partial(shared_kernel, step, tall, 1024), in_spe...]
    ppermute x2 -> x18, starting transfers between devices: 0.92 us -> 26.5 us  [swap(): return lax.ppermute(array, 'ep', [(d, d ^ mask) for d in range(devices)])]
    convert_element_type x8 -> x0, other arithmetic: 25 us -> none  [the longest x3 22 us: dequant(): return scaled.reshape(height, breadth).astype(jnp.bfloat16)]
    dot_general x9 -> x0, matrix products: 24.3 us -> none  [the longest x1 7.26 us: shared_rows(): return jnp.dot(hidden, down_matrix, preferred_element_type=jnp.float32)]
    all_to_all x2 -> x0, waiting for transfers between devices: 13 us -> none  [the longest x1 13 us: on_device(): lax.all_to_all(partial_value, 'ep', split_axis=0, concat_axis=0, tiled=True)]
    all_to_all x2 -> x0, starting transfers between devices: 13 us -> none  [the longest x1 7.05 us: on_device(): lax.all_to_all(spread, 'ep', split_axis=0, concat_axis=0, tiled=True)]
    ppermute x2 -> x18, waiting for transfers between devices: 0.01 us -> 7.63 us  [swap(): return lax.ppermute(array, 'ep', [(d, d ^ mask) for d in range(devices)])]
    gather x1 -> x0, local copies, waits for them, and re-layouts: 2.39 us -> none  [split_inputs(): picked = jnp.take(inputs, columns, axis=1)]
  transfers between devices with their start and end apart: 4 -> 18, of which waited for: 1 -> 6; matrix products, arithmetic and copies ran while one was open for 49% -> 0% of each run, Pallas kernels for 0% -> 27%
where the time goes in v1:
time: 65.3 us; the launch traced here: 65 us
  Pallas kernels  27.5 us (42%)
  starting transfers between devices  26.5 us (41%)
  waiting for transfers between devices  7.63 us (12%)
  local copies, waits for them, and re-layouts  3.18 us (5%)
    ppermute x18, starting transfers between devices, swap(): return lax.ppermute(array, 'ep', [(d, d ^ mask) for d in range(devices)])  26.5 us
    pallas_call x1, Pallas kernels, on_device(): pl.pallas_call(functools.partial(shared_kernel, step, tall, 1024), in_spe...  9.31 us
    pallas_call x1, Pallas kernels, on_device(): pl.pallas_call(functools.partial(prepare_kernel, step, tall), in_specs=[A...  8.13 us
    ppermute x18, waiting for transfers between devices, swap(): return lax.ppermute(array, 'ep', [(d, d ^ mask) for d in range(devices)])  7.63 us
    pallas_call x1, Pallas kernels, on_device(): pl.pallas_call(functools.partial(expert_kernel, 1024, 1024), in_specs=[VM...  6.14 us
    unnamed x22, local copies, waits for them, and re-layouts  3.17 us
    pallas_call x1, Pallas kernels, on_device(): pl.pallas_call(functools.partial(send_kernel, cap, order), in_specs=[SMEM...  1.7 us
    pallas_call x1, Pallas kernels, on_device(): pl.pallas_call(functools.partial(combine_kernel, cap, order), in_specs=[S...  1.68 us
  transfers between devices with their start and end apart: 18, of which 6 were waited for; matrix products, arithmetic and copies ran while one was open for 0% of the time, Pallas kernels for 27%

profile of v1, /device:TPU:0, one launch (start us, length us, event | category | flops | bytes accessed | tf_op | source)
XLA Modules:
  0.0 65.0 jit_solution(9991273812159282029)
XLA Ops:
  0.0 0.7 %copy-done.8 = s32[1,8,2]{1,2,0:T(2,128)S(1)} copy-done((s32[1,8,2]{1,2,0:T(2,128)S(1)}, s32[1,8,2]{1,2,0:T(2,128)}, u32[]{:S(2)}) %copy-start.8) | copy-done | bytes 88
  0.7 1.7 %send.1 = (bf16[16,1792]{1,0:T(8,128)(2,1)S(1)}, bf16[16,1792]{1,0:T(8,128)(2,1)S(1)}, bf16[16,1792]{1,0:T(8,128)(2,1)S(1)}, bf16[16,1792]{1,0:T(8,128)(2,1)S(1)...) custom-call(s32[2,8]{1,0:T(2,128)S(1)} %bitcast.28, ...), custom_call_target="tpu_custom_call" | custom-call | flops 100000000 | bytes 1000000 | tf_op jit(solution)/shard_map/send/pallas_call | solution.py:322
  2.4 4.1 %collective-permute-start.1 = (bf16[16,1792]{1,0:T(8,128)(2,1)S(1)}, bf16[16,1792]{1,0:T(8,128)(2,1)S(1)}, u32[]{:S(2)}, u32[]{:S(2)}) collective-permute-start(bf16[16,1792]{1,0:T(8,128)(2,1)S(1)} %get-tuple-element.48), channel_id=1, source_target_pairs={{0,8},{1,9},{2,10},{3,11},{4,12},{5,13},{6,14},{7,15},{8,0},{9,1},... | collective-permute-start | bytes 172040 | tf_op jit(solution)/shard_map/ppermute | solution.py:310
  6.5 1.3 %collective-permute-start.2 = (bf16[16,1792]{1,0:T(8,128)(2,1)S(1)}, bf16[16,1792]{1,0:T(8,128)(2,1)S(1)}, u32[]{:S(2)}, u32[]{:S(2)}) collective-permute-start(bf16[16,1792]{1,0:T(8,128)(2,1)S(1)} %get-tuple-element.49), channel_id=1, source_target_pairs={{0,10},{1,11},{2,8},{3,9},{4,14},{5,15},{6,12},{7,13},{8,2},{9,3},... | collective-permute-start | bytes 172040 | tf_op jit(solution)/shard_map/ppermute | solution.py:310
  7.8 3.6 %collective-permute-start.3 = (bf16[16,1792]{1,0:T(8,128)(2,1)S(1)}, bf16[16,1792]{1,0:T(8,128)(2,1)S(1)}, u32[]{:S(2)}, u32[]{:S(2)}) collective-permute-start(bf16[16,1792]{1,0:T(8,128)(2,1)S(1)} %get-tuple-element.50), channel_id=1, source_target_pairs={{0,12},{1,13},{2,14},{3,15},{4,8},{5,9},{6,10},{7,11},{8,4},{9,5},... | collective-permute-start | bytes 172040 | tf_op jit(solution)/shard_map/ppermute | solution.py:310
  11.4 3.2 %collective-permute-start.6 = (bf16[16,1792]{1,0:T(8,128)(2,1)S(1)}, bf16[16,1792]{1,0:T(8,128)(2,1)S(1)}, u32[]{:S(2)}, u32[]{:S(2)}) collective-permute-start(bf16[16,1792]{1,0:T(8,128)(2,1)S(1)} %get-tuple-element.53), channel_id=1, source_target_pairs={{0,6},{1,7},{2,4},{3,5},{4,2},{5,3},{6,0},{7,1},{8,14},{9,15},{10,... | collective-permute-start | bytes 172040 | tf_op jit(solution)/shard_map/ppermute | solution.py:310
  14.6 0.6 collective-permute-done.2.refs_2_
  15.2 2.3 %collective-permute-start.7 = (bf16[16,1792]{1,0:T(8,128)(2,1)S(1)}, bf16[16,1792]{1,0:T(8,128)(2,1)S(1)}, u32[]{:S(2)}, u32[]{:S(2)}) collective-permute-start(bf16[16,1792]{1,0:T(8,128)(2,1)S(1)} %get-tuple-element.54), channel_id=1, source_target_pairs={{0,2},{1,3},{2,0},{3,1},{4,6},{5,7},{6,4},{7,5},{8,10},{9,11},{10,... | collective-permute-start | bytes 172040 | tf_op jit(solution)/shard_map/ppermute | solution.py:310
  17.5 0.8 %copy-done.5 = bf16[1,56,512]{2,1,0:T(8,128)(2,1)S(1)} copy-done((bf16[1,56,512]{2,1,0:T(8,128)(2,1)S(1)}, bf16[1,56,512]{2,1,0:T(8,128)(2,1)}, u32[]{:S(2)}) %copy-start.5) | copy-done | bytes 57368
  18.3 0.8 %copy-done.6 = bf16[1,56,512]{2,1,0:T(8,128)(2,1)S(1)} copy-done((bf16[1,56,512]{2,1,0:T(8,128)(2,1)S(1)}, bf16[1,56,512]{2,1,0:T(8,128)(2,1)}, u32[]{:S(2)}) %copy-start.6) | copy-done | bytes 57368
  19.2 0.8 %copy-done.7 = bf16[1,4,7168]{2,1,0:T(4,128)(2,1)S(1)} copy-done((bf16[1,4,7168]{2,1,0:T(4,128)(2,1)S(1)}, bf16[1,4,7168]{2,1,0:T(4,128)(2,1)}, u32[]{:S(2)}) %copy-start.7) | copy-done | bytes 57368
  20.0 8.1 %prepare.1 = (bf16[7168,512]{1,0:T(8,128)(2,1)S(1)}, bf16[7168,512]{1,0:T(8,128)(2,1)S(1)}, bf16[512,7168]{1,0:T(8,128)(2,1)S(1)}, bf16[7168,128]{1,0:T(8,128)(2,1)S(1)}, f32[8,7168]{1,0:T(8,128)S(1)}) custom-call(bf16[7168,512]{1,0:T(8,128)(2,1)} %bitcast.31, bf16[7168,512]{1,0:T(8,128)(2,1)} %bitcast.32, bf16[512,7168]{1,0:T(8,128)(2,1)} %bitcast.33, ...), custom_call_target="tpu_custom_call" | custom-call | flops 1000000000 | bytes 22020096 | tf_op jit(solution)/shard_map/prepare/pallas_call | solution.py:344
  28.2 0.3 unpack.1.refs_0_
  28.5 0.1 collective-permute-start.8
  28.5 1.8 %collective-permute-done.8.refs_1_ = bf16[32,7168]{1,0:T(8,128)(2,1)S(1)} collective-permute-done((bf16[32,7168]{1,0:T(8,128)(2,1)S(1)}, bf16[32,7168]{1,0:T(8,128)(2,1)S(1)}, u32[]{:S(2)}, u32[]{:S(2)}) %collective-permute-start.8) | collective-permute-done | bytes 458784 | tf_op jit(solution)/shard_map/ppermute | solution.py:310
  30.3 6.1 %expert.1 = (bf16[32,7168]{1,0:T(8,128)(2,1)S(1)}, bf16[32,7168]{1,0:T(8,128)(2,1)S(1)}) custom-call(bf16[7168,512]{1,0:T(8,128)(2,1)S(1)} %get-tuple-element.44.gate, bf16[7168,512]{1,0:T(8,128)(2,1)S(1)} %get-tuple-element.45.up, bf16[512,7168]{1,0:T(8,128)(2,1)S(1)} %get-tuple-element.46.down, bf16[7168,128]{1,0:T(8,128)(2,1)S(1)} %get-tuple-element.47.onehot, ...), custom_call_target="tpu_custom_call" | custom-call | flops 1409286144 | bytes 22020096 | tf_op jit(solution)/shard_map/expert/pallas_call | solution.py:387
  36.5 0.2 collective-permute-start.9
  36.7 0.4 collective-permute-start
  37.1 1.3 %collective-permute-done.9.other_ref = bf16[32,7168]{1,0:T(8,128)(2,1)S(1)} collective-permute-done((bf16[32,7168]{1,0:T(8,128)(2,1)S(1)}, bf16[32,7168]{1,0:T(8,128)(2,1)S(1)}, u32[]{:S(2)}, u32[]{:S(2)}) %collective-permute-start.9) | collective-permute-done | bytes 458784 | tf_op jit(solution)/shard_map/ppermute | solution.py:310
  38.4 0.3 pack.1
  38.7 0.1 collective-permute-start.11
  38.8 2.3 %collective-permute-start.12 = (bf16[16,1792]{1,0:T(8,128)(2,1)S(1)}, bf16[16,1792]{1,0:T(8,128)(2,1)S(1)}, u32[]{:S(2)}, u32[]{:S(2)}) collective-permute-start(bf16[16,1792]{1,0:T(8,128)(2,1)S(1)} %get-tuple-element.73), channel_id=1, source_target_pairs={{0,10},{1,11},{2,8},{3,9},{4,14},{5,15},{6,12},{7,13},{8,2},{9,3},... | collective-permute-start | bytes 172040 | tf_op jit(solution)/shard_map/ppermute | solution.py:310
  41.1 3.7 %collective-permute-start.13 = (bf16[16,1792]{1,0:T(8,128)(2,1)S(1)}, bf16[16,1792]{1,0:T(8,128)(2,1)S(1)}, u32[]{:S(2)}, u32[]{:S(2)}) collective-permute-start(bf16[16,1792]{1,0:T(8,128)(2,1)S(1)} %get-tuple-element.74), channel_id=1, source_target_pairs={{0,12},{1,13},{2,14},{3,15},{4,8},{5,9},{6,10},{7,11},{8,4},{9,5},... | collective-permute-start | bytes 172040 | tf_op jit(solution)/shard_map/ppermute | solution.py:310
  44.8 9.3 %shared.1 = (f32[8,7168]{1,0:T(8,128)S(1)}, bf16[8,7168]{1,0:T(8,128)(2,1)S(1)}) custom-call(bf16[7168,512]{1,0:T(8,128)(2,1)} %bitcast.34, bf16[7168,512]{1,0:T(8,128)(2,1)} %bitcast.35, bf16[512,7168]{1,0:T(8,128)(2,1)} %bitcast.36, bf16[8,7168]{1,0:T(8,128)(2,1)S(1)} %bitcast.24, bf16[8,7168]{1,0:T(8,128)(2,1)S(1)} %collective-permute-done.refs_1_), custom_call_target="tpu_custom_call" | custom-call | flops 352321536 | bytes 22020096 | tf_op jit(solution)/shard_map/shared/pallas_call | solution.py:422
  54.1 0.1 collective-permute-start.10
  54.2 1.7 %collective-permute-start.14 = (bf16[16,1792]{1,0:T(8,128)(2,1)S(1)}, bf16[16,1792]{1,0:T(8,128)(2,1)S(1)}, u32[]{:S(2)}, u32[]{:S(2)}) collective-permute-start(bf16[16,1792]{1,0:T(8,128)(2,1)S(1)} %get-tuple-element.75), channel_id=1, source_target_pairs={{0,14},{1,15},{2,12},{3,13},{4,10},{5,11},{6,8},{7,9},{8,6},{9,7},... | collective-permute-start | bytes 172040 | tf_op jit(solution)/shard_map/ppermute | solution.py:310
  55.9 1.5 %collective-permute-start.16 = (bf16[16,1792]{1,0:T(8,128)(2,1)S(1)}, bf16[16,1792]{1,0:T(8,128)(2,1)S(1)}, u32[]{:S(2)}, u32[]{:S(2)}) collective-permute-start(bf16[16,1792]{1,0:T(8,128)(2,1)S(1)} %get-tuple-element.77), channel_id=1, source_target_pairs={{0,6},{1,7},{2,4},{3,5},{4,2},{5,3},{6,0},{7,1},{8,14},{9,15},{10,... | collective-permute-start | bytes 172040 | tf_op jit(solution)/shard_map/ppermute | solution.py:310
  57.3 2.0 %collective-permute-start.17 = (bf16[16,1792]{1,0:T(8,128)(2,1)S(1)}, bf16[16,1792]{1,0:T(8,128)(2,1)S(1)}, u32[]{:S(2)}, u32[]{:S(2)}) collective-permute-start(bf16[16,1792]{1,0:T(8,128)(2,1)S(1)} %get-tuple-element.78), channel_id=1, source_target_pairs={{0,2},{1,3},{2,0},{3,1},{4,6},{5,7},{6,4},{7,5},{8,10},{9,11},{10,... | collective-permute-start | bytes 172040 | tf_op jit(solution)/shard_map/ppermute | solution.py:310
  59.4 2.4 %collective-permute-done.14.refs_4_ = bf16[16,1792]{1,0:T(8,128)(2,1)S(1)} collective-permute-done((bf16[16,1792]{1,0:T(8,128)(2,1)S(1)}, bf16[16,1792]{1,0:T(8,128)(2,1)S(1)}, u32[]{:S(2)}, u32[]{:S(2)}) %collective-permute-start.14) | collective-permute-done | bytes 57376 | tf_op jit(solution)/shard_map/ppermute | solution.py:310
  61.8 0.4 collective-permute-done.16.refs_6_
  62.2 1.1 %collective-permute-done.17.refs_7_ = bf16[16,1792]{1,0:T(8,128)(2,1)S(1)} collective-permute-done((bf16[16,1792]{1,0:T(8,128)(2,1)S(1)}, bf16[16,1792]{1,0:T(8,128)(2,1)S(1)}, u32[]{:S(2)}, u32[]{:S(2)}) %collective-permute-start.17) | collective-permute-done | bytes 57376 | tf_op jit(solution)/shard_map/ppermute | solution.py:310
  63.3 1.7 %combine.1 = bf16[8,7168]{1,0:T(8,128)(2,1)} custom-call(s32[2,8]{1,0:T(2,128)S(1)} %bitcast.29, s32[1]{0:T(128)} %bitcast.2.home_ref, f32[2,8]{1,0:T(2,128)S(1)} %bitcast.30, f32[8,7168]{1,0:T(8,128)S(1)} %get-tuple-element.70.mine_ref, bf16[8,7168]{1,0:T(8,128)(2,1)S(1)} %collective-permute-done.10.other_ref, ...), custom_call_target="tpu_custom_call" | custom-call | flops 100000000 | bytes 1000000 | tf_op jit(solution)/shard_map/combine/pallas_call | solution.py:445
  (34 shorter events, 0.1 us)
Async XLA Ops:
  0.0 11.4 %copy-start = (s32[8,128]{1,0:T(8,128)S(1)}, s32[8,128]{1,0:T(8,128)}, u32[]{:S(2)}) copy-start(s32[8,128]{1,0:T(8,128)} %param.24) | copy-start | bytes 12292
  0.0 0.7 %copy-start.8 = (s32[1,8,2]{1,2,0:T(2,128)S(1)}, s32[1,8,2]{1,2,0:T(2,128)}, u32[]{:S(2)}) copy-start(s32[1,8,2]{1,2,0:T(2,128)} %param.16) | copy-start | bytes 196
  2.4 9.0 %collective-permute-start.1 = (bf16[16,1792]{1,0:T(8,128)(2,1)S(1)}, bf16[16,1792]{1,0:T(8,128)(2,1)S(1)}, u32[]{:S(2)}, u32[]{:S(2)}) collective-permute-start(bf16[16,1792]{1,0:T(8,128)(2,1)S(1)} %get-tuple-element.48), channel_id=1, source_target_pairs={{0,8},{1,9},{2,10},{3,11},{4,12},{5,13},{6,14},{7,15},{8,0},{9,1},... | collective-permute-start | bytes 172040 | tf_op jit(solution)/shard_map/ppermute | solution.py:310
  6.5 8.7 %collective-permute-start.2 = (bf16[16,1792]{1,0:T(8,128)(2,1)S(1)}, bf16[16,1792]{1,0:T(8,128)(2,1)S(1)}, u32[]{:S(2)}, u32[]{:S(2)}) collective-permute-start(bf16[16,1792]{1,0:T(8,128)(2,1)S(1)} %get-tuple-element.49), channel_id=1, source_target_pairs={{0,10},{1,11},{2,8},{3,9},{4,14},{5,15},{6,12},{7,13},{8,2},{9,3},... | collective-permute-start | bytes 172040 | tf_op jit(solution)/shard_map/ppermute | solution.py:310
  7.8 20.3 %collective-permute-start.3 = (bf16[16,1792]{1,0:T(8,128)(2,1)S(1)}, bf16[16,1792]{1,0:T(8,128)(2,1)S(1)}, u32[]{:S(2)}, u32[]{:S(2)}) collective-permute-start(bf16[16,1792]{1,0:T(8,128)(2,1)S(1)} %get-tuple-element.50), channel_id=1, source_target_pairs={{0,12},{1,13},{2,14},{3,15},{4,8},{5,9},{6,10},{7,11},{8,4},{9,5},... | collective-permute-start | bytes 172040 | tf_op jit(solution)/shard_map/ppermute | solution.py:310
  11.4 16.7 %collective-permute-start.4 = (bf16[16,1792]{1,0:T(8,128)(2,1)S(1)}, bf16[16,1792]{1,0:T(8,128)(2,1)S(1)}, u32[]{:S(2)}, u32[]{:S(2)}) collective-permute-start(bf16[16,1792]{1,0:T(8,128)(2,1)S(1)} %get-tuple-element.51), channel_id=1, source_target_pairs={{0,14},{1,15},{2,12},{3,13},{4,10},{5,11},{6,8},{7,9},{8,6},{9,7},... | collective-permute-start | bytes 172040 | tf_op jit(solution)/shard_map/ppermute | solution.py:310
  11.4 16.7 %collective-permute-start.5 = (bf16[16,1792]{1,0:T(8,128)(2,1)S(1)}, bf16[16,1792]{1,0:T(8,128)(2,1)S(1)}, u32[]{:S(2)}, u32[]{:S(2)}) collective-permute-start(bf16[16,1792]{1,0:T(8,128)(2,1)S(1)} %get-tuple-element.52), channel_id=1, source_target_pairs={{0,4},{1,5},{2,6},{3,7},{4,0},{5,1},{6,2},{7,3},{8,12},{9,13},{10,... | collective-permute-start | bytes 172040 | tf_op jit(solution)/shard_map/ppermute | solution.py:310
  11.4 16.7 %collective-permute-start.6 = (bf16[16,1792]{1,0:T(8,128)(2,1)S(1)}, bf16[16,1792]{1,0:T(8,128)(2,1)S(1)}, u32[]{:S(2)}, u32[]{:S(2)}) collective-permute-start(bf16[16,1792]{1,0:T(8,128)(2,1)S(1)} %get-tuple-element.53), channel_id=1, source_target_pairs={{0,6},{1,7},{2,4},{3,5},{4,2},{5,3},{6,0},{7,1},{8,14},{9,15},{10,... | collective-permute-start | bytes 172040 | tf_op jit(solution)/shard_map/ppermute | solution.py:310
  15.2 12.9 %collective-permute-start.7 = (bf16[16,1792]{1,0:T(8,128)(2,1)S(1)}, bf16[16,1792]{1,0:T(8,128)(2,1)S(1)}, u32[]{:S(2)}, u32[]{:S(2)}) collective-permute-start(bf16[16,1792]{1,0:T(8,128)(2,1)S(1)} %get-tuple-element.54), channel_id=1, source_target_pairs={{0,2},{1,3},{2,0},{3,1},{4,6},{5,7},{6,4},{7,5},{8,10},{9,11},{10,... | collective-permute-start | bytes 172040 | tf_op jit(solution)/shard_map/ppermute | solution.py:310
  17.5 0.8 %copy-start.5 = (bf16[1,56,512]{2,1,0:T(8,128)(2,1)S(1)}, bf16[1,56,512]{2,1,0:T(8,128)(2,1)}, u32[]{:S(2)}) copy-start(bf16[1,56,512]{2,1,0:T(8,128)(2,1)} %param.19) | copy-start | bytes 172036
  18.3 0.8 %copy-start.6 = (bf16[1,56,512]{2,1,0:T(8,128)(2,1)S(1)}, bf16[1,56,512]{2,1,0:T(8,128)(2,1)}, u32[]{:S(2)}) copy-start(bf16[1,56,512]{2,1,0:T(8,128)(2,1)} %param.21) | copy-start | bytes 172036
  19.2 0.8 %copy-start.7 = (bf16[1,4,7168]{2,1,0:T(4,128)(2,1)S(1)}, bf16[1,4,7168]{2,1,0:T(4,128)(2,1)}, u32[]{:S(2)}) copy-start(bf16[1,4,7168]{2,1,0:T(4,128)(2,1)} %param.23) | copy-start | bytes 172036
  20.0 10.4 %copy-start.2 = (bf16[1,128,512]{2,1,0:T(8,128)(2,1)S(1)}, bf16[1,128,512]{2,1,0:T(8,128)(2,1)}, u32[]{:S(2)}) copy-start(bf16[1,128,512]{2,1,0:T(8,128)(2,1)} %param.25) | copy-start | bytes 393220
  20.0 10.4 %copy-start.3 = (bf16[1,128,512]{2,1,0:T(8,128)(2,1)S(1)}, bf16[1,128,512]{2,1,0:T(8,128)(2,1)}, u32[]{:S(2)}) copy-start(bf16[1,128,512]{2,1,0:T(8,128)(2,1)} %param.26) | copy-start | bytes 393220
  28.5 1.9 %collective-permute-start.8 = (bf16[32,7168]{1,0:T(8,128)(2,1)S(1)}, bf16[32,7168]{1,0:T(8,128)(2,1)S(1)}, u32[]{:S(2)}, u32[]{:S(2)}) collective-permute-start(bf16[32,7168]{1,0:T(8,128)(2,1)S(1)} %unpack.1.refs_0_), channel_id=1, source_target_pairs={{0,1},{1,0},{2,3},{3,2},{4,5},{5,4},{6,7},{7,6},{8,9},{9,8},{10,11... | collective-permute-start | bytes 1376264 | tf_op jit(solution)/shard_map/ppermute | solution.py:310
  30.3 6.3 %copy-start.4 = (bf16[1,8,7168]{2,1,0:T(8,128)(2,1)S(1)}, bf16[1,8,7168]{2,1,0:T(8,128)(2,1)}, u32[]{:S(2)}) copy-start(bf16[1,8,7168]{2,1,0:T(8,128)(2,1)} %param.15) | copy-start | bytes 344068
  36.5 1.9 %collective-permute-start.9 = (bf16[32,7168]{1,0:T(8,128)(2,1)S(1)}, bf16[32,7168]{1,0:T(8,128)(2,1)S(1)}, u32[]{:S(2)}, u32[]{:S(2)}) collective-permute-start(bf16[32,7168]{1,0:T(8,128)(2,1)S(1)} %get-tuple-element.66), channel_id=1, source_target_pairs={{0,1},{1,0},{2,3},{3,2},{4,5},{5,4},{6,7},{7,6},{8,9},{9,8},{10,11... | collective-permute-start | bytes 1376264 | tf_op jit(solution)/shard_map/ppermute | solution.py:310
  36.7 2.0 %collective-permute-start = (bf16[8,7168]{1,0:T(8,128)(2,1)S(1)}, bf16[8,7168]{1,0:T(8,128)(2,1)S(1)}, u32[]{:S(2)}, u32[]{:S(2)}) collective-permute-start(bf16[8,7168]{1,0:T(8,128)(2,1)S(1)} %bitcast.23), channel_id=1, source_target_pairs={{0,1},{1,0},{2,3},{3,2},{4,5},{5,4},{6,7},{7,6},{8,9},{9,8},{10,11... | collective-permute-start | bytes 344072 | tf_op jit(solution)/shard_map/ppermute | solution.py:310
  38.7 17.2 %collective-permute-start.11 = (bf16[16,1792]{1,0:T(8,128)(2,1)S(1)}, bf16[16,1792]{1,0:T(8,128)(2,1)S(1)}, u32[]{:S(2)}, u32[]{:S(2)}) collective-permute-start(bf16[16,1792]{1,0:T(8,128)(2,1)S(1)} %get-tuple-element.72), channel_id=1, source_target_pairs={{0,8},{1,9},{2,10},{3,11},{4,12},{5,13},{6,14},{7,15},{8,0},{9,1},... | collective-permute-start | bytes 172040 | tf_op jit(solution)/shard_map/ppermute | solution.py:310
  38.8 17.1 %collective-permute-start.12 = (bf16[16,1792]{1,0:T(8,128)(2,1)S(1)}, bf16[16,1792]{1,0:T(8,128)(2,1)S(1)}, u32[]{:S(2)}, u32[]{:S(2)}) collective-permute-start(bf16[16,1792]{1,0:T(8,128)(2,1)S(1)} %get-tuple-element.73), channel_id=1, source_target_pairs={{0,10},{1,11},{2,8},{3,9},{4,14},{5,15},{6,12},{7,13},{8,2},{9,3},... | collective-permute-start | bytes 172040 | tf_op jit(solution)/shard_map/ppermute | solution.py:310
  41.1 16.2 %collective-permute-start.13 = (bf16[16,1792]{1,0:T(8,128)(2,1)S(1)}, bf16[16,1792]{1,0:T(8,128)(2,1)S(1)}, u32[]{:S(2)}, u32[]{:S(2)}) collective-permute-start(bf16[16,1792]{1,0:T(8,128)(2,1)S(1)} %get-tuple-element.74), channel_id=1, source_target_pairs={{0,12},{1,13},{2,14},{3,15},{4,8},{5,9},{6,10},{7,11},{8,4},{9,5},... | collective-permute-start | bytes 172040 | tf_op jit(solution)/shard_map/ppermute | solution.py:310
  44.8 20.2 %copy-start.1 = (s32[8,128]{1,0:T(8,128)S(1)}, s32[8,128]{1,0:T(8,128)}, u32[]{:S(2)}) copy-start(s32[8,128]{1,0:T(8,128)} %param.24) | copy-start | bytes 12292
  44.8 18.5 %copy-start.9 = (s32[1,8,2]{1,2,0:T(2,128)S(1)}, s32[1,8,2]{1,2,0:T(2,128)}, u32[]{:S(2)}) copy-start(s32[1,8,2]{1,2,0:T(2,128)} %param.16) | copy-start | bytes 196
  44.8 18.5 %copy-start.10 = (f32[1,8,2]{1,2,0:T(2,128)S(1)}, f32[1,8,2]{1,2,0:T(2,128)}, u32[]{:S(2)}) copy-start(f32[1,8,2]{1,2,0:T(2,128)} %param.17) | copy-start | bytes 196
  54.1 9.2 %collective-permute-start.10 = (bf16[8,7168]{1,0:T(8,128)(2,1)S(1)}, bf16[8,7168]{1,0:T(8,128)(2,1)S(1)}, u32[]{:S(2)}, u32[]{:S(2)}) collective-permute-start(bf16[8,7168]{1,0:T(8,128)(2,1)S(1)} %get-tuple-element.71), channel_id=1, source_target_pairs={{0,1},{1,0},{2,3},{3,2},{4,5},{5,4},{6,7},{7,6},{8,9},{9,8},{10,11... | collective-permute-start | bytes 344072 | tf_op jit(solution)/shard_map/ppermute | solution.py:310
  54.2 7.5 %collective-permute-start.14 = (bf16[16,1792]{1,0:T(8,128)(2,1)S(1)}, bf16[16,1792]{1,0:T(8,128)(2,1)S(1)}, u32[]{:S(2)}, u32[]{:S(2)}) collective-permute-start(bf16[16,1792]{1,0:T(8,128)(2,1)S(1)} %get-tuple-element.75), channel_id=1, source_target_pairs={{0,14},{1,15},{2,12},{3,13},{4,10},{5,11},{6,8},{7,9},{8,6},{9,7},... | collective-permute-start | bytes 172040 | tf_op jit(solution)/shard_map/ppermute | solution.py:310
  55.9 5.9 %collective-permute-start.15 = (bf16[16,1792]{1,0:T(8,128)(2,1)S(1)}, bf16[16,1792]{1,0:T(8,128)(2,1)S(1)}, u32[]{:S(2)}, u32[]{:S(2)}) collective-permute-start(bf16[16,1792]{1,0:T(8,128)(2,1)S(1)} %get-tuple-element.76), channel_id=1, source_target_pairs={{0,4},{1,5},{2,6},{3,7},{4,0},{5,1},{6,2},{7,3},{8,12},{9,13},{10,... | collective-permute-start | bytes 172040 | tf_op jit(solution)/shard_map/ppermute | solution.py:310
  55.9 6.3 %collective-permute-start.16 = (bf16[16,1792]{1,0:T(8,128)(2,1)S(1)}, bf16[16,1792]{1,0:T(8,128)(2,1)S(1)}, u32[]{:S(2)}, u32[]{:S(2)}) collective-permute-start(bf16[16,1792]{1,0:T(8,128)(2,1)S(1)} %get-tuple-element.77), channel_id=1, source_target_pairs={{0,6},{1,7},{2,4},{3,5},{4,2},{5,3},{6,0},{7,1},{8,14},{9,15},{10,... | collective-permute-start | bytes 172040 | tf_op jit(solution)/shard_map/ppermute | solution.py:310
  57.3 6.0 %collective-permute-start.17 = (bf16[16,1792]{1,0:T(8,128)(2,1)S(1)}, bf16[16,1792]{1,0:T(8,128)(2,1)S(1)}, u32[]{:S(2)}, u32[]{:S(2)}) collective-permute-start(bf16[16,1792]{1,0:T(8,128)(2,1)S(1)} %get-tuple-element.78), channel_id=1, source_target_pairs={{0,2},{1,3},{2,0},{3,1},{4,6},{5,7},{6,4},{7,5},{8,10},{9,11},{10,... | collective-permute-start | bytes 172040 | tf_op jit(solution)/shard_map/ppermute | solution.py:310

commit v2 on v1

v2 whole, which is shorter than its diff:
```python
import functools

import jax
import jax.numpy as jnp
from jax import lax
from jax.experimental import pallas as pl
from jax.experimental.pallas import tpu as pltpu
from jax.sharding import PartitionSpec as P

FF = 1024
TOPK = 2
TILE = 16
BF16 = jnp.bfloat16
F32 = jnp.float32
VMEM = pl.BlockSpec(memory_space=pltpu.VMEM)
ANY = pl.BlockSpec(memory_space=pl.ANY)
SMEM = pl.BlockSpec(memory_space=pltpu.SMEM)


def params(mib):
    return pltpu.CompilerParams(vmem_limit_bytes=mib << 20)


def cost(flops, nbytes):
    return pl.CostEstimate(flops=int(flops), bytes_accessed=int(nbytes), transcendentals=0)


def matmul(left, right):
    return jnp.dot(left, right, preferred_element_type=F32)


def in_hbm(array):
    return pltpu.with_memory_space_constraint(array, pltpu.HBM)


def iota(shape, dim):
    return lax.broadcasted_iota(jnp.int32, shape, dim)


def slot_codes(ids_ref, home, rows, capacity):
    ids = [ids_ref[t, r] for r in range(rows) for t in range(TOPK)]
    codes = []
    for n, e in enumerate(ids):
        place = jnp.int32(0)
        for earlier in ids[:n]:
            place += (earlier == e).astype(jnp.int32)
        apart = e ^ home
        codes.append(jnp.where(apart & 1 == 0, (apart >> 1) * capacity + place, -1))
    return codes


def block_codes(block, slot, capacity, masks):
    code = jnp.zeros(block.shape, jnp.int32)
    for n, mask in enumerate(masks):
        code = jnp.where(block == n, mask // 2 * capacity, code)
    return code + slot


def by_row(values, position, rows, choice):
    out = jnp.zeros(position.shape, values[0].dtype)
    for r in range(rows):
        out = jnp.where(position == r, values[r * TOPK + choice], out)
    return out


def choose_kernel(cap, masks, rows, own_ids, neighbour_ids, home_ref, out):
    parts = TILE // cap
    span = parts * rows
    shape = (out.shape[0], span)
    j, lane = iota(shape, 0), iota(shape, 1)
    code = block_codes(j // (2 * TILE), j % cap, cap, masks)
    same = j % TILE // cap == lane // rows
    position = iota((1, span), 1) % rows
    for n, ids in enumerate((own_ids, neighbour_ids)):
        codes = slot_codes(ids, home_ref[0], rows, cap)
        here = same & (j // TILE % 2 == n)
        hit = jnp.zeros(shape, F32)
        for t in range(TOPK):
            hit += jnp.where(here & (code == by_row(codes, position, rows, t)), 1.0, 0.0)
        out[:, n * span : (n + 1) * span] = hit


def send_kernel(cap, hit_ref, own_hbm, neighbour, *refs):
    blocks, (own, stacked, sem) = refs[:-3], refs[-3:]
    copy = pltpu.make_async_copy(own_hbm, own, sem)
    copy.start()
    rows = own.shape[0]
    parts = TILE // cap
    width = own.shape[1] // parts
    for n, tokens in ((1, neighbour), (0, own)):
        if n == 0:
            copy.wait()
        for q in range(parts):
            start = (n * parts + q) * rows
            stacked[start : start + rows, :] = tokens[:, q * width : (q + 1) * width].astype(F32)
    chosen = matmul(hit_ref[...].astype(BF16), stacked[...].astype(BF16)).astype(BF16)
    for m, block in enumerate(blocks):
        block[...] = chosen[2 * m * TILE : 2 * (m + 1) * TILE]


def unpack_kernel(cap, *refs):
    blocks, out = refs[:-1], refs[-1]
    parts, slots, width = TILE // cap, out.shape[0], blocks[0].shape[1]
    shape = (parts * slots, slots // cap * TILE)
    i, j = iota(shape, 0), iota(shape, 1)
    source = i % slots // cap * TILE + i // slots * cap + i % cap
    arranged = matmul(
        jnp.where(source == j, 1.0, 0.0).astype(BF16),
        jnp.concatenate([b[...] for b in blocks], axis=0),
    ).astype(BF16)
    for q in range(parts):
        out[:, q * width : (q + 1) * width] = arranged[q * slots : (q + 1) * slots]


def pack_kernel(cap, mine_ref, other_ref, *blocks):
    parts, slots = TILE // cap, mine_ref.shape[0]
    width = mine_ref.shape[1] // parts
    total = (mine_ref[...].astype(F32) + other_ref[...].astype(F32)).astype(BF16)
    shape = (slots // cap * TILE, parts * slots)
    j, i = iota(shape, 0), iota(shape, 1)
    source = j % TILE // cap * slots + j // TILE * cap + j % cap
    arranged = matmul(
        jnp.where(source == i, 1.0, 0.0).astype(BF16),
        jnp.concatenate([total[:, q * width : (q + 1) * width] for q in range(parts)], axis=0),
    ).astype(BF16)
    start = 0
    for block in blocks:
        block[...] = arranged[start : start + block.shape[0]]
        start += block.shape[0]


def moved(source, target, sems, k, start, size, units=None):
    here = pl.ds(start, size)
    source = source.at[here] if units is None else source.at[here, units]
    return pltpu.make_async_copy(source, target.at[here], sems.at[k])


def load_kernel(step, half_ref, wg, wu, sg, su, sd, cols, gate, up, s_gate, s_up, s_down, onehot, keep, sems):
    chunks = wg.shape[0] // step
    units = s_gate.shape[1]
    split = units < wg.shape[1]
    used = pl.ds(pl.multiple_of(half_ref[0] * units, units), units) if split else None
    copies = []
    for pairs, part in ((((wg, gate), (wu, up)), None), (((sg, s_gate), (su, s_up)), used)):
        for c in range(chunks):
            for source, target in pairs:
                copies.append(moved(source, target, sems, len(copies), c * step, step, part))
    copies.append(pltpu.make_async_copy(sd.at[used] if split else sd, s_down, sems.at[len(copies)]))
    for copy in copies:
        copy.start()
    outliers = cols.shape[1]
    for c in range(chunks):
        here = slice(c * step, (c + 1) * step)
        hot = jnp.where(iota((step, outliers), 0) + c * step == cols[...], 1.0, 0.0).astype(BF16)
        onehot[here, :] = hot
        count = lax.dot_general(
            jnp.ones((8, outliers), BF16), hot, (((1,), (1,)), ((), ())), preferred_element_type=F32
        )
        keep[:, here] = jnp.where(count == 0.0, 1.0, 0.0)
    for copy in copies:
        copy.wait()


def scaled(codes, scales, block):
    return jnp.concatenate(
        [
            codes[b * block : (b + 1) * block] * jnp.broadcast_to(scales[b : b + 1], (block, codes.shape[1]))
            for b in range(codes.shape[0] // block)
        ],
        axis=0,
    )


def expert_kernel(
    step, wide, count, gate, up, wd, onehot, keep, sg, su, sd, extra_gate, extra_up, *refs
):
    pieces, outs = refs[:count], refs[count : 2 * count]
    down, gate_acc, up_acc, picked, hidden_ref, gate_scale, up_scale, down_scale, sem = refs[2 * count :]
    height = pieces[0].shape[0]
    width, hid = gate.shape
    load = pltpu.make_async_copy(wd, down, sem)
    load.start()
    gate_acc[...] = jnp.zeros_like(gate_acc)
    up_acc[...] = jnp.zeros_like(up_acc)
    picked[...] = jnp.zeros_like(picked)
    gate_scale[...] = sg[...].astype(F32)
    up_scale[...] = su[...].astype(F32)
    down_scale[...] = sd[...].astype(F32)
    block = width // sg.shape[0]
    for c in range(width // step):
        here = slice(c * step, (c + 1) * step)
        there = slice(c * step // block, (c + 1) * step // block)
        whole = jnp.concatenate([piece[:, here] for piece in pieces], axis=0)
        masked = whole * jnp.broadcast_to(keep[0:1, here].astype(BF16), whole.shape)
        picked[...] += matmul(whole, onehot[here, :])
        gate_acc[...] += matmul(masked, scaled(gate[here, :], gate_scale[there, :].astype(BF16), block))
        up_acc[...] += matmul(masked, scaled(up[here, :], up_scale[there, :].astype(BF16), block))

    outliers = picked[...].astype(BF16)
    gate_val = gate_acc[...] + matmul(outliers, extra_gate[...])
    up_val = up_acc[...] + matmul(outliers, extra_up[...])
    hidden_ref[...] = (gate_val / (1.0 + jnp.exp(-gate_val)) * up_val).astype(BF16)
    load.wait()
    tall = hid // sd.shape[0]
    for c in range(width // wide):
        here = slice(c * wide, (c + 1) * wide)
        weights = jnp.concatenate(
            [
                down[b * tall : (b + 1) * tall, here]
                * jnp.broadcast_to(down_scale[b : b + 1, here].astype(BF16), (tall, wide))
                for b in range(hid // tall)
            ],
            axis=0,
        )
        result = matmul(hidden_ref[...], weights).astype(BF16)
        for n, out in enumerate(outs):
            out[:, here] = result[n * height : (n + 1) * height]


def shared_kernel(step, wide, group, split, gate, up, down, *refs):
    pieces, outs = refs[: 2 * group], refs[2 * group : 3 * group]
    rows_ref, gate_acc, up_acc, hidden_ref = refs[3 * group :]
    height = pieces[0].shape[0]
    rows_ref[...] = jnp.concatenate([p[...].astype(F32) for p in pieces], axis=0).astype(BF16)
    gate_acc[...] = jnp.zeros_like(gate_acc)
    up_acc[...] = jnp.zeros_like(up_acc)
    for c in range(gate.shape[0] // step):
        here = slice(c * step, (c + 1) * step)
        gate_acc[...] += matmul(rows_ref[:, here], gate[here, :])
        up_acc[...] += matmul(rows_ref[:, here], up[here, :])
    value = gate_acc[...]
    hidden = value / (1.0 + jnp.exp(-value)) * up_acc[...]
    if not split:
        hidden = jnp.where(iota(hidden.shape, 0) // height % 2 == 0, hidden, 0.0)
    hidden_ref[...] = hidden.astype(BF16)
    for c in range(down.shape[1] // wide):
        here = slice(c * wide, (c + 1) * wide)
        result = matmul(hidden_ref[...], down[:, here])
        for n, out in enumerate(outs):
            out[:, here] = result[2 * n * height : 2 * (n + 1) * height].astype(out.dtype)


def share_kernel(cap, masks, rows, ids_ref, home_ref, weights_ref, out):
    parts = TILE // cap
    codes = slot_codes(ids_ref, home_ref[0], rows, cap)
    weights = [weights_ref[t, r] for r in range(rows) for t in range(TOPK)]
    shape = (parts * rows, out.shape[1])
    i, j = iota(shape, 0), iota(shape, 1)
    code = block_codes(j // TILE, j % cap, cap, masks)
    same = j % TILE // cap == i // rows
    position = iota((parts * rows, 1), 0) % rows
    rest = jnp.zeros(shape, F32)
    for t in range(TOPK):
        rest += jnp.where(
            same & (code == by_row(codes, position, rows, t)),
            by_row(weights, position, rows, t),
            0.0,
        )
    for k in range(3):
        term = rest.astype(BF16)
        out[k * parts * rows : (k + 1) * parts * rows, :] = term
        rest = rest - term.astype(F32)


def combine_kernel(cap, count, first, start, share_ref, mine_ref, *refs):
    others, blocks, out = refs[:count], refs[count:-1], refs[-1]
    rows = out.shape[0]
    parts = TILE // cap
    width = out.shape[1] // parts
    arrived = jnp.concatenate([b[start : start + TILE, :] for b in blocks], axis=0)
    terms = matmul(share_ref[...], arrived)
    size = parts * rows
    routed = terms[:size] + terms[size : 2 * size] + terms[2 * size :]
    for q in range(parts):
        here = slice(q * width, (q + 1) * width)
        total = routed[q * rows : (q + 1) * rows]
        for other in (mine_ref,) + others:
            total += other[:, here].astype(F32)[first : first + rows]
        out[:, here] = total.astype(out.dtype)


def add_kernel(mine_ref, other_ref, out):
    out[...] = (mine_ref[...] + other_ref[...].astype(F32)).astype(out.dtype)


def on_device(
    tokens,
    expert_ids,
    gate_weights,
    w_gate,
    scale_gate,
    w_up,
    scale_up,
    w_down,
    scale_down,
    outlier_cols,
    outlier_gate,
    outlier_up,
    shared_gate,
    shared_up,
    shared_down,
):
    devices = lax.axis_size("ep")
    device = lax.axis_index("ep")
    hid = w_gate.shape[2]
    group = FF // hid
    experts = devices // group
    bits = group.bit_length() - 1
    rows, width = tokens.shape[1], tokens.shape[2]
    cap = max(2, rows * TOPK * 2 // experts)
    home = device // group
    part_width = width * cap // TILE
    slots = experts * cap

    def swap(array, mask):
        return lax.ppermute(array, "ep", [(d, d ^ mask) for d in range(devices)])

    def spread(pieces):
        for bit in range(bits):
            pieces = pieces + [swap(piece, 1 << bit) for piece in pieces]
        return pieces

    current = tokens[0]
    ids, weights = expert_ids[0].T, gate_weights[0].T
    home_ref = home.astype(jnp.int32).reshape(1)
    columns = experts // 2
    masks = [0] + sorted(range(2, experts, 2), key=lambda m: -m.bit_length())

    neighbour_ids, neighbour_weights = swap(ids, group), swap(weights, group)
    neighbour, own_rows = swap(current, group), spread([current])
    hit = pl.pallas_call(
        functools.partial(choose_kernel, cap, masks, rows),
        in_specs=[SMEM] * 3,
        out_specs=VMEM,
        out_shape=jax.ShapeDtypeStruct((columns * 2 * TILE, 2 * TILE // cap * rows), F32),
        compiler_params=params(4),
        cost_estimate=cost(1e6, 1e6),
        name="choose",
    )(ids, neighbour_ids, home_ref)
    hit, neighbour, neighbour_weights, own_rows = lax.optimization_barrier(
        (hit, neighbour, neighbour_weights, own_rows)
    )
    sent = pl.pallas_call(
        functools.partial(send_kernel, cap),
        in_specs=[VMEM, ANY, VMEM],
        out_specs=[VMEM] * columns,
        out_shape=[jax.ShapeDtypeStruct((2 * TILE, part_width), BF16)] * columns,
        scratch_shapes=[
            pltpu.VMEM((rows, width), BF16),
            pltpu.VMEM((2 * TILE // cap * rows, part_width), F32),
            pltpu.SemaphoreType.DMA,
        ],
        compiler_params=params(8),
        cost_estimate=cost(1e8, 1e6),
        name="send",
    )(hit, in_hbm(current), neighbour)

    def across(blocks):
        return [blocks[0]] + [swap(block, mask * group) for mask, block in zip(masks[1:], blocks[1:])]

    arrived = across(sent)
    cols, _ = lax.optimization_barrier((lax.dynamic_slice_in_dim(outlier_cols, home, 1, 0), sent[0]))
    step = 1024
    units = hid // 2 if hid % 256 == 0 else hid
    stored = jax.ShapeDtypeStruct((width, hid), BF16)
    gate, up, *shared_weights, onehot, keep = pl.pallas_call(
        functools.partial(load_kernel, step),
        in_specs=[SMEM] + [ANY] * 5 + [VMEM],
        out_specs=[VMEM] * 7,
        out_shape=[
            stored,
            stored,
            jax.ShapeDtypeStruct((width, units), BF16),
            jax.ShapeDtypeStruct((width, units), BF16),
            jax.ShapeDtypeStruct((units, width), BF16),
            jax.ShapeDtypeStruct((width, outlier_cols.shape[1]), BF16),
            jax.ShapeDtypeStruct((8, width), F32),
        ],
        scratch_shapes=[pltpu.SemaphoreType.DMA((4 * width // step + 1,))],
        compiler_params=params(8),
        cost_estimate=cost(1e9, 4 * hid * width),
        name="load",
    )(
        home_ref & 1,
        in_hbm(w_gate[0]),
        in_hbm(w_up[0]),
        in_hbm(shared_gate[0]),
        in_hbm(shared_up[0]),
        in_hbm(shared_down[0]),
        cols,
    )
    arrived, keep, neighbour = lax.optimization_barrier((arrived, keep, neighbour))
    row_pieces = [p for pair in zip(own_rows, spread([neighbour])) for p in pair]

    whole = jax.ShapeDtypeStruct((slots, width), BF16)
    taken = pl.pallas_call(
        functools.partial(unpack_kernel, cap),
        in_specs=[VMEM] * len(arrived),
        out_specs=VMEM,
        out_shape=whole,
        compiler_params=params(16),
        cost_estimate=cost(1e8, 1e6),
        name="unpack",
    )(*arrived)
    pieces = spread([taken])

    row_pieces, _ = lax.optimization_barrier((row_pieces, taken))
    shared = pl.pallas_call(
        functools.partial(shared_kernel, step, 1024, group, units < hid),
        in_specs=[VMEM] * (3 + 2 * group),
        out_specs=[VMEM] * group,
        out_shape=[jax.ShapeDtypeStruct((2 * rows, width), F32)]
        + [jax.ShapeDtypeStruct((2 * rows, width), BF16)] * (group - 1),
        scratch_shapes=[
            pltpu.VMEM((2 * group * rows, width), BF16),
            pltpu.VMEM((2 * group * rows, units), F32),
            pltpu.VMEM((2 * group * rows, units), F32),
            pltpu.VMEM((2 * group * rows, units), BF16),
        ],
        compiler_params=params(12),
        cost_estimate=cost(6 * group * rows * width * hid, 3 * hid * width),
        name="shared",
    )(*shared_weights, *row_pieces)
    pieces, first = lax.optimization_barrier((pieces, shared[0]))
    shared = [first] + list(shared[1:])
    others = [swap(shared[n], n) for n in range(1, group)]

    partials = pl.pallas_call(
        functools.partial(expert_kernel, step, 1024, group),
        in_specs=[VMEM, VMEM, ANY] + [VMEM] * (7 + group),
        out_specs=[VMEM] * group,
        out_shape=[whole] * group,
        scratch_shapes=[
            pltpu.VMEM((hid, width), BF16),
            pltpu.VMEM((group * slots, hid), F32),
            pltpu.VMEM((group * slots, hid), F32),
            pltpu.VMEM((group * slots, outlier_cols.shape[1]), F32),
            pltpu.VMEM((group * slots, hid), BF16),
            pltpu.VMEM(scale_gate.shape[1:], F32),
            pltpu.VMEM(scale_up.shape[1:], F32),
            pltpu.VMEM(scale_down.shape[1:], F32),
            pltpu.SemaphoreType.DMA,
        ],
        compiler_params=params(24),
        cost_estimate=cost(6 * group * slots * width * hid, 6 * hid * width),
        name="expert",
    )(
        gate,
        up,
        in_hbm(w_down[0]),
        onehot,
        keep,
        scale_gate[0],
        scale_up[0],
        scale_down[0],
        outlier_gate[0],
        outlier_up[0],
        *pieces,
    )

    for bit in reversed(range(1, bits)):
        half = 1 << bit
        partials = [
            (mine.astype(F32) + swap(other, half).astype(F32)).astype(BF16)
            for mine, other in zip(partials[:half], partials[half:])
        ]
    returning = pl.pallas_call(
        functools.partial(pack_kernel, cap),
        in_specs=[VMEM] * 2,
        out_specs=[VMEM] * columns,
        out_shape=[jax.ShapeDtypeStruct((2 * TILE, part_width), BF16)] * columns,
        compiler_params=params(16),
        cost_estimate=cost(1e8, 1e6),
        name="pack",
    )(partials[0], swap(partials[1], 1))
    returned = across(returning)

    def share(ids, weights):
        return pl.pallas_call(
            functools.partial(share_kernel, cap, masks, rows),
            in_specs=[SMEM] * 3,
            out_specs=VMEM,
            out_shape=jax.ShapeDtypeStruct((3 * TILE // cap * rows, columns * TILE), BF16),
            compiler_params=params(4),
            cost_estimate=cost(1e6, 1e5),
            name="share",
        )(ids, home_ref, weights)

    def combine(own, shares):
        return pl.pallas_call(
            functools.partial(
                combine_kernel, cap, group - 1, 0 if own else rows, 0 if own else TILE
            ),
            in_specs=[VMEM] * (1 + group + columns),
            out_specs=VMEM,
            out_shape=jax.ShapeDtypeStruct((rows, width), F32 if own else BF16),
            compiler_params=params(16),
            cost_estimate=cost(1e8, 1e6),
            name="combine",
        )(shares, shared[0], *others, *returned)

    shares = [share(neighbour_ids, neighbour_weights), share(ids, weights)]
    shares, others = lax.optimization_barrier((shares, others))
    crossing = combine(False, shares[0])
    mine, crossing = lax.optimization_barrier((shares[1], crossing))
    mine = combine(True, mine)
    out = pl.pallas_call(
        add_kernel,
        in_specs=[VMEM] * 2,
        out_specs=VMEM,
        out_shape=jax.ShapeDtypeStruct((rows, width), BF16),
        compiler_params=params(4),
        cost_estimate=cost(1e6, 1e6),
        name="add",
    )(mine, swap(crossing, group))
    return out[None]


def solution(mesh):
    rows = P(None, ("parts", "ep"), None)
    held = P("ep", None, None)
    placed = (rows, rows, rows) + (held,) * 6 + (P(),) + (held,) * 5
    return jax.shard_map(
        on_device, mesh=mesh, in_specs=placed, out_specs=rows, check_vma=False
    )
```

time: 65.3 us -> 52.5 us (0.80)
  starting transfers between devices: 26.5 us -> 16 us
  waiting for transfers between devices: 7.63 us -> 14.6 us
  Pallas kernels: 27.5 us -> 20.7 us
  local copies, waits for them, and re-layouts: 3.18 us -> 0.75 us
    ppermute x18 -> x15, starting transfers between devices: 26.5 us -> 16 us  [swap(): return lax.ppermute(array, 'ep', [(d, d ^ mask) for d in range(devices)])]
    ppermute x18 -> x15, waiting for transfers between devices: 7.63 us -> 14.6 us  [swap(): return lax.ppermute(array, 'ep', [(d, d ^ mask) for d in range(devices)])]
    pallas_call x7 -> x12, Pallas kernels: 27.5 us -> 20.7 us  [the longest x1 8.84 us: on_device(): pl.pallas_call(functools.partial(load_kernel, step), in_specs=[SMEM] + [A...]
    unnamed x22, local copies, waits for them, and re-layouts: 3.17 us -> 0.75 us
  transfers between devices with their start and end apart: 18 -> 15, of which waited for: 6 -> 6; matrix products, arithmetic and copies ran while one was open for 0% -> 0% of each run, Pallas kernels for 27% -> 27%
where the time goes in v2:
time: 52.5 us; the launch traced here: 52.3 us
  Pallas kernels  20.7 us (39%)
  starting transfers between devices  16 us (30%)
  waiting for transfers between devices  14.6 us (28%)
  local copies, waits for them, and re-layouts  0.75 us (1%)
    ppermute x15, starting transfers between devices, swap(): return lax.ppermute(array, 'ep', [(d, d ^ mask) for d in range(devices)])  16 us
    ppermute x15, waiting for transfers between devices, swap(): return lax.ppermute(array, 'ep', [(d, d ^ mask) for d in range(devices)])  14.6 us
    pallas_call x1, Pallas kernels, on_device(): pl.pallas_call(functools.partial(load_kernel, step), in_specs=[SMEM] + [A...  8.84 us
    pallas_call x1, Pallas kernels, on_device(): pl.pallas_call(functools.partial(expert_kernel, step, 1024, group), in_sp...  4.5 us
    pallas_call x1, Pallas kernels, on_device(): pl.pallas_call(functools.partial(shared_kernel, step, 1024, group, units...  2.07 us
    pallas_call x2, Pallas kernels, share(): pl.pallas_call(functools.partial(share_kernel, cap, masks, rows), in_spec...  1.51 us
    pallas_call x1, Pallas kernels, on_device(): pl.pallas_call(functools.partial(send_kernel, cap), in_specs=[VMEM, ANY,...  1.16 us
  transfers between devices with their start and end apart: 15, of which 6 were waited for; matrix products, arithmetic and copies ran while one was open for 0% of the time, Pallas kernels for 27%

profile of v2, /device:TPU:0, one launch (start us, length us, event | category | flops | bytes accessed | tf_op | source)
XLA Modules:
  0.0 52.3 jit_solution(11459307748498661891)
XLA Ops:
  0.0 3.0 %collective-permute-start.1 = (bf16[8,7168]{1,0:T(8,128)(2,1)}, bf16[8,7168]{1,0:T(8,128)(2,1)S(1)}, u32[]{:S(2)}, u32[]{:S(2)}) collective-permute-start(bf16[8,7168]{1,0:T(8,128)(2,1)} %bitcast.22), channel_id=1, source_target_pairs={{0,2},{1,3},{2,0},{3,1},{4,6},{5,7},{6,4},{7,5},{8,10},{9,11},{10,... | collective-permute-start | bytes 344072 | tf_op jit(solution)/shard_map/ppermute | solution.py:316
  3.0 0.1 collective-permute-start
  3.1 1.9 %collective-permute-start.2 = (f32[2,8]{1,0:T(2,128)}, f32[2,8]{1,0:T(2,128)S(1)}, u32[]{:S(2)}, u32[]{:S(2)}) collective-permute-start(f32[2,8]{1,0:T(2,128)} %bitcast.32), channel_id=1, source_target_pairs={{0,2},{1,3},{2,0},{3,1},{4,6},{5,7},{6,4},{7,5},{8,10},{9,11},{10,... | collective-permute-start | bytes 200 | tf_op jit(solution)/shard_map/ppermute | solution.py:316
  5.0 1.8 %collective-permute-done.neighbour_ids.ids_ref = s32[2,8]{1,0:T(2,128)S(1)} collective-permute-done((s32[2,8]{1,0:T(2,128)}, s32[2,8]{1,0:T(2,128)S(1)}, u32[]{:S(2)}, u32[]{:S(2)}) %collective-permute-start) | collective-permute-done | bytes 96 | tf_op jit(solution)/shard_map/ppermute | solution.py:316
  6.8 0.7 %copy-done.8 = s32[1,8,2]{1,2,0:T(2,128)S(1)} copy-done((s32[1,8,2]{1,2,0:T(2,128)S(1)}, s32[1,8,2]{1,2,0:T(2,128)}, u32[]{:S(2)}) %copy-start.8) | copy-done | bytes 88
  7.4 0.9 %choose.1.hit_ref = f32[128,64]{1,0:T(8,128)S(1)} custom-call(s32[2,8]{1,0:T(2,128)S(1)} %bitcast.30, s32[2,8]{1,0:T(2,128)S(1)} %collective-permute-done.neighbour_ids.ids_ref, s32[1]{0:T(128)} %bitcast.2.home_ref), custom_call_target="tpu_custom_call" | custom-call | flops 1000000 | bytes 1000000 | tf_op jit(solution)/shard_map/choose/pallas_call | solution.py:331
  8.4 1.2 %send.1 = (bf16[32,1792]{1,0:T(8,128)(2,1)S(1)}, bf16[32,1792]{1,0:T(8,128)(2,1)S(1)}, bf16[32,1792]{1,0:T(8,128)(2,1)S(1)}, bf16[32,1792]{1,0:T(8,128)(2,1)S(1)}) custom-call(f32[128,64]{1,0:T(8,128)S(1)} %choose.1.hit_ref, bf16[8,7168]{1,0:T(8,128)(2,1)} %bitcast.24, bf16[8,7168]{1,0:T(8,128)(2,1)S(1)} %collective-permute-done.1.neighbour.refs_1_), custom_call_target="tpu_custom_call" | custom-call | flops 100000000 | bytes 1000000 | tf_op jit(solution)/shard_map/send/pallas_call | solution.py:343
  9.5 2.7 %collective-permute-start.4 = (bf16[32,1792]{1,0:T(8,128)(2,1)S(1)}, bf16[32,1792]{1,0:T(8,128)(2,1)S(1)}, u32[]{:S(2)}, u32[]{:S(2)}) collective-permute-start(bf16[32,1792]{1,0:T(8,128)(2,1)S(1)} %get-tuple-element.57), channel_id=1, source_target_pairs={{0,8},{1,9},{2,10},{3,11},{4,12},{5,13},{6,14},{7,15},{8,0},{9,1},... | collective-permute-start | bytes 344072 | tf_op jit(solution)/shard_map/ppermute | solution.py:316
  12.2 1.3 %collective-permute-start.5 = (bf16[32,1792]{1,0:T(8,128)(2,1)S(1)}, bf16[32,1792]{1,0:T(8,128)(2,1)S(1)}, u32[]{:S(2)}, u32[]{:S(2)}) collective-permute-start(bf16[32,1792]{1,0:T(8,128)(2,1)S(1)} %get-tuple-element.58), channel_id=1, source_target_pairs={{0,12},{1,13},{2,14},{3,15},{4,8},{5,9},{6,10},{7,11},{8,4},{9,5},... | collective-permute-start | bytes 344072 | tf_op jit(solution)/shard_map/ppermute | solution.py:316
  13.5 0.2 collective-permute-start.6
  13.8 8.8 %load.1 = (bf16[7168,512]{1,0:T(8,128)(2,1)S(1)}, bf16[7168,512]{1,0:T(8,128)(2,1)S(1)}, bf16[7168,256]{1,0:T(8,128)(2,1)S(1)}, bf16[7168,256]{1,0:T(8,128)(2,1)...) custom-call(s32[1]{0:T(128)S(6)} %and.10.half_ref, ...), custom_call_target="tpu_custom_call" | custom-call | flops 1000000000 | bytes 14680064 | tf_op jit(solution)/shard_map/load/pallas_call | solution.py:366
  22.7 0.3 unpack.1.refs_0_
  23.0 0.1 collective-permute-start.9
  23.1 0.5 collective-permute-start.7
  23.6 1.5 %collective-permute-done.7.refs_3_ = bf16[8,7168]{1,0:T(8,128)(2,1)S(1)} collective-permute-done((bf16[8,7168]{1,0:T(8,128)(2,1)S(1)}, bf16[8,7168]{1,0:T(8,128)(2,1)S(1)}, u32[]{:S(2)}, u32[]{:S(2)}) %collective-permute-start.7) | collective-permute-done | bytes 114720 | tf_op jit(solution)/shard_map/ppermute | solution.py:316
  25.1 2.1 %shared.1 = (f32[16,7168]{1,0:T(8,128)S(1)}, bf16[16,7168]{1,0:T(8,128)(2,1)S(1)}) custom-call(bf16[7168,256]{1,0:T(8,128)(2,1)S(1)} %get-tuple-element.53.gate, bf16[7168,256]{1,0:T(8,128)(2,1)S(1)} %get-tuple-element.54.up, bf16[256,7168]{1,0:T(8,128)(2,1)S(1)} %get-tuple-element.55.down, bf16[8,7168]{1,0:T(8,128)(2,1)S(1)} %bitcast.25, ...), custom_call_target="tpu_custom_call" | custom-call | flops 352321536 | bytes 11010048 | tf_op jit(solution)/shard_map/shared/pallas_call | solution.py:408
  27.2 4.5 %expert.1 = (bf16[32,7168]{1,0:T(8,128)(2,1)S(1)}, bf16[32,7168]{1,0:T(8,128)(2,1)S(1)}) custom-call(bf16[7168,512]{1,0:T(8,128)(2,1)S(1)} %get-tuple-element.77.gate, bf16[7168,512]{1,0:T(8,128)(2,1)S(1)} %get-tuple-element.78.up, bf16[512,7168]{1,0:T(8,128)(2,1)} %bitcast.34, bf16[7168,128]{1,0:T(8,128)(2,1)S(1)} %get-tuple-element.79.onehot, ...), custom_call_target="tpu_custom_call" | custom-call | flops 1409286144 | bytes 22020096 | tf_op jit(solution)/shard_map/expert/pallas_call | solution.py:428
  31.8 0.2 collective-permute-start.10
  32.0 0.4 collective-permute-start.8
  32.3 1.3 %collective-permute-done.10.other_ref = bf16[32,7168]{1,0:T(8,128)(2,1)S(1)} collective-permute-done((bf16[32,7168]{1,0:T(8,128)(2,1)S(1)}, bf16[32,7168]{1,0:T(8,128)(2,1)S(1)}, u32[]{:S(2)}, u32[]{:S(2)}) %collective-permute-start.10) | collective-permute-done | bytes 458784 | tf_op jit(solution)/shard_map/ppermute | solution.py:316
  33.6 0.3 pack.1
  33.9 2.9 %collective-permute-start.11 = (bf16[32,1792]{1,0:T(8,128)(2,1)S(1)}, bf16[32,1792]{1,0:T(8,128)(2,1)S(1)}, u32[]{:S(2)}, u32[]{:S(2)}) collective-permute-start(bf16[32,1792]{1,0:T(8,128)(2,1)S(1)} %get-tuple-element.86), channel_id=1, source_target_pairs={{0,8},{1,9},{2,10},{3,11},{4,12},{5,13},{6,14},{7,15},{8,0},{9,1},... | collective-permute-start | bytes 344072 | tf_op jit(solution)/shard_map/ppermute | solution.py:316
  36.8 1.3 %collective-permute-start.12 = (bf16[32,1792]{1,0:T(8,128)(2,1)S(1)}, bf16[32,1792]{1,0:T(8,128)(2,1)S(1)}, u32[]{:S(2)}, u32[]{:S(2)}) collective-permute-start(bf16[32,1792]{1,0:T(8,128)(2,1)S(1)} %get-tuple-element.87), channel_id=1, source_target_pairs={{0,12},{1,13},{2,14},{3,15},{4,8},{5,9},{6,10},{7,11},{8,4},{9,5},... | collective-permute-start | bytes 344072 | tf_op jit(solution)/shard_map/ppermute | solution.py:316
  38.2 0.8 %share.3.share_ref = bf16[96,64]{1,0:T(8,128)(2,1)S(1)} custom-call(s32[2,8]{1,0:T(2,128)S(1)} %bitcast.31, s32[1]{0:T(128)} %bitcast.2.home_ref, f32[2,8]{1,0:T(2,128)S(1)} %bitcast.33), custom_call_target="tpu_custom_call" | custom-call | flops 1000000 | bytes 100000 | tf_op jit(solution)/shard_map/share/pallas_call | solution.py:479
  38.9 0.8 %share.2.share_ref = bf16[96,64]{1,0:T(8,128)(2,1)S(1)} custom-call(s32[2,8]{1,0:T(2,128)S(1)} %collective-permute-done.neighbour_ids.ids_ref, s32[1]{0:T(128)} %bitcast.2.home_ref, f32[2,8]{1,0:T(2,128)S(1)} %collective-permute-done.2.weights_ref), custom_call_target="tpu_custom_call" | custom-call | flops 1000000 | bytes 100000 | tf_op jit(solution)/shard_map/share/pallas_call | solution.py:479
  39.7 6.1 %collective-permute-done.11.refs_2_ = bf16[32,1792]{1,0:T(8,128)(2,1)S(1)} collective-permute-done((bf16[32,1792]{1,0:T(8,128)(2,1)S(1)}, bf16[32,1792]{1,0:T(8,128)(2,1)S(1)}, u32[]{:S(2)}, u32[]{:S(2)}) %collective-permute-start.11) | collective-permute-done | bytes 114720 | tf_op jit(solution)/shard_map/ppermute | solution.py:316
  45.8 0.7 %collective-permute-done.13.refs_4_ = bf16[32,1792]{1,0:T(8,128)(2,1)S(1)} collective-permute-done((bf16[32,1792]{1,0:T(8,128)(2,1)S(1)}, bf16[32,1792]{1,0:T(8,128)(2,1)S(1)}, u32[]{:S(2)}, u32[]{:S(2)}) %collective-permute-start.13) | collective-permute-done | bytes 114720 | tf_op jit(solution)/shard_map/ppermute | solution.py:316
  46.5 0.2 combine.2
  46.8 1.4 %collective-permute-start.14 = (bf16[8,7168]{1,0:T(8,128)(2,1)S(1)}, bf16[8,7168]{1,0:T(8,128)(2,1)S(1)}, u32[]{:S(2)}, u32[]{:S(2)}) collective-permute-start(bf16[8,7168]{1,0:T(8,128)(2,1)S(1)} %combine.2), channel_id=1, source_target_pairs={{0,2},{1,3},{2,0},{3,1},{4,6},{5,7},{6,4},{7,5},{8,10},{9,11},{10,... | collective-permute-start | bytes 344072 | tf_op jit(solution)/shard_map/ppermute | solution.py:316
  48.2 0.2 combine.3.mine_ref
  48.4 3.2 %collective-permute-done.14.other_ref = bf16[8,7168]{1,0:T(8,128)(2,1)S(1)} collective-permute-done((bf16[8,7168]{1,0:T(8,128)(2,1)S(1)}, bf16[8,7168]{1,0:T(8,128)(2,1)S(1)}, u32[]{:S(2)}, u32[]{:S(2)}) %collective-permute-start.14) | collective-permute-done | bytes 114720 | tf_op jit(solution)/shard_map/ppermute | solution.py:316
  51.6 0.7 %add.6 = bf16[8,7168]{1,0:T(8,128)(2,1)} custom-call(f32[8,7168]{1,0:T(8,128)S(1)} %combine.3.mine_ref, bf16[8,7168]{1,0:T(8,128)(2,1)S(1)} %collective-permute-done.14.other_ref), custom_call_target="tpu_custom_call" | custom-call | flops 1000000 | bytes 1000000 | tf_op jit(solution)/shard_map/add/pallas_call | solution.py:507
  (33 shorter events, 0.1 us)
Async XLA Ops:
  0.0 13.8 %copy-start = (s32[8,128]{1,0:T(8,128)S(1)}, s32[8,128]{1,0:T(8,128)}, u32[]{:S(2)}) copy-start(s32[8,128]{1,0:T(8,128)} %param.24) | copy-start | bytes 12292
  0.0 8.4 %collective-permute-start.1 = (bf16[8,7168]{1,0:T(8,128)(2,1)}, bf16[8,7168]{1,0:T(8,128)(2,1)S(1)}, u32[]{:S(2)}, u32[]{:S(2)}) collective-permute-start(bf16[8,7168]{1,0:T(8,128)(2,1)} %bitcast.22), channel_id=1, source_target_pairs={{0,2},{1,3},{2,0},{3,1},{4,6},{5,7},{6,4},{7,5},{8,10},{9,11},{10,... | collective-permute-start | bytes 344072 | tf_op jit(solution)/shard_map/ppermute | solution.py:316
  3.0 5.4 %collective-permute-start.3 = (bf16[8,7168]{1,0:T(8,128)(2,1)}, bf16[8,7168]{1,0:T(8,128)(2,1)S(1)}, u32[]{:S(2)}, u32[]{:S(2)}) collective-permute-start(bf16[8,7168]{1,0:T(8,128)(2,1)} %bitcast.23), channel_id=1, source_target_pairs={{0,1},{1,0},{2,3},{3,2},{4,5},{5,4},{6,7},{7,6},{8,9},{9,8},{10,11... | collective-permute-start | bytes 344072 | tf_op jit(solution)/shard_map/ppermute | solution.py:316
  3.0 3.8 %collective-permute-start = (s32[2,8]{1,0:T(2,128)}, s32[2,8]{1,0:T(2,128)S(1)}, u32[]{:S(2)}, u32[]{:S(2)}) collective-permute-start(s32[2,8]{1,0:T(2,128)} %bitcast.29), channel_id=1, source_target_pairs={{0,2},{1,3},{2,0},{3,1},{4,6},{5,7},{6,4},{7,5},{8,10},{9,11},{10,... | collective-permute-start | bytes 200 | tf_op jit(solution)/shard_map/ppermute | solution.py:316
  3.1 5.2 %collective-permute-start.2 = (f32[2,8]{1,0:T(2,128)}, f32[2,8]{1,0:T(2,128)S(1)}, u32[]{:S(2)}, u32[]{:S(2)}) collective-permute-start(f32[2,8]{1,0:T(2,128)} %bitcast.32), channel_id=1, source_target_pairs={{0,2},{1,3},{2,0},{3,1},{4,6},{5,7},{6,4},{7,5},{8,10},{9,11},{10,... | collective-permute-start | bytes 200 | tf_op jit(solution)/shard_map/ppermute | solution.py:316
  6.8 0.7 %copy-start.8 = (s32[1,8,2]{1,2,0:T(2,128)S(1)}, s32[1,8,2]{1,2,0:T(2,128)}, u32[]{:S(2)}) copy-start(s32[1,8,2]{1,2,0:T(2,128)} %param.16) | copy-start | bytes 196
  9.5 13.2 %collective-permute-start.4 = (bf16[32,1792]{1,0:T(8,128)(2,1)S(1)}, bf16[32,1792]{1,0:T(8,128)(2,1)S(1)}, u32[]{:S(2)}, u32[]{:S(2)}) collective-permute-start(bf16[32,1792]{1,0:T(8,128)(2,1)S(1)} %get-tuple-element.57), channel_id=1, source_target_pairs={{0,8},{1,9},{2,10},{3,11},{4,12},{5,13},{6,14},{7,15},{8,0},{9,1},... | collective-permute-start | bytes 344072 | tf_op jit(solution)/shard_map/ppermute | solution.py:316
  12.2 10.5 %collective-permute-start.5 = (bf16[32,1792]{1,0:T(8,128)(2,1)S(1)}, bf16[32,1792]{1,0:T(8,128)(2,1)S(1)}, u32[]{:S(2)}, u32[]{:S(2)}) collective-permute-start(bf16[32,1792]{1,0:T(8,128)(2,1)S(1)} %get-tuple-element.58), channel_id=1, source_target_pairs={{0,12},{1,13},{2,14},{3,15},{4,8},{5,9},{6,10},{7,11},{8,4},{9,5},... | collective-permute-start | bytes 344072 | tf_op jit(solution)/shard_map/ppermute | solution.py:316
  13.5 9.2 %collective-permute-start.6 = (bf16[32,1792]{1,0:T(8,128)(2,1)S(1)}, bf16[32,1792]{1,0:T(8,128)(2,1)S(1)}, u32[]{:S(2)}, u32[]{:S(2)}) collective-permute-start(bf16[32,1792]{1,0:T(8,128)(2,1)S(1)} %get-tuple-element.59), channel_id=1, source_target_pairs={{0,4},{1,5},{2,6},{3,7},{4,0},{5,1},{6,2},{7,3},{8,12},{9,13},{10,... | collective-permute-start | bytes 344072 | tf_op jit(solution)/shard_map/ppermute | solution.py:316
  13.8 11.3 %copy-start.4 = (bf16[1,8,7168]{2,1,0:T(8,128)(2,1)S(1)}, bf16[1,8,7168]{2,1,0:T(8,128)(2,1)}, u32[]{:S(2)}) copy-start(bf16[1,8,7168]{2,1,0:T(8,128)(2,1)} %param.15) | copy-start | bytes 344068
  22.7 4.5 %copy-start.2 = (bf16[1,128,512]{2,1,0:T(8,128)(2,1)S(1)}, bf16[1,128,512]{2,1,0:T(8,128)(2,1)}, u32[]{:S(2)}) copy-start(bf16[1,128,512]{2,1,0:T(8,128)(2,1)} %param.25) | copy-start | bytes 393220
  22.7 4.5 %copy-start.3 = (bf16[1,128,512]{2,1,0:T(8,128)(2,1)S(1)}, bf16[1,128,512]{2,1,0:T(8,128)(2,1)}, u32[]{:S(2)}) copy-start(bf16[1,128,512]{2,1,0:T(8,128)(2,1)} %param.26) | copy-start | bytes 393220
  22.7 4.5 %copy-start.5 = (bf16[1,56,512]{2,1,0:T(8,128)(2,1)S(1)}, bf16[1,56,512]{2,1,0:T(8,128)(2,1)}, u32[]{:S(2)}) copy-start(bf16[1,56,512]{2,1,0:T(8,128)(2,1)} %param.19) | copy-start | bytes 172036
  22.7 4.5 %copy-start.6 = (bf16[1,56,512]{2,1,0:T(8,128)(2,1)S(1)}, bf16[1,56,512]{2,1,0:T(8,128)(2,1)}, u32[]{:S(2)}) copy-start(bf16[1,56,512]{2,1,0:T(8,128)(2,1)} %param.21) | copy-start | bytes 172036
  22.7 4.5 %copy-start.7 = (bf16[1,4,7168]{2,1,0:T(4,128)(2,1)S(1)}, bf16[1,4,7168]{2,1,0:T(4,128)(2,1)}, u32[]{:S(2)}) copy-start(bf16[1,4,7168]{2,1,0:T(4,128)(2,1)} %param.23) | copy-start | bytes 172036
  23.0 4.1 %collective-permute-start.9 = (bf16[32,7168]{1,0:T(8,128)(2,1)S(1)}, bf16[32,7168]{1,0:T(8,128)(2,1)S(1)}, u32[]{:S(2)}, u32[]{:S(2)}) collective-permute-start(bf16[32,7168]{1,0:T(8,128)(2,1)S(1)} %unpack.1.refs_0_), channel_id=1, source_target_pairs={{0,1},{1,0},{2,3},{3,2},{4,5},{5,4},{6,7},{7,6},{8,9},{9,8},{10,11... | collective-permute-start | bytes 1376264 | tf_op jit(solution)/shard_map/ppermute | solution.py:316
  23.1 2.0 %collective-permute-start.7 = (bf16[8,7168]{1,0:T(8,128)(2,1)S(1)}, bf16[8,7168]{1,0:T(8,128)(2,1)S(1)}, u32[]{:S(2)}, u32[]{:S(2)}) collective-permute-start(bf16[8,7168]{1,0:T(8,128)(2,1)S(1)} %collective-permute-done.1.neighbour.refs_1_), channel_id=1, source_target_pairs={{0,1},{1,0},{2,3},{3,2},{4,5},{5,4},{6,7},{7,6},{8,9},{9,8},{10,11... | collective-permute-start | bytes 344072 | tf_op jit(solution)/shard_map/ppermute | solution.py:316
  27.2 10.9 %copy-start.9 = (s32[1,8,2]{1,2,0:T(2,128)S(1)}, s32[1,8,2]{1,2,0:T(2,128)}, u32[]{:S(2)}) copy-start(s32[1,8,2]{1,2,0:T(2,128)} %param.16) | copy-start | bytes 196
  27.2 10.9 %copy-start.10 = (f32[1,8,2]{1,2,0:T(2,128)S(1)}, f32[1,8,2]{1,2,0:T(2,128)}, u32[]{:S(2)}) copy-start(f32[1,8,2]{1,2,0:T(2,128)} %param.17) | copy-start | bytes 196
  27.2 25.1 %copy-start.1 = (s32[8,128]{1,0:T(8,128)S(1)}, s32[8,128]{1,0:T(8,128)}, u32[]{:S(2)}) copy-start(s32[8,128]{1,0:T(8,128)} %param.24) | copy-start | bytes 12292
  31.8 1.9 %collective-permute-start.10 = (bf16[32,7168]{1,0:T(8,128)(2,1)S(1)}, bf16[32,7168]{1,0:T(8,128)(2,1)S(1)}, u32[]{:S(2)}, u32[]{:S(2)}) collective-permute-start(bf16[32,7168]{1,0:T(8,128)(2,1)S(1)} %get-tuple-element.84), channel_id=1, source_target_pairs={{0,1},{1,0},{2,3},{3,2},{4,5},{5,4},{6,7},{7,6},{8,9},{9,8},{10,11... | collective-permute-start | bytes 1376264 | tf_op jit(solution)/shard_map/ppermute | solution.py:316
  32.0 7.7 %collective-permute-start.8 = (bf16[16,7168]{1,0:T(8,128)(2,1)S(1)}, bf16[16,7168]{1,0:T(8,128)(2,1)S(1)}, u32[]{:S(2)}, u32[]{:S(2)}) collective-permute-start(bf16[16,7168]{1,0:T(8,128)(2,1)S(1)} %get-tuple-element.71), channel_id=1, source_target_pairs={{0,1},{1,0},{2,3},{3,2},{4,5},{5,4},{6,7},{7,6},{8,9},{9,8},{10,11... | collective-permute-start | bytes 688136 | tf_op jit(solution)/shard_map/ppermute | solution.py:316
  33.9 11.9 %collective-permute-start.11 = (bf16[32,1792]{1,0:T(8,128)(2,1)S(1)}, bf16[32,1792]{1,0:T(8,128)(2,1)S(1)}, u32[]{:S(2)}, u32[]{:S(2)}) collective-permute-start(bf16[32,1792]{1,0:T(8,128)(2,1)S(1)} %get-tuple-element.86), channel_id=1, source_target_pairs={{0,8},{1,9},{2,10},{3,11},{4,12},{5,13},{6,14},{7,15},{8,0},{9,1},... | collective-permute-start | bytes 344072 | tf_op jit(solution)/shard_map/ppermute | solution.py:316
  36.8 9.0 %collective-permute-start.12 = (bf16[32,1792]{1,0:T(8,128)(2,1)S(1)}, bf16[32,1792]{1,0:T(8,128)(2,1)S(1)}, u32[]{:S(2)}, u32[]{:S(2)}) collective-permute-start(bf16[32,1792]{1,0:T(8,128)(2,1)S(1)} %get-tuple-element.87), channel_id=1, source_target_pairs={{0,12},{1,13},{2,14},{3,15},{4,8},{5,9},{6,10},{7,11},{8,4},{9,5},... | collective-permute-start | bytes 344072 | tf_op jit(solution)/shard_map/ppermute | solution.py:316
  38.1 8.4 %collective-permute-start.13 = (bf16[32,1792]{1,0:T(8,128)(2,1)S(1)}, bf16[32,1792]{1,0:T(8,128)(2,1)S(1)}, u32[]{:S(2)}, u32[]{:S(2)}) collective-permute-start(bf16[32,1792]{1,0:T(8,128)(2,1)S(1)} %get-tuple-element.88), channel_id=1, source_target_pairs={{0,4},{1,5},{2,6},{3,7},{4,0},{5,1},{6,2},{7,3},{8,12},{9,13},{10,... | collective-permute-start | bytes 344072 | tf_op jit(solution)/shard_map/ppermute | solution.py:316
  46.8 4.9 %collective-permute-start.14 = (bf16[8,7168]{1,0:T(8,128)(2,1)S(1)}, bf16[8,7168]{1,0:T(8,128)(2,1)S(1)}, u32[]{:S(2)}, u32[]{:S(2)}) collective-permute-start(bf16[8,7168]{1,0:T(8,128)(2,1)S(1)} %combine.2), channel_id=1, source_target_pairs={{0,2},{1,3},{2,0},{3,1},{4,6},{5,7},{6,4},{7,5},{8,10},{9,11},{10,... | collective-permute-start | bytes 344072 | tf_op jit(solution)/shard_map/ppermute | solution.py:316

commit v3 on v2

v3 whole, which is shorter than its diff:
```python
import functools

import jax
import jax.numpy as jnp
from jax import lax
from jax.experimental import pallas as pl
from jax.experimental.pallas import tpu as pltpu
from jax.sharding import PartitionSpec as P

FF = 1024
TOPK = 2
TILE = 16
LANES = 128
BF16 = jnp.bfloat16
F32 = jnp.float32
VMEM = pl.BlockSpec(memory_space=pltpu.VMEM)
ANY = pl.BlockSpec(memory_space=pl.ANY)
SMEM = pl.BlockSpec(memory_space=pltpu.SMEM)


def params(mib):
    return pltpu.CompilerParams(vmem_limit_bytes=mib << 20)


def cost(flops, nbytes):
    return pl.CostEstimate(flops=int(flops), bytes_accessed=int(nbytes), transcendentals=0)


def matmul(left, right):
    return jnp.dot(left, right, preferred_element_type=F32)


def in_hbm(array):
    return pltpu.with_memory_space_constraint(array, pltpu.HBM)


def iota(shape, dim):
    return lax.broadcasted_iota(jnp.int32, shape, dim)


def by_row(values, position, choice):
    out = jnp.zeros(position.shape, values[0].dtype)
    for r in range(len(values) // TOPK):
        out = jnp.where(position == r, values[r * TOPK + choice], out)
    return out


def slot_marks(ids_ref, weights_ref, home, rows, cap):
    pairs = [(r, t) for r in range(rows) for t in range(TOPK)]
    ids = [ids_ref[t, r] for r, t in pairs]
    weights = [weights_ref[t, r] for r, t in pairs]
    own, other = [], []
    for n, e in enumerate(ids):
        place = jnp.int32(0)
        for earlier in ids[:n]:
            place += (earlier == e).astype(jnp.int32)
        apart = e ^ home
        code = (apart >> 1) * cap + place
        own.append(jnp.where(apart & 1 == 0, code, -1))
        other.append(jnp.where(apart & 1 == 1, code, -1))
    shape = (rows, LANES)
    position, lane = iota(shape, 0), iota(shape, 1)
    quarter = LANES // 4
    marks = [jnp.zeros(shape, F32), jnp.zeros(shape, F32)]
    for t in range(TOPK):
        rest = by_row(weights, position, t)
        value = jnp.ones(shape, F32)
        for k in range(1, 4):
            term = rest.astype(BF16).astype(F32)
            value = jnp.where(lane // quarter == k, term, value)
            rest = rest - term
        for n, codes in enumerate((own, other)):
            marks[n] += jnp.where(lane % quarter == by_row(codes, position, t), value, 0.0)
    return marks


def block_lanes(shape, dim, cap, masks):
    j = iota(shape, dim)
    lane = j % cap
    for n, mask in enumerate(masks):
        lane += jnp.where(j // TILE == n, mask // 2 * cap, 0)
    return lane, j % TILE // cap


def tiled(marks, cap):
    return jnp.concatenate([marks.astype(F32)] * (TILE // cap), axis=0).astype(BF16)


def lanes_dot(left, right):
    return lax.dot_general(left, right, (((1,), (1,)), ((), ())), preferred_element_type=F32)


def write_blocks(cap, masks, marks, tokens, stacked, blocks):
    rows = marks.shape[0]
    parts = TILE // cap
    width = blocks[0].shape[1]
    height = len(blocks) * TILE
    lane, part = block_lanes((height, LANES), 0, cap, masks)
    wanted = jnp.where(lane == iota((height, LANES), 1), 1.0, 0.0).astype(BF16)
    hit = lanes_dot(wanted, tiled(marks, cap))
    part = block_lanes(hit.shape, 0, cap, masks)[1]
    hit = jnp.where(part == iota(hit.shape, 1) // rows, hit, 0.0)
    for q in range(parts):
        stacked[q * rows : (q + 1) * rows, :] = tokens[:, q * width : (q + 1) * width].astype(F32)
    chosen = matmul(hit.astype(BF16), stacked[...].astype(BF16)).astype(BF16)
    for m, block in enumerate(blocks):
        block[...] = chosen[m * TILE : (m + 1) * TILE]


def first_kernel(cap, masks, home_ref, ids_hbm, weights_hbm, own_hbm, other_ref, marks_ref, *refs):
    blocks, (ids_ref, weights_ref, own, stacked, sems) = refs[:-5], refs[-5:]
    small = [
        pltpu.make_async_copy(ids_hbm, ids_ref, sems.at[1]),
        pltpu.make_async_copy(weights_hbm, weights_ref, sems.at[2]),
    ]
    copy = pltpu.make_async_copy(own_hbm, own, sems.at[0])
    for each in small:
        each.start()
    copy.start()
    for each in small:
        each.wait()
    rows = own.shape[0]
    marks, other = slot_marks(ids_ref, weights_ref, home_ref[0], rows, cap)
    marks_ref[...] = marks.astype(BF16)
    other_ref[...] = other.astype(BF16)
    copy.wait()
    write_blocks(cap, masks, marks, own, stacked, blocks)


def send_kernel(cap, masks, marks, tokens, *refs):
    count = len(masks)
    own, blocks, stacked = refs[:count], refs[count : 2 * count], refs[2 * count]
    for mine, block in zip(own, blocks):
        block[:TILE, :] = mine[...]
    lower = [block.at[pl.ds(TILE, TILE)] for block in blocks]
    write_blocks(cap, masks, marks[...], tokens, stacked, lower)


def unpack_kernel(cap, *refs):
    blocks, out = refs[:-1], refs[-1]
    parts, slots, width = TILE // cap, out.shape[0], blocks[0].shape[1]
    shape = (parts * slots, slots // cap * TILE)
    i, j = iota(shape, 0), iota(shape, 1)
    source = i % slots // cap * TILE + i // slots * cap + i % cap
    arranged = matmul(
        jnp.where(source == j, 1.0, 0.0).astype(BF16),
        jnp.concatenate([b[...] for b in blocks], axis=0),
    ).astype(BF16)
    for q in range(parts):
        out[:, q * width : (q + 1) * width] = arranged[q * slots : (q + 1) * slots]


def pack_kernel(cap, mine_ref, other_ref, *blocks):
    parts, slots = TILE // cap, mine_ref.shape[0]
    width = mine_ref.shape[1] // parts
    total = (mine_ref[...].astype(F32) + other_ref[...].astype(F32)).astype(BF16)
    shape = (slots // cap * TILE, parts * slots)
    j, i = iota(shape, 0), iota(shape, 1)
    source = j % TILE // cap * slots + j // TILE * cap + j % cap
    arranged = matmul(
        jnp.where(source == i, 1.0, 0.0).astype(BF16),
        jnp.concatenate([total[:, q * width : (q + 1) * width] for q in range(parts)], axis=0),
    ).astype(BF16)
    start = 0
    for block in blocks:
        block[...] = arranged[start : start + block.shape[0]]
        start += block.shape[0]


def moved(source, target, sems, k, start, size, units=None):
    here = pl.ds(start, size)
    source = source.at[here] if units is None else source.at[here, units]
    return pltpu.make_async_copy(source, target.at[here], sems.at[k])


def load_kernel(step, wg, wu, cols, gate, up, onehot, keep, sems):
    chunks = wg.shape[0] // step
    copies = [
        moved(source, target, sems, 2 * c + k, c * step, step)
        for c in range(chunks)
        for k, (source, target) in enumerate(((wg, gate), (wu, up)))
    ]
    for copy in copies:
        copy.start()
    outliers = cols.shape[1]
    for c in range(chunks):
        here = slice(c * step, (c + 1) * step)
        hot = jnp.where(iota((step, outliers), 0) + c * step == cols[...], 1.0, 0.0).astype(BF16)
        onehot[here, :] = hot
        count = lanes_dot(jnp.ones((8, outliers), BF16), hot)
        keep[:, here] = jnp.where(count == 0.0, 1.0, 0.0)
    for copy in copies:
        copy.wait()


def scaled(codes, scales, block):
    return jnp.concatenate(
        [
            codes[b * block : (b + 1) * block] * jnp.broadcast_to(scales[b : b + 1], (block, codes.shape[1]))
            for b in range(codes.shape[0] // block)
        ],
        axis=0,
    )


def expert_kernel(
    step, wide, count, gate, up, wd, onehot, keep, sg, su, sd, extra_gate, extra_up, *refs
):
    pieces, outs = refs[:count], refs[count : 2 * count]
    down, gate_acc, up_acc, picked, hidden_ref, gate_scale, up_scale, down_scale, sem = refs[2 * count :]
    height = pieces[0].shape[0]
    width, hid = gate.shape
    chunks = width // step
    load = pltpu.make_async_copy(wd, down, sem)
    load.start()
    gate_acc[...] = jnp.zeros_like(gate_acc)
    up_acc[...] = jnp.zeros_like(up_acc)
    picked[...] = jnp.zeros_like(picked)
    gate_scale[...] = sg[...].astype(F32)
    up_scale[...] = su[...].astype(F32)
    down_scale[...] = sd[...].astype(F32)
    block = width // sg.shape[0]
    for c in range(chunks):
        here = slice(c * step, (c + 1) * step)
        there = slice(c * step // block, (c + 1) * step // block)
        whole = jnp.concatenate([piece[:, here] for piece in pieces], axis=0)
        masked = whole * jnp.broadcast_to(keep[0:1, here].astype(BF16), whole.shape)
        picked[...] += matmul(whole, onehot[here, :])
        gate_acc[...] += matmul(masked, scaled(gate[here, :], gate_scale[there, :].astype(BF16), block))
        up_acc[...] += matmul(masked, scaled(up[here, :], up_scale[there, :].astype(BF16), block))

    outliers = picked[...].astype(BF16)
    gate_val = gate_acc[...] + matmul(outliers, extra_gate[...])
    up_val = up_acc[...] + matmul(outliers, extra_up[...])
    hidden_ref[...] = (gate_val / (1.0 + jnp.exp(-gate_val)) * up_val).astype(BF16)
    load.wait()
    tall = hid // sd.shape[0]
    for c in range(width // wide):
        here = slice(c * wide, (c + 1) * wide)
        weights = jnp.concatenate(
            [
                down[b * tall : (b + 1) * tall, here]
                * jnp.broadcast_to(down_scale[b : b + 1, here].astype(BF16), (tall, wide))
                for b in range(hid // tall)
            ],
            axis=0,
        )
        result = matmul(hidden_ref[...], weights).astype(BF16)
        for n, out in enumerate(outs):
            out[:, here] = result[n * height : (n + 1) * height]


def shared_kernel(step, wide, group, half_ref, wg, wu, wd, *refs):
    pieces, outs = refs[: 2 * group], refs[2 * group : 4 * group]
    gate, up, down, rows_ref, gate_acc, up_acc, hidden_ref, sems = refs[4 * group :]
    height = pieces[0].shape[0]
    width, units = gate.shape
    chunks = width // step
    split = units < wg.shape[1]
    used = pl.ds(pl.multiple_of(half_ref[0] * units, units), units) if split else None
    copies = []
    for c in range(chunks):
        for source, target in ((wg, gate), (wu, up)):
            copies.append(moved(source, target, sems, len(copies), c * step, step, used))
    copies.append(pltpu.make_async_copy(wd.at[used] if split else wd, down, sems.at[len(copies)]))
    for copy in copies:
        copy.start()
    rows_ref[...] = jnp.concatenate([p[:, :width].astype(F32) for p in pieces], axis=0).astype(BF16)
    gate_acc[...] = jnp.zeros_like(gate_acc)
    up_acc[...] = jnp.zeros_like(up_acc)
    for c in range(chunks):
        here = slice(c * step, (c + 1) * step)
        copies[2 * c].wait()
        gate_acc[...] += matmul(rows_ref[:, here], gate[here, :])
        copies[2 * c + 1].wait()
        up_acc[...] += matmul(rows_ref[:, here], up[here, :])
    value = gate_acc[...]
    hidden = value / (1.0 + jnp.exp(-value)) * up_acc[...]
    if not split:
        hidden = jnp.where(iota(hidden.shape, 0) // height % 2 == 0, hidden, 0.0)
    hidden_ref[...] = hidden.astype(BF16)
    copies[-1].wait()
    for c in range(width // wide):
        here = slice(c * wide, (c + 1) * wide)
        result = matmul(hidden_ref[...], down[:, here])
        for n, out in enumerate(outs):
            out[:, here] = result[n * height : (n + 1) * height].astype(out.dtype)


def share_kernel(cap, masks, *refs):
    for marks, out in zip(refs[: len(refs) // 2], refs[len(refs) // 2 :]):
        rows = marks.shape[0]
        size, height = TILE // cap * rows, out.shape[1]
        repeated = tiled(marks[...], cap)
        lane, _ = block_lanes((height, LANES), 0, cap, masks)
        part = block_lanes((size, height), 1, cap, masks)[1]
        same = part == iota((size, height), 0) // rows
        for k in range(3):
            wanted = lane + (k + 1) * (LANES // 4) == iota((height, LANES), 1)
            term = lanes_dot(repeated, jnp.where(wanted, 1.0, 0.0).astype(BF16))
            out[k * size : (k + 1) * size, :] = jnp.where(same, term, 0.0).astype(BF16)


def combine_kernel(cap, start, share_ref, *refs):
    blocks, out = refs[:-1], refs[-1]
    rows = out.shape[0]
    parts = TILE // cap
    width = out.shape[1] // parts
    arrived = jnp.concatenate([b[start : start + TILE, :] for b in blocks], axis=0)
    terms = matmul(share_ref[...], arrived)
    size = parts * rows
    routed = terms[:size] + terms[size : 2 * size] + terms[2 * size :]
    for q in range(parts):
        out[:, q * width : (q + 1) * width] = routed[q * rows : (q + 1) * rows]


def merge_kernel(routed, *refs):
    out = refs[-1]
    total = routed[...]
    for part in refs[:-1]:
        total += part[...].astype(F32)
    out[...] = total.astype(out.dtype)


def add_kernel(mine_ref, other_ref, out):
    out[...] = (mine_ref[...] + other_ref[...].astype(F32)).astype(out.dtype)


def on_device(
    tokens,
    expert_ids,
    gate_weights,
    w_gate,
    scale_gate,
    w_up,
    scale_up,
    w_down,
    scale_down,
    outlier_cols,
    outlier_gate,
    outlier_up,
    shared_gate,
    shared_up,
    shared_down,
):
    devices = lax.axis_size("ep")
    device = lax.axis_index("ep")
    hid = w_gate.shape[2]
    group = FF // hid
    experts = devices // group
    bits = group.bit_length() - 1
    rows, width = tokens.shape[1], tokens.shape[2]
    cap = max(2, rows * TOPK * 2 // experts)
    home = device // group
    part_width = width * cap // TILE
    slots = experts * cap

    def swap(array, mask):
        return lax.ppermute(array, "ep", [(d, d ^ mask) for d in range(devices)])

    def spread(pieces):
        for bit in range(bits):
            pieces = pieces + [swap(piece, 1 << bit) for piece in pieces]
        return pieces

    current = tokens[0]
    ids, weights = expert_ids[0].T, gate_weights[0].T
    home_ref = home.astype(jnp.int32).reshape(1)
    columns = experts // 2
    masks = [0] + sorted(range(2, experts, 2), key=lambda m: -m.bit_length())

    parts = TILE // cap
    sent_block = jax.ShapeDtypeStruct((TILE, part_width), BF16)
    stack = pltpu.VMEM((parts * rows, part_width), F32)
    marks_to_send, marks, *own_blocks = pl.pallas_call(
        functools.partial(first_kernel, cap, masks),
        in_specs=[SMEM] + [ANY] * 3,
        out_specs=[VMEM] * (2 + columns),
        out_shape=[
            jax.ShapeDtypeStruct((rows, LANES), BF16),
            jax.ShapeDtypeStruct((rows, LANES), BF16),
        ]
        + [sent_block] * columns,
        scratch_shapes=[
            pltpu.SMEM(ids.shape, jnp.int32),
            pltpu.SMEM(weights.shape, F32),
            pltpu.VMEM((rows, width), BF16),
            stack,
            pltpu.SemaphoreType.DMA((3,)),
        ],
        compiler_params=params(8),
        cost_estimate=cost(1e8, 1e6),
        name="first",
    )(home_ref, in_hbm(ids), in_hbm(weights), in_hbm(current))
    def across(blocks):
        return [blocks[0]] + [swap(block, mask * group) for mask, block in zip(masks[1:], blocks[1:])]

    neighbour, neighbour_marks = swap(current, group), swap(marks_to_send, group)
    blocks = pl.pallas_call(
        functools.partial(send_kernel, cap, masks),
        in_specs=[VMEM] * (2 + columns),
        out_specs=[VMEM] * columns,
        out_shape=[jax.ShapeDtypeStruct((2 * TILE, part_width), BF16)] * columns,
        scratch_shapes=[stack],
        compiler_params=params(8),
        cost_estimate=cost(1e8, 1e6),
        name="send",
    )(neighbour_marks, neighbour, *own_blocks)
    arrived = across(blocks)

    cols, _ = lax.optimization_barrier((lax.dynamic_slice_in_dim(outlier_cols, home, 1, 0), blocks[0]))
    step = 1024
    units = hid // 2 if hid % 256 == 0 else hid
    gate, up, onehot, keep = pl.pallas_call(
        functools.partial(load_kernel, step),
        in_specs=[ANY, ANY, VMEM],
        out_specs=[VMEM] * 4,
        out_shape=[
            jax.ShapeDtypeStruct((width, hid), BF16),
            jax.ShapeDtypeStruct((width, hid), BF16),
            jax.ShapeDtypeStruct((width, outlier_cols.shape[1]), BF16),
            jax.ShapeDtypeStruct((8, width), F32),
        ],
        scratch_shapes=[pltpu.SemaphoreType.DMA((2 * width // step,))],
        compiler_params=params(8),
        cost_estimate=cost(1e9, 2 * hid * width),
        name="load",
    )(in_hbm(w_gate[0]), in_hbm(w_up[0]), cols)
    arrived, keep = lax.optimization_barrier((arrived, keep))

    whole = jax.ShapeDtypeStruct((slots, width), BF16)
    taken = pl.pallas_call(
        functools.partial(unpack_kernel, cap),
        in_specs=[VMEM] * len(arrived),
        out_specs=VMEM,
        out_shape=whole,
        compiler_params=params(16),
        cost_estimate=cost(1e8, 1e6),
        name="unpack",
    )(*arrived)
    pieces = spread([taken])

    neighbour_marks, _ = lax.optimization_barrier((neighbour_marks, taken))
    back = list(range(columns))
    shares = pl.pallas_call(
        functools.partial(share_kernel, cap, [masks[n] for n in back]),
        in_specs=[VMEM] * 2,
        out_specs=[VMEM] * 2,
        out_shape=[jax.ShapeDtypeStruct((3 * parts * rows, columns * TILE), BF16)] * 2,
        compiler_params=params(4),
        cost_estimate=cost(1e6, 1e5),
        name="share",
    )(neighbour_marks, marks)
    pieces, shares = lax.optimization_barrier((pieces, shares))

    partials = pl.pallas_call(
        functools.partial(expert_kernel, step, 1024, group),
        in_specs=[VMEM, VMEM, ANY] + [VMEM] * (7 + group),
        out_specs=[VMEM] * group,
        out_shape=[whole] * group,
        scratch_shapes=[
            pltpu.VMEM((hid, width), BF16),
            pltpu.VMEM((group * slots, hid), F32),
            pltpu.VMEM((group * slots, hid), F32),
            pltpu.VMEM((group * slots, outlier_cols.shape[1]), F32),
            pltpu.VMEM((group * slots, hid), BF16),
            pltpu.VMEM(scale_gate.shape[1:], F32),
            pltpu.VMEM(scale_up.shape[1:], F32),
            pltpu.VMEM(scale_down.shape[1:], F32),
            pltpu.SemaphoreType.DMA,
        ],
        compiler_params=params(24),
        cost_estimate=cost(6 * group * slots * width * hid, 6 * hid * width),
        name="expert",
    )(
        gate,
        up,
        in_hbm(w_down[0]),
        onehot,
        keep,
        scale_gate[0],
        scale_up[0],
        scale_down[0],
        outlier_gate[0],
        outlier_up[0],
        *pieces,
    )

    for bit in reversed(range(1, bits)):
        half = 1 << bit
        partials = [
            (mine.astype(F32) + swap(other, half).astype(F32)).astype(BF16)
            for mine, other in zip(partials[:half], partials[half:])
        ]
    returning = pl.pallas_call(
        functools.partial(pack_kernel, cap),
        in_specs=[VMEM] * 2,
        out_specs=[VMEM] * columns,
        out_shape=[jax.ShapeDtypeStruct((2 * TILE, part_width), BF16)] * columns,
        compiler_params=params(16),
        cost_estimate=cost(1e8, 1e6),
        name="pack",
    )(partials[0], swap(partials[1], 1))
    returned = [across(returning)[n] for n in back]

    row_pieces = [p for pair in zip(spread([current]), spread([neighbour])) for p in pair]
    row_pieces, _ = lax.optimization_barrier((row_pieces, returning[0]))
    shared = pl.pallas_call(
        functools.partial(shared_kernel, step, 1024, group),
        in_specs=[SMEM] + [ANY] * 3 + [VMEM] * (2 * group),
        out_specs=[VMEM] * (2 * group),
        out_shape=[jax.ShapeDtypeStruct((rows, width), F32)] * 2
        + [jax.ShapeDtypeStruct((rows, width), BF16)] * (2 * group - 2),
        scratch_shapes=[
            pltpu.VMEM((width, units), BF16),
            pltpu.VMEM((width, units), BF16),
            pltpu.VMEM((units, width), BF16),
            pltpu.VMEM((2 * group * rows, width), BF16),
            pltpu.VMEM((2 * group * rows, units), F32),
            pltpu.VMEM((2 * group * rows, units), F32),
            pltpu.VMEM((2 * group * rows, units), BF16),
            pltpu.SemaphoreType.DMA((2 * width // step + 1,)),
        ],
        compiler_params=params(24),
        cost_estimate=cost(6 * group * rows * width * hid, 3 * hid * width),
        name="shared",
    )(
        home_ref & 1,
        in_hbm(shared_gate[0]),
        in_hbm(shared_up[0]),
        in_hbm(shared_down[0]),
        *row_pieces,
    )
    shared_sums = [[shared[k]] + [swap(shared[2 * n + k], n) for n in range(1, group)] for k in (0, 1)]
    def combine(own, shares):
        return pl.pallas_call(
            functools.partial(combine_kernel, cap, 0 if own else TILE),
            in_specs=[VMEM] * (1 + columns),
            out_specs=VMEM,
            out_shape=jax.ShapeDtypeStruct((rows, width), F32),
            compiler_params=params(16),
            cost_estimate=cost(1e8, 1e6),
            name="combine",
        )(shares, *returned)

    def merge(own, routed):
        return pl.pallas_call(
            merge_kernel,
            in_specs=[VMEM] * (1 + group),
            out_specs=VMEM,
            out_shape=jax.ShapeDtypeStruct((rows, width), F32 if own else BF16),
            compiler_params=params(8),
            cost_estimate=cost(1e6, 1e6),
            name="merge",
        )(routed, *shared_sums[0 if own else 1])

    crossing = combine(False, shares[0])
    shared_sums[1], crossing = lax.optimization_barrier((shared_sums[1], crossing))
    crossing = merge(False, crossing)
    mine, crossing = lax.optimization_barrier((shares[1], crossing))
    mine = merge(True, combine(True, mine))
    out = pl.pallas_call(
        add_kernel,
        in_specs=[VMEM] * 2,
        out_specs=VMEM,
        out_shape=jax.ShapeDtypeStruct((rows, width), BF16),
        compiler_params=params(4),
        cost_estimate=cost(1e6, 1e6),
        name="add",
    )(mine, swap(crossing, group))
    return out[None]


def solution(mesh):
    rows = P(None, ("parts", "ep"), None)
    held = P("ep", None, None)
    placed = (rows, rows, rows) + (held,) * 6 + (P(),) + (held,) * 5
    return jax.shard_map(
        on_device, mesh=mesh, in_specs=placed, out_specs=rows, check_vma=False
    )
```

time: 52.5 us -> 47.6 us (0.907)
  starting transfers between devices: 16 us -> 13.6 us
  Pallas kernels: 20.7 us -> 18.8 us
  local copies, waits for them, and re-layouts: 0.75 us -> 0.05 us
    ppermute x15, starting transfers between devices: 16 us -> 13.6 us  [swap(): return lax.ppermute(array, 'ep', [(d, d ^ mask) for d in range(devices)])]
    pallas_call x8 -> x9, Pallas kernels: 15 us -> 13 us  [the longest x1 5.53 us: on_device(): pl.pallas_call(functools.partial(load_kernel, step), in_specs=[ANY, ANY,...]
    unnamed x22 -> x16, local copies, waits for them, and re-layouts: 0.75 us -> 0.04 us
  transfers between devices with their start and end apart: 15 -> 15, of which waited for: 6 -> 8; matrix products, arithmetic and copies ran while one was open for 0% -> 0% of each run, Pallas kernels for 27% -> 27%
where the time goes in v3:
time: 47.6 us; the launch traced here: 47.5 us
  Pallas kernels  18.8 us (39%)
  waiting for transfers between devices  14.9 us (31%)
  starting transfers between devices  13.6 us (29%)
    ppermute x15, waiting for transfers between devices, swap(): return lax.ppermute(array, 'ep', [(d, d ^ mask) for d in range(devices)])  14.9 us
    ppermute x15, starting transfers between devices, swap(): return lax.ppermute(array, 'ep', [(d, d ^ mask) for d in range(devices)])  13.6 us
    pallas_call x1, Pallas kernels, on_device(): pl.pallas_call(functools.partial(load_kernel, step), in_specs=[ANY, ANY,...  5.53 us
    pallas_call x1, Pallas kernels, on_device(): pl.pallas_call(functools.partial(shared_kernel, step, 1024, group), in_sp...  5.13 us
    pallas_call x1, Pallas kernels, on_device(): pl.pallas_call(functools.partial(expert_kernel, step, 1024, group), in_sp...  4.52 us
    pallas_call x1, Pallas kernels, on_device(): pl.pallas_call(functools.partial(first_kernel, cap, masks), in_specs=[SME...  1.32 us
  transfers between devices with their start and end apart: 15, of which 8 were waited for; matrix products, arithmetic and copies ran while one was open for 0% of the time, Pallas kernels for 27%

profile of v3, /device:TPU:0, one launch (start us, length us, event | category | flops | bytes accessed | tf_op | source)
XLA Modules:
  0.0 47.5 jit_solution(14327077338416709633)
XLA Ops:
  0.0 3.0 %collective-permute-start.1 = (bf16[8,7168]{1,0:T(8,128)(2,1)}, bf16[8,7168]{1,0:T(8,128)(2,1)S(1)}, u32[]{:S(2)}, u32[]{:S(2)}) collective-permute-start(bf16[8,7168]{1,0:T(8,128)(2,1)} %bitcast.22), channel_id=1, source_target_pairs={{0,2},{1,3},{2,0},{3,1},{4,6},{5,7},{6,4},{7,5},{8,10},{9,11},{10,... | collective-permute-start | bytes 344072 | tf_op jit(solution)/shard_map/ppermute | solution.py:359
  3.0 1.3 %first.1 = (bf16[8,128]{1,0:T(8,128)(2,1)S(1)}, bf16[8,128]{1,0:T(8,128)(2,1)S(1)}, bf16[16,1792]{1,0:T(8,128)(2,1)S(1)}, bf16[16,1792]{1,0:T(8,128)(2,1)S(1)}, ...) custom-call(s32[1]{0:T(128)} %bitcast.home_ref, s32[2,8]{1,0:T(2,128)} %bitcast.35, f32[2,8]{1,0:T(2,128)} %bitcast.36, ...), custom_call_target="tpu_custom_call" | custom-call | flops 100000000 | bytes 1000000 | tf_op jit(solution)/shard_map/first/pallas_call | solution.py:375
  4.3 0.1 collective-permute-start
  4.4 3.6 %collective-permute-done.marks.refs_0_ = bf16[8,128]{1,0:T(8,128)(2,1)S(1)} collective-permute-done((bf16[8,128]{1,0:T(8,128)(2,1)S(1)}, bf16[8,128]{1,0:T(8,128)(2,1)S(1)}, u32[]{:S(2)}, u32[]{:S(2)}) %collective-permute-start) | collective-permute-done | bytes 2080 | tf_op jit(solution)/shard_map/ppermute | solution.py:359
  8.0 0.3 send.1
  8.3 2.7 %collective-permute-start.2 = (bf16[32,1792]{1,0:T(8,128)(2,1)S(1)}, bf16[32,1792]{1,0:T(8,128)(2,1)S(1)}, u32[]{:S(2)}, u32[]{:S(2)}) collective-permute-start(bf16[32,1792]{1,0:T(8,128)(2,1)S(1)} %get-tuple-element.57), channel_id=1, source_target_pairs={{0,8},{1,9},{2,10},{3,11},{4,12},{5,13},{6,14},{7,15},{8,0},{9,1},... | collective-permute-start | bytes 344072 | tf_op jit(solution)/shard_map/ppermute | solution.py:359
  10.9 1.3 %collective-permute-start.3 = (bf16[32,1792]{1,0:T(8,128)(2,1)S(1)}, bf16[32,1792]{1,0:T(8,128)(2,1)S(1)}, u32[]{:S(2)}, u32[]{:S(2)}) collective-permute-start(bf16[32,1792]{1,0:T(8,128)(2,1)S(1)} %get-tuple-element.58), channel_id=1, source_target_pairs={{0,12},{1,13},{2,14},{3,15},{4,8},{5,9},{6,10},{7,11},{8,4},{9,5},... | collective-permute-start | bytes 344072 | tf_op jit(solution)/shard_map/ppermute | solution.py:359
  12.3 0.2 collective-permute-start.4
  12.6 5.5 %load.1 = (bf16[7168,512]{1,0:T(8,128)(2,1)S(1)}, bf16[7168,512]{1,0:T(8,128)(2,1)S(1)}, bf16[7168,128]{1,0:T(8,128)(2,1)S(1)}, f32[8,7168]{1,0:T(8,128)S(1)}) custom-call(bf16[7168,512]{1,0:T(8,128)(2,1)} %bitcast.29, bf16[7168,512]{1,0:T(8,128)(2,1)} %bitcast.30, s32[1,128]{1,0:T(1,128)S(1)} %constant_dynamic-slice_fusion.cols), custom_call_target="tpu_custom_call" | custom-call | flops 1000000000 | bytes 7340032 | tf_op jit(solution)/shard_map/load/pallas_call | solution.py:414
  18.1 1.0 %collective-permute-done.2.refs_1_ = bf16[32,1792]{1,0:T(8,128)(2,1)S(1)} collective-permute-done((bf16[32,1792]{1,0:T(8,128)(2,1)S(1)}, bf16[32,1792]{1,0:T(8,128)(2,1)S(1)}, u32[]{:S(2)}, u32[]{:S(2)}) %collective-permute-start.2) | collective-permute-done | bytes 114720 | tf_op jit(solution)/shard_map/ppermute | solution.py:359
  19.1 0.2 collective-permute-done.4.refs_3_
  19.3 0.3 unpack.1.refs_0_
  19.6 0.2 share.1
  19.8 1.6 %collective-permute-done.5.refs_1_ = bf16[32,7168]{1,0:T(8,128)(2,1)S(1)} collective-permute-done((bf16[32,7168]{1,0:T(8,128)(2,1)S(1)}, bf16[32,7168]{1,0:T(8,128)(2,1)S(1)}, u32[]{:S(2)}, u32[]{:S(2)}) %collective-permute-start.5) | collective-permute-done | bytes 458784 | tf_op jit(solution)/shard_map/ppermute | solution.py:359
  21.5 4.5 %expert.1 = (bf16[32,7168]{1,0:T(8,128)(2,1)S(1)}, bf16[32,7168]{1,0:T(8,128)(2,1)S(1)}) custom-call(bf16[7168,512]{1,0:T(8,128)(2,1)S(1)} %get-tuple-element.71.gate, bf16[7168,512]{1,0:T(8,128)(2,1)S(1)} %get-tuple-element.72.up, bf16[512,7168]{1,0:T(8,128)(2,1)} %bitcast.31, bf16[7168,128]{1,0:T(8,128)(2,1)S(1)} %get-tuple-element.73.onehot, ...), custom_call_target="tpu_custom_call" | custom-call | flops 1409286144 | bytes 22020096 | tf_op jit(solution)/shard_map/expert/pallas_call | solution.py:456
  26.0 0.2 collective-permute-start.8
  26.2 0.4 collective-permute-start.6
  26.6 0.1 collective-permute-start.7
  26.7 1.2 %collective-permute-done.8.other_ref = bf16[32,7168]{1,0:T(8,128)(2,1)S(1)} collective-permute-done((bf16[32,7168]{1,0:T(8,128)(2,1)S(1)}, bf16[32,7168]{1,0:T(8,128)(2,1)S(1)}, u32[]{:S(2)}, u32[]{:S(2)}) %collective-permute-start.8) | collective-permute-done | bytes 458784 | tf_op jit(solution)/shard_map/ppermute | solution.py:359
  27.9 0.3 pack.1
  28.2 3.8 %collective-permute-start.10 = (bf16[32,1792]{1,0:T(8,128)(2,1)S(1)}, bf16[32,1792]{1,0:T(8,128)(2,1)S(1)}, u32[]{:S(2)}, u32[]{:S(2)}) collective-permute-start(bf16[32,1792]{1,0:T(8,128)(2,1)S(1)} %get-tuple-element.87), channel_id=1, source_target_pairs={{0,8},{1,9},{2,10},{3,11},{4,12},{5,13},{6,14},{7,15},{8,0},{9,1},... | collective-permute-start | bytes 344072 | tf_op jit(solution)/shard_map/ppermute | solution.py:359
  32.0 0.4 collective-permute-start.11
  32.4 0.2 collective-permute-start.12
  32.6 5.1 %shared.1 = (f32[8,7168]{1,0:T(8,128)S(1)}, f32[8,7168]{1,0:T(8,128)S(1)}, bf16[8,7168]{1,0:T(8,128)(2,1)S(1)}, bf16[8,7168]{1,0:T(8,128)(2,1)S(1)}) custom-call(s32[1]{0:T(128)S(6)} %and.10.half_ref, bf16[7168,512]{1,0:T(8,128)(2,1)} %bitcast.32, bf16[7168,512]{1,0:T(8,128)(2,1)} %bitcast.33, bf16[512,7168]{1,0:T(8,128)(2,1)} %bitcast.34, ...), custom_call_target="tpu_custom_call" | custom-call | flops 352321536 | bytes 11010048 | tf_op jit(solution)/shard_map/shared/pallas_call | solution.py:508
  37.8 0.5 %collective-permute-start.13 = (bf16[8,7168]{1,0:T(8,128)(2,1)S(1)}, bf16[8,7168]{1,0:T(8,128)(2,1)S(1)}, u32[]{:S(2)}, u32[]{:S(2)}) collective-permute-start(bf16[8,7168]{1,0:T(8,128)(2,1)S(1)} %get-tuple-element.95), channel_id=1, source_target_pairs={{0,1},{1,0},{2,3},{3,2},{4,5},{5,4},{6,7},{7,6},{8,9},{9,8},{10,11... | collective-permute-start | bytes 344072 | tf_op jit(solution)/shard_map/ppermute | solution.py:359
  38.3 2.3 %collective-permute-done.10.refs_1_ = bf16[32,1792]{1,0:T(8,128)(2,1)S(1)} collective-permute-done((bf16[32,1792]{1,0:T(8,128)(2,1)S(1)}, bf16[32,1792]{1,0:T(8,128)(2,1)S(1)}, u32[]{:S(2)}, u32[]{:S(2)}) %collective-permute-start.10) | collective-permute-done | bytes 114720 | tf_op jit(solution)/shard_map/ppermute | solution.py:359
  40.6 1.1 %collective-permute-done.12.refs_3_ = bf16[32,1792]{1,0:T(8,128)(2,1)S(1)} collective-permute-done((bf16[32,1792]{1,0:T(8,128)(2,1)S(1)}, bf16[32,1792]{1,0:T(8,128)(2,1)S(1)}, u32[]{:S(2)}, u32[]{:S(2)}) %collective-permute-start.12) | collective-permute-done | bytes 114720 | tf_op jit(solution)/shard_map/ppermute | solution.py:359
  41.7 0.2 combine.2.routed
  42.0 0.6 %collective-permute-start.14 = (bf16[8,7168]{1,0:T(8,128)(2,1)S(1)}, bf16[8,7168]{1,0:T(8,128)(2,1)S(1)}, u32[]{:S(2)}, u32[]{:S(2)}) collective-permute-start(bf16[8,7168]{1,0:T(8,128)(2,1)S(1)} %merge.2), channel_id=1, source_target_pairs={{0,2},{1,3},{2,0},{3,1},{4,6},{5,7},{6,4},{7,5},{8,10},{9,11},{10,... | collective-permute-start | bytes 344072 | tf_op jit(solution)/shard_map/ppermute | solution.py:359
  42.6 0.2 combine.3.routed
  42.8 4.0 %collective-permute-done.14.other_ref = bf16[8,7168]{1,0:T(8,128)(2,1)S(1)} collective-permute-done((bf16[8,7168]{1,0:T(8,128)(2,1)S(1)}, bf16[8,7168]{1,0:T(8,128)(2,1)S(1)}, u32[]{:S(2)}, u32[]{:S(2)}) %collective-permute-start.14) | collective-permute-done | bytes 114720 | tf_op jit(solution)/shard_map/ppermute | solution.py:359
  46.8 0.7 %add.6 = bf16[8,7168]{1,0:T(8,128)(2,1)} custom-call(f32[8,7168]{1,0:T(8,128)S(1)} %merge.3.mine_ref, bf16[8,7168]{1,0:T(8,128)(2,1)S(1)} %collective-permute-done.14.other_ref), custom_call_target="tpu_custom_call" | custom-call | flops 1000000 | bytes 1000000 | tf_op jit(solution)/shard_map/add/pallas_call | solution.py:562
  (28 shorter events, 0.3 us)
Async XLA Ops:
  0.0 12.5 %copy-start = (s32[8,128]{1,0:T(8,128)S(1)}, s32[8,128]{1,0:T(8,128)}, u32[]{:S(2)}) copy-start(s32[8,128]{1,0:T(8,128)} %param.24) | copy-start | bytes 12292
  0.0 7.9 %collective-permute-start.1 = (bf16[8,7168]{1,0:T(8,128)(2,1)}, bf16[8,7168]{1,0:T(8,128)(2,1)S(1)}, u32[]{:S(2)}, u32[]{:S(2)}) collective-permute-start(bf16[8,7168]{1,0:T(8,128)(2,1)} %bitcast.22), channel_id=1, source_target_pairs={{0,2},{1,3},{2,0},{3,1},{4,6},{5,7},{6,4},{7,5},{8,10},{9,11},{10,... | collective-permute-start | bytes 344072 | tf_op jit(solution)/shard_map/ppermute | solution.py:359
  4.3 3.7 %collective-permute-start = (bf16[8,128]{1,0:T(8,128)(2,1)S(1)}, bf16[8,128]{1,0:T(8,128)(2,1)S(1)}, u32[]{:S(2)}, u32[]{:S(2)}) collective-permute-start(bf16[8,128]{1,0:T(8,128)(2,1)S(1)} %get-tuple-element.51), channel_id=1, source_target_pairs={{0,2},{1,3},{2,0},{3,1},{4,6},{5,7},{6,4},{7,5},{8,10},{9,11},{10,... | collective-permute-start | bytes 6152 | tf_op jit(solution)/shard_map/ppermute | solution.py:359
  8.3 10.8 %collective-permute-start.2 = (bf16[32,1792]{1,0:T(8,128)(2,1)S(1)}, bf16[32,1792]{1,0:T(8,128)(2,1)S(1)}, u32[]{:S(2)}, u32[]{:S(2)}) collective-permute-start(bf16[32,1792]{1,0:T(8,128)(2,1)S(1)} %get-tuple-element.57), channel_id=1, source_target_pairs={{0,8},{1,9},{2,10},{3,11},{4,12},{5,13},{6,14},{7,15},{8,0},{9,1},... | collective-permute-start | bytes 344072 | tf_op jit(solution)/shard_map/ppermute | solution.py:359
  10.9 8.2 %collective-permute-start.3 = (bf16[32,1792]{1,0:T(8,128)(2,1)S(1)}, bf16[32,1792]{1,0:T(8,128)(2,1)S(1)}, u32[]{:S(2)}, u32[]{:S(2)}) collective-permute-start(bf16[32,1792]{1,0:T(8,128)(2,1)S(1)} %get-tuple-element.58), channel_id=1, source_target_pairs={{0,12},{1,13},{2,14},{3,15},{4,8},{5,9},{6,10},{7,11},{8,4},{9,5},... | collective-permute-start | bytes 344072 | tf_op jit(solution)/shard_map/ppermute | solution.py:359
  12.3 7.0 %collective-permute-start.4 = (bf16[32,1792]{1,0:T(8,128)(2,1)S(1)}, bf16[32,1792]{1,0:T(8,128)(2,1)S(1)}, u32[]{:S(2)}, u32[]{:S(2)}) collective-permute-start(bf16[32,1792]{1,0:T(8,128)(2,1)S(1)} %get-tuple-element.59), channel_id=1, source_target_pairs={{0,4},{1,5},{2,6},{3,7},{4,0},{5,1},{6,2},{7,3},{8,12},{9,13},{10,... | collective-permute-start | bytes 344072 | tf_op jit(solution)/shard_map/ppermute | solution.py:359
  12.5 8.9 %copy-start.2 = (bf16[1,128,512]{2,1,0:T(8,128)(2,1)S(1)}, bf16[1,128,512]{2,1,0:T(8,128)(2,1)}, u32[]{:S(2)}) copy-start(bf16[1,128,512]{2,1,0:T(8,128)(2,1)} %param.25) | copy-start | bytes 393220
  12.5 8.9 %copy-start.3 = (bf16[1,128,512]{2,1,0:T(8,128)(2,1)S(1)}, bf16[1,128,512]{2,1,0:T(8,128)(2,1)}, u32[]{:S(2)}) copy-start(bf16[1,128,512]{2,1,0:T(8,128)(2,1)} %param.26) | copy-start | bytes 393220
  12.5 8.9 %copy-start.5 = (bf16[1,56,512]{2,1,0:T(8,128)(2,1)S(1)}, bf16[1,56,512]{2,1,0:T(8,128)(2,1)}, u32[]{:S(2)}) copy-start(bf16[1,56,512]{2,1,0:T(8,128)(2,1)} %param.19) | copy-start | bytes 172036
  12.5 8.9 %copy-start.6 = (bf16[1,56,512]{2,1,0:T(8,128)(2,1)S(1)}, bf16[1,56,512]{2,1,0:T(8,128)(2,1)}, u32[]{:S(2)}) copy-start(bf16[1,56,512]{2,1,0:T(8,128)(2,1)} %param.21) | copy-start | bytes 172036
  12.6 8.9 %copy-start.7 = (bf16[1,4,7168]{2,1,0:T(4,128)(2,1)S(1)}, bf16[1,4,7168]{2,1,0:T(4,128)(2,1)}, u32[]{:S(2)}) copy-start(bf16[1,4,7168]{2,1,0:T(4,128)(2,1)} %param.23) | copy-start | bytes 172036
  19.6 1.9 %collective-permute-start.5 = (bf16[32,7168]{1,0:T(8,128)(2,1)S(1)}, bf16[32,7168]{1,0:T(8,128)(2,1)S(1)}, u32[]{:S(2)}, u32[]{:S(2)}) collective-permute-start(bf16[32,7168]{1,0:T(8,128)(2,1)S(1)} %unpack.1.refs_0_), channel_id=1, source_target_pairs={{0,1},{1,0},{2,3},{3,2},{4,5},{5,4},{6,7},{7,6},{8,9},{9,8},{10,11... | collective-permute-start | bytes 1376264 | tf_op jit(solution)/shard_map/ppermute | solution.py:359
  21.5 4.7 %copy-start.4 = (bf16[1,8,7168]{2,1,0:T(8,128)(2,1)S(1)}, bf16[1,8,7168]{2,1,0:T(8,128)(2,1)}, u32[]{:S(2)}) copy-start(bf16[1,8,7168]{2,1,0:T(8,128)(2,1)} %param.15) | copy-start | bytes 344068
  26.0 1.9 %collective-permute-start.8 = (bf16[32,7168]{1,0:T(8,128)(2,1)S(1)}, bf16[32,7168]{1,0:T(8,128)(2,1)S(1)}, u32[]{:S(2)}, u32[]{:S(2)}) collective-permute-start(bf16[32,7168]{1,0:T(8,128)(2,1)S(1)} %get-tuple-element.78), channel_id=1, source_target_pairs={{0,1},{1,0},{2,3},{3,2},{4,5},{5,4},{6,7},{7,6},{8,9},{9,8},{10,11... | collective-permute-start | bytes 1376264 | tf_op jit(solution)/shard_map/ppermute | solution.py:359
  26.2 6.4 %collective-permute-start.6 = (bf16[8,7168]{1,0:T(8,128)(2,1)S(1)}, bf16[8,7168]{1,0:T(8,128)(2,1)S(1)}, u32[]{:S(2)}, u32[]{:S(2)}) collective-permute-start(bf16[8,7168]{1,0:T(8,128)(2,1)S(1)} %bitcast.24), channel_id=1, source_target_pairs={{0,1},{1,0},{2,3},{3,2},{4,5},{5,4},{6,7},{7,6},{8,9},{9,8},{10,11... | collective-permute-start | bytes 344072 | tf_op jit(solution)/shard_map/ppermute | solution.py:359
  26.6 6.0 %collective-permute-start.7 = (bf16[8,7168]{1,0:T(8,128)(2,1)S(1)}, bf16[8,7168]{1,0:T(8,128)(2,1)S(1)}, u32[]{:S(2)}, u32[]{:S(2)}) collective-permute-start(bf16[8,7168]{1,0:T(8,128)(2,1)S(1)} %collective-permute-done.1.tokens.refs_1_), channel_id=1, source_target_pairs={{0,1},{1,0},{2,3},{3,2},{4,5},{5,4},{6,7},{7,6},{8,9},{9,8},{10,11... | collective-permute-start | bytes 344072 | tf_op jit(solution)/shard_map/ppermute | solution.py:359
  28.2 12.4 %collective-permute-start.10 = (bf16[32,1792]{1,0:T(8,128)(2,1)S(1)}, bf16[32,1792]{1,0:T(8,128)(2,1)S(1)}, u32[]{:S(2)}, u32[]{:S(2)}) collective-permute-start(bf16[32,1792]{1,0:T(8,128)(2,1)S(1)} %get-tuple-element.87), channel_id=1, source_target_pairs={{0,8},{1,9},{2,10},{3,11},{4,12},{5,13},{6,14},{7,15},{8,0},{9,1},... | collective-permute-start | bytes 344072 | tf_op jit(solution)/shard_map/ppermute | solution.py:359
  32.0 8.7 %collective-permute-start.11 = (bf16[32,1792]{1,0:T(8,128)(2,1)S(1)}, bf16[32,1792]{1,0:T(8,128)(2,1)S(1)}, u32[]{:S(2)}, u32[]{:S(2)}) collective-permute-start(bf16[32,1792]{1,0:T(8,128)(2,1)S(1)} %get-tuple-element.88), channel_id=1, source_target_pairs={{0,12},{1,13},{2,14},{3,15},{4,8},{5,9},{6,10},{7,11},{8,4},{9,5},... | collective-permute-start | bytes 344072 | tf_op jit(solution)/shard_map/ppermute | solution.py:359
  32.4 9.3 %collective-permute-start.12 = (bf16[32,1792]{1,0:T(8,128)(2,1)S(1)}, bf16[32,1792]{1,0:T(8,128)(2,1)S(1)}, u32[]{:S(2)}, u32[]{:S(2)}) collective-permute-start(bf16[32,1792]{1,0:T(8,128)(2,1)S(1)} %get-tuple-element.89), channel_id=1, source_target_pairs={{0,4},{1,5},{2,6},{3,7},{4,0},{5,1},{6,2},{7,3},{8,12},{9,13},{10,... | collective-permute-start | bytes 344072 | tf_op jit(solution)/shard_map/ppermute | solution.py:359
  32.6 14.9 %copy-start.1 = (s32[8,128]{1,0:T(8,128)S(1)}, s32[8,128]{1,0:T(8,128)}, u32[]{:S(2)}) copy-start(s32[8,128]{1,0:T(8,128)} %param.24) | copy-start | bytes 12292
  37.8 4.2 %collective-permute-start.9 = (bf16[8,7168]{1,0:T(8,128)(2,1)S(1)}, bf16[8,7168]{1,0:T(8,128)(2,1)S(1)}, u32[]{:S(2)}, u32[]{:S(2)}) collective-permute-start(bf16[8,7168]{1,0:T(8,128)(2,1)S(1)} %get-tuple-element.85), channel_id=1, source_target_pairs={{0,1},{1,0},{2,3},{3,2},{4,5},{5,4},{6,7},{7,6},{8,9},{9,8},{10,11... | collective-permute-start | bytes 344072 | tf_op jit(solution)/shard_map/ppermute | solution.py:359
  37.8 4.9 %collective-permute-start.13 = (bf16[8,7168]{1,0:T(8,128)(2,1)S(1)}, bf16[8,7168]{1,0:T(8,128)(2,1)S(1)}, u32[]{:S(2)}, u32[]{:S(2)}) collective-permute-start(bf16[8,7168]{1,0:T(8,128)(2,1)S(1)} %get-tuple-element.95), channel_id=1, source_target_pairs={{0,1},{1,0},{2,3},{3,2},{4,5},{5,4},{6,7},{7,6},{8,9},{9,8},{10,11... | collective-permute-start | bytes 344072 | tf_op jit(solution)/shard_map/ppermute | solution.py:359
  42.0 4.9 %collective-permute-start.14 = (bf16[8,7168]{1,0:T(8,128)(2,1)S(1)}, bf16[8,7168]{1,0:T(8,128)(2,1)S(1)}, u32[]{:S(2)}, u32[]{:S(2)}) collective-permute-start(bf16[8,7168]{1,0:T(8,128)(2,1)S(1)} %merge.2), channel_id=1, source_target_pairs={{0,2},{1,3},{2,0},{3,1},{4,6},{5,7},{6,4},{7,5},{8,10},{9,11},{10,... | collective-permute-start | bytes 344072 | tf_op jit(solution)/shard_map/ppermute | solution.py:359

commit v4 on v3

v4 whole, which is shorter than its diff:
```python
import functools

import jax
import jax.numpy as jnp
from jax import lax
from jax.experimental import pallas as pl
from jax.experimental.pallas import tpu as pltpu
from jax.sharding import PartitionSpec as P

FF = 1024
TOPK = 2
TILE = 16
LANES = 128
AHEAD = 2e11
BF16 = jnp.bfloat16
F32 = jnp.float32
VMEM = pl.BlockSpec(memory_space=pltpu.VMEM)
ANY = pl.BlockSpec(memory_space=pl.ANY)
SMEM = pl.BlockSpec(memory_space=pltpu.SMEM)


def params(mib):
    return pltpu.CompilerParams(vmem_limit_bytes=mib << 20)


def cost(flops, nbytes):
    return pl.CostEstimate(flops=int(flops), bytes_accessed=int(nbytes), transcendentals=0)


def matmul(left, right):
    return jnp.dot(left, right, preferred_element_type=F32)


def in_hbm(array):
    return pltpu.with_memory_space_constraint(array, pltpu.HBM)


def iota(shape, dim):
    return lax.broadcasted_iota(jnp.int32, shape, dim)


def by_row(values, position, choice):
    out = jnp.zeros(position.shape, values[0].dtype)
    for r in range(len(values) // TOPK):
        out = jnp.where(position == r, values[r * TOPK + choice], out)
    return out


def slot_marks(ids_ref, weights_ref, rows, cap):
    pairs = [(r, t) for r in range(rows) for t in range(TOPK)]
    ids = [ids_ref[t, r] for r, t in pairs]
    weights = [weights_ref[t, r] for r, t in pairs]
    codes = []
    for n, e in enumerate(ids):
        place = jnp.int32(0)
        for earlier in ids[:n]:
            place += (earlier == e).astype(jnp.int32)
        codes.append(e * cap + place)
    shape = (rows, LANES)
    position, lane = iota(shape, 0), iota(shape, 1)
    quarter = LANES // 4
    marks = jnp.zeros(shape, F32)
    for t in range(TOPK):
        rest = by_row(weights, position, t)
        value = jnp.ones(shape, F32)
        for k in range(1, 4):
            term = rest.astype(BF16).astype(F32)
            value = jnp.where(lane // quarter == k, term, value)
            rest = rest - term
        marks += jnp.where(lane % quarter == by_row(codes, position, t), value, 0.0)
    return marks


def block_lanes(shape, dim, cap, masks, home):
    j = iota(shape, dim)
    lane = j % cap
    for n, mask in enumerate(masks):
        lane += jnp.where(j // TILE == n, (home ^ mask) * cap, 0)
    return lane, j % TILE // cap


def tiled(marks, cap):
    return jnp.concatenate([marks.astype(F32)] * (TILE // cap), axis=0).astype(BF16)


def lanes_dot(left, right):
    return lax.dot_general(left, right, (((1,), (1,)), ((), ())), preferred_element_type=F32)


def write_blocks(cap, masks, home, marks, tokens, stacked, blocks):
    rows = marks.shape[0]
    parts = TILE // cap
    width = blocks[0].shape[1]
    height = len(blocks) * TILE
    lane, _ = block_lanes((height, LANES), 0, cap, masks, home)
    wanted = jnp.where(lane == iota((height, LANES), 1), 1.0, 0.0).astype(BF16)
    hit = lanes_dot(wanted, tiled(marks, cap))
    part = iota(hit.shape, 0) % TILE // cap
    hit = jnp.where(part == iota(hit.shape, 1) // rows, hit, 0.0)
    for q in range(parts):
        stacked[q * rows : (q + 1) * rows, :] = tokens[:, q * width : (q + 1) * width].astype(F32)
    chosen = matmul(hit.astype(BF16), stacked[...].astype(BF16)).astype(BF16)
    for m, block in enumerate(blocks):
        block[...] = chosen[m * TILE : (m + 1) * TILE]


def first_kernel(cap, masks, home_ref, ids_hbm, weights_hbm, own_hbm, marks_ref, *refs):
    blocks, (ids_ref, weights_ref, own, stacked, sems) = refs[:-5], refs[-5:]
    small = [
        pltpu.make_async_copy(ids_hbm, ids_ref, sems.at[1]),
        pltpu.make_async_copy(weights_hbm, weights_ref, sems.at[2]),
    ]
    copy = pltpu.make_async_copy(own_hbm, own, sems.at[0])
    for each in small:
        each.start()
    copy.start()
    for each in small:
        each.wait()
    rows = own.shape[0]
    marks = slot_marks(ids_ref, weights_ref, rows, cap)
    marks_ref[...] = marks.astype(BF16)
    copy.wait()
    write_blocks(cap, masks, home_ref[0], marks, own, stacked, blocks)


def unpack_kernel(cap, *refs):
    blocks, out = refs[:-1], refs[-1]
    parts, slots, width = TILE // cap, out.shape[0], blocks[0].shape[1]
    shape = (parts * slots, slots // cap * TILE)
    i, j = iota(shape, 0), iota(shape, 1)
    source = i % slots // cap * TILE + i // slots * cap + i % cap
    arranged = matmul(
        jnp.where(source == j, 1.0, 0.0).astype(BF16),
        jnp.concatenate([b[...] for b in blocks], axis=0),
    ).astype(BF16)
    for q in range(parts):
        out[:, q * width : (q + 1) * width] = arranged[q * slots : (q + 1) * slots]


def pack_kernel(cap, mine_ref, other_ref, *blocks):
    parts, slots = TILE // cap, mine_ref.shape[0]
    width = mine_ref.shape[1] // parts
    total = (mine_ref[...].astype(F32) + other_ref[...].astype(F32)).astype(BF16)
    shape = (slots // cap * TILE, parts * slots)
    j, i = iota(shape, 0), iota(shape, 1)
    source = j % TILE // cap * slots + j // TILE * cap + j % cap
    arranged = matmul(
        jnp.where(source == i, 1.0, 0.0).astype(BF16),
        jnp.concatenate([total[:, q * width : (q + 1) * width] for q in range(parts)], axis=0),
    ).astype(BF16)
    start = 0
    for block in blocks:
        block[...] = arranged[start : start + block.shape[0]]
        start += block.shape[0]


def outlier_kernel(step, cols, *refs):
    onehot, keep = refs[-2:]
    chunks = onehot.shape[0] // step
    outliers = cols.shape[1]
    for c in range(chunks):
        here = slice(c * step, (c + 1) * step)
        hot = jnp.where(iota((step, outliers), 0) + c * step == cols[...], 1.0, 0.0).astype(BF16)
        onehot[here, :] = hot
        count = lanes_dot(jnp.ones((8, outliers), BF16), hot)
        keep[:, here] = jnp.where(count == 0.0, 1.0, 0.0)


def scaled(codes, scales, block):
    return jnp.concatenate(
        [
            codes[b * block : (b + 1) * block] * jnp.broadcast_to(scales[b : b + 1], (block, codes.shape[1]))
            for b in range(codes.shape[0] // block)
        ],
        axis=0,
    )


def expert_kernel(
    step, wide, count, gate, up, wd, onehot, keep, sg, su, sd, extra_gate, extra_up, *refs
):
    pieces, outs = refs[:count], refs[count : 2 * count]
    down, gate_acc, up_acc, picked, hidden_ref, gate_scale, up_scale, down_scale, sem = refs[2 * count :]
    height = pieces[0].shape[0]
    width, hid = gate.shape
    chunks = width // step
    load = pltpu.make_async_copy(wd, down, sem)
    load.start()
    gate_acc[...] = jnp.zeros_like(gate_acc)
    up_acc[...] = jnp.zeros_like(up_acc)
    picked[...] = jnp.zeros_like(picked)
    gate_scale[...] = sg[...].astype(F32)
    up_scale[...] = su[...].astype(F32)
    down_scale[...] = sd[...].astype(F32)
    block = width // sg.shape[0]
    for c in range(chunks):
        here = slice(c * step, (c + 1) * step)
        there = slice(c * step // block, (c + 1) * step // block)
        whole = jnp.concatenate([piece[:, here] for piece in pieces], axis=0)
        masked = whole * jnp.broadcast_to(keep[0:1, here].astype(BF16), whole.shape)
        picked[...] += matmul(whole, onehot[here, :])
        gate_acc[...] += matmul(masked, scaled(gate[here, :], gate_scale[there, :].astype(BF16), block))
        up_acc[...] += matmul(masked, scaled(up[here, :], up_scale[there, :].astype(BF16), block))

    outliers = picked[...].astype(BF16)
    gate_val = gate_acc[...] + matmul(outliers, extra_gate[...])
    up_val = up_acc[...] + matmul(outliers, extra_up[...])
    hidden_ref[...] = (gate_val / (1.0 + jnp.exp(-gate_val)) * up_val).astype(BF16)
    load.wait()
    tall = hid // sd.shape[0]
    for c in range(width // wide):
        here = slice(c * wide, (c + 1) * wide)
        weights = jnp.concatenate(
            [
                down[b * tall : (b + 1) * tall, here]
                * jnp.broadcast_to(down_scale[b : b + 1, here].astype(BF16), (tall, wide))
                for b in range(hid // tall)
            ],
            axis=0,
        )
        result = matmul(hidden_ref[...], weights).astype(BF16)
        for n, out in enumerate(outs):
            out[:, here] = result[n * height : (n + 1) * height]


def shared_up_kernel(step, gate, up, *refs):
    pieces, (hidden, rows_ref, gate_acc, up_acc) = refs[:-4], refs[-4:]
    rows_ref[...] = jnp.concatenate([p[...].astype(F32) for p in pieces], axis=0).astype(BF16)
    gate_acc[...] = jnp.zeros_like(gate_acc)
    up_acc[...] = jnp.zeros_like(up_acc)
    for c in range(gate.shape[0] // step):
        here = slice(c * step, (c + 1) * step)
        gate_acc[...] += matmul(rows_ref[:, here], gate[here, :])
        up_acc[...] += matmul(rows_ref[:, here], up[here, :])
    value = gate_acc[...]
    hidden[...] = (value / (1.0 + jnp.exp(-value)) * up_acc[...]).astype(BF16)


def shared_down_kernel(wide, hidden, down, *outs):
    height = outs[0].shape[0]
    for c in range(down.shape[1] // wide):
        here = slice(c * wide, (c + 1) * wide)
        result = matmul(hidden[...], down[:, here])
        for n, out in enumerate(outs):
            out[:, here] = result[n * height : (n + 1) * height].astype(out.dtype)


def share_kernel(cap, masks, home_ref, *refs):
    for marks, out in zip(refs[: len(refs) // 2], refs[len(refs) // 2 :]):
        rows = marks.shape[0]
        size, height = TILE // cap * rows, out.shape[1]
        repeated = tiled(marks[...], cap)
        lane, _ = block_lanes((height, LANES), 0, cap, masks, home_ref[0])
        part = iota((size, height), 1) % TILE // cap
        same = part == iota((size, height), 0) // rows
        for k in range(3):
            wanted = lane + (k + 1) * (LANES // 4) == iota((height, LANES), 1)
            term = lanes_dot(repeated, jnp.where(wanted, 1.0, 0.0).astype(BF16))
            out[k * size : (k + 1) * size, :] = jnp.where(same, term, 0.0).astype(BF16)


def combine_kernel(cap, count, share_ref, *refs):
    blocks, sums, out = refs[:count], refs[count:-1], refs[-1]
    rows = out.shape[0]
    parts = TILE // cap
    width = out.shape[1] // parts
    arrived = jnp.concatenate([b[...] for b in blocks], axis=0)
    terms = matmul(share_ref[...], arrived)
    size = parts * rows
    routed = terms[:size] + terms[size : 2 * size] + terms[2 * size :]
    for q in range(parts):
        here = slice(q * width, (q + 1) * width)
        total = routed[q * rows : (q + 1) * rows]
        for part in sums:
            total += part[:, here].astype(F32)
        out[:, here] = total.astype(out.dtype)


def on_device(
    tokens,
    expert_ids,
    gate_weights,
    w_gate,
    scale_gate,
    w_up,
    scale_up,
    w_down,
    scale_down,
    outlier_cols,
    outlier_gate,
    outlier_up,
    shared_gate,
    shared_up,
    shared_down,
):
    devices = lax.axis_size("ep")
    device = lax.axis_index("ep")
    hid = w_gate.shape[2]
    group = FF // hid
    experts = devices // group
    bits = group.bit_length() - 1
    rows, width = tokens.shape[1], tokens.shape[2]
    cap = max(2, rows * TOPK * 2 // experts)
    home = device // group
    part_width = width * cap // TILE
    slots = experts * cap

    def swap(array, mask):
        return lax.ppermute(array, "ep", [(d, d ^ mask) for d in range(devices)])

    def spread(pieces):
        for bit in range(bits):
            pieces = pieces + [swap(piece, 1 << bit) for piece in pieces]
        return pieces

    current = tokens[0]
    ids, weights = expert_ids[0].T, gate_weights[0].T
    home_ref = home.astype(jnp.int32).reshape(1)
    masks = list(range(experts))

    parts = TILE // cap
    sent_block = jax.ShapeDtypeStruct((TILE, part_width), BF16)
    stack = pltpu.VMEM((parts * rows, part_width), F32)
    marks, *blocks = pl.pallas_call(
        functools.partial(first_kernel, cap, masks),
        in_specs=[SMEM] + [ANY] * 3,
        out_specs=[VMEM] * (1 + experts),
        out_shape=[jax.ShapeDtypeStruct((rows, LANES), BF16)] + [sent_block] * experts,
        scratch_shapes=[
            pltpu.SMEM(ids.shape, jnp.int32),
            pltpu.SMEM(weights.shape, F32),
            pltpu.VMEM((rows, width), BF16),
            stack,
            pltpu.SemaphoreType.DMA((3,)),
        ],
        compiler_params=params(8),
        cost_estimate=cost(AHEAD, 1e6),
        name="first",
    )(home_ref, in_hbm(ids), in_hbm(weights), in_hbm(current))
    def exchanged(blocks):
        return [swap(block, mask * group) if mask else block for mask, block in zip(masks, blocks)]

    arrived = exchanged(blocks)

    step = 1024
    cols, rows_here, _ = lax.optimization_barrier(
        (lax.dynamic_slice_in_dim(outlier_cols, home, 1, 0), current, blocks[0])
    )
    early = [w_gate[0], w_up[0], shared_gate[0], shared_up[0]]
    onehot, keep = pl.pallas_call(
        functools.partial(outlier_kernel, step),
        in_specs=[VMEM] * (1 + len(early)),
        out_specs=[VMEM] * 2,
        out_shape=[
            jax.ShapeDtypeStruct((width, outlier_cols.shape[1]), BF16),
            jax.ShapeDtypeStruct((8, width), F32),
        ],
        compiler_params=params(8),
        cost_estimate=cost(1e8, 1e6),
        name="outlier",
    )(cols, *early)
    row_pieces = spread([rows_here])
    hidden = pl.pallas_call(
        functools.partial(shared_up_kernel, step),
        in_specs=[VMEM] * (2 + group),
        out_specs=VMEM,
        out_shape=jax.ShapeDtypeStruct((group * rows, hid), BF16),
        scratch_shapes=[
            pltpu.VMEM((group * rows, width), BF16),
            pltpu.VMEM((group * rows, hid), F32),
            pltpu.VMEM((group * rows, hid), F32),
        ],
        compiler_params=params(8),
        cost_estimate=cost(4 * group * rows * width * hid, 4 * hid * width),
        name="shared_up",
    )(shared_gate[0], shared_up[0], *row_pieces)
    arrived, keep, hidden = lax.optimization_barrier((arrived, keep, hidden))

    whole = jax.ShapeDtypeStruct((slots, width), BF16)
    taken = pl.pallas_call(
        functools.partial(unpack_kernel, cap),
        in_specs=[VMEM] * len(arrived),
        out_specs=VMEM,
        out_shape=whole,
        compiler_params=params(10),
        cost_estimate=cost(1e8, 1e6),
        name="unpack",
    )(*arrived)
    pieces = spread([taken])

    hidden, marks, _ = lax.optimization_barrier((hidden, marks, taken))
    shared = pl.pallas_call(
        functools.partial(shared_down_kernel, 1024),
        in_specs=[VMEM] * 2,
        out_specs=[VMEM] * group,
        out_shape=[jax.ShapeDtypeStruct((rows, width), F32)]
        + [jax.ShapeDtypeStruct((rows, width), BF16)] * (group - 1),
        compiler_params=params(8),
        cost_estimate=cost(2 * group * rows * width * hid, 2 * hid * width),
        name="shared_down",
    )(hidden, shared_down[0])
    shares = pl.pallas_call(
        functools.partial(share_kernel, cap, masks),
        in_specs=[SMEM, VMEM],
        out_specs=[VMEM],
        out_shape=[jax.ShapeDtypeStruct((3 * parts * rows, experts * TILE), BF16)],
        compiler_params=params(4),
        cost_estimate=cost(1e6, 1e5),
        name="share",
    )(home_ref, marks)
    pieces, shares, shared = lax.optimization_barrier((pieces, shares, shared))

    partials = pl.pallas_call(
        functools.partial(expert_kernel, step, 1024, group),
        in_specs=[VMEM, VMEM, ANY] + [VMEM] * (7 + group),
        out_specs=[VMEM] * group,
        out_shape=[whole] * group,
        scratch_shapes=[
            pltpu.VMEM((hid, width), BF16),
            pltpu.VMEM((group * slots, hid), F32),
            pltpu.VMEM((group * slots, hid), F32),
            pltpu.VMEM((group * slots, outlier_cols.shape[1]), F32),
            pltpu.VMEM((group * slots, hid), BF16),
            pltpu.VMEM(scale_gate.shape[1:], F32),
            pltpu.VMEM(scale_up.shape[1:], F32),
            pltpu.VMEM(scale_down.shape[1:], F32),
            pltpu.SemaphoreType.DMA,
        ],
        compiler_params=params(10),
        cost_estimate=cost(6 * group * slots * width * hid, 6 * hid * width),
        name="expert",
    )(
        w_gate[0],
        w_up[0],
        in_hbm(w_down[0]),
        onehot,
        keep,
        scale_gate[0],
        scale_up[0],
        scale_down[0],
        outlier_gate[0],
        outlier_up[0],
        *pieces,
    )

    for bit in reversed(range(1, bits)):
        half = 1 << bit
        partials = [
            (mine.astype(F32) + swap(other, half).astype(F32)).astype(BF16)
            for mine, other in zip(partials[:half], partials[half:])
        ]
    returning = pl.pallas_call(
        functools.partial(pack_kernel, cap),
        in_specs=[VMEM] * 2,
        out_specs=[VMEM] * experts,
        out_shape=[sent_block] * experts,
        compiler_params=params(10),
        cost_estimate=cost(1e8, 1e6),
        name="pack",
    )(partials[0], swap(partials[1], 1))
    returned = exchanged(returning)
    sums = [shared[0]] + [swap(shared[n], n) for n in range(1, group)]
    out = pl.pallas_call(
        functools.partial(combine_kernel, cap, experts),
        in_specs=[VMEM] * (1 + experts + group),
        out_specs=VMEM,
        out_shape=jax.ShapeDtypeStruct((rows, width), BF16),
        compiler_params=params(10),
        cost_estimate=cost(1e8, 1e6),
        name="combine",
    )(*shares, *returned, *sums)
    return out[None]


def solution(mesh):
    rows = P(None, ("parts", "ep"), None)
    held = P("ep", None, None)
    placed = (rows, rows, rows) + (held,) * 6 + (P(),) + (held,) * 5
    return jax.shard_map(
        on_device, mesh=mesh, in_specs=placed, out_specs=rows, check_vma=False
    )
```

time: 47.6 us -> 46.8 us (0.983)
  starting transfers between devices: 13.6 us -> 25 us
  Pallas kernels: 18.8 us -> 11.5 us
  waiting for transfers between devices: 14.9 us -> 9.15 us
  local copies, waits for them, and re-layouts: 0.05 us -> 0.75 us
    ppermute x15 -> x18, starting transfers between devices: 13.6 us -> 25 us  [swap(): return lax.ppermute(array, 'ep', [(d, d ^ mask) for d in range(devices)])]
    pallas_call x9 -> x5, Pallas kernels: 12.4 us -> 4.94 us  [the longest x1 2.01 us: on_device(): pl.pallas_call(functools.partial(shared_up_kernel, step), in_specs=[VMEM]...]
    ppermute x15 -> x18, waiting for transfers between devices: 14.9 us -> 9.15 us  [swap(): return lax.ppermute(array, 'ep', [(d, d ^ mask) for d in range(devices)])]
    unnamed x16 -> x24, local copies, waits for them, and re-layouts: 0.04 us -> 0.74 us
  transfers between devices with their start and end apart: 15 -> 18, of which waited for: 8 -> 7; matrix products, arithmetic and copies ran while one was open for 0% -> 0% of each run, Pallas kernels for 27% -> 9%
where the time goes in v4:
time: 46.8 us; the launch traced here: 46.6 us
  starting transfers between devices  25 us (53%)
  Pallas kernels  11.5 us (25%)
  waiting for transfers between devices  9.15 us (20%)
  local copies, waits for them, and re-layouts  0.75 us (2%)
    ppermute x18, starting transfers between devices, swap(): return lax.ppermute(array, 'ep', [(d, d ^ mask) for d in range(devices)])  25 us
    ppermute x18, waiting for transfers between devices, swap(): return lax.ppermute(array, 'ep', [(d, d ^ mask) for d in range(devices)])  9.15 us
    pallas_call x1, Pallas kernels, on_device(): pl.pallas_call(functools.partial(expert_kernel, step, 1024, group), in_sp...  4.49 us
    pallas_call x1, Pallas kernels, on_device(): pl.pallas_call(functools.partial(shared_up_kernel, step), in_specs=[VMEM]...  2.01 us
    pallas_call x1, Pallas kernels, on_device(): pl.pallas_call(functools.partial(first_kernel, cap, masks), in_specs=[SME...  1.48 us
    pallas_call x1, Pallas kernels, on_device(): pl.pallas_call(functools.partial(shared_down_kernel, 1024), in_specs=[VME...  1.08 us
  transfers between devices with their start and end apart: 18, of which 7 were waited for; matrix products, arithmetic and copies ran while one was open for 0% of the time, Pallas kernels for 9%

profile of v4, /device:TPU:0, one launch (start us, length us, event | category | flops | bytes accessed | tf_op | source)
XLA Modules:
  0.0 46.6 jit_solution(11196551499170752348)
XLA Ops:
  0.0 0.7 %copy-done = s32[8,128]{1,0:T(8,128)S(1)} copy-done((s32[8,128]{1,0:T(8,128)S(1)}, s32[8,128]{1,0:T(8,128)}, u32[]{:S(2)}) %copy-start) | copy-done | bytes 4120
  0.7 1.5 %first.1 = (bf16[8,128]{1,0:T(8,128)(2,1)S(1)}, bf16[16,1792]{1,0:T(8,128)(2,1)S(1)}, bf16[16,1792]{1,0:T(8,128)(2,1)S(1)}, bf16[16,1792]{1,0:T(8,128)(2,1)S(1)}...) custom-call(s32[1]{0:T(128)} %bitcast.home_ref, ...), custom_call_target="tpu_custom_call" | custom-call | flops 199999995904 | bytes 1000000 | tf_op jit(solution)/shard_map/first/pallas_call | solution.py:324
  2.2 0.5 %collective-permute-start.7 = (bf16[8,7168]{1,0:T(8,128)(2,1)S(1)}, bf16[8,7168]{1,0:T(8,128)(2,1)S(1)}, u32[]{:S(2)}, u32[]{:S(2)}) collective-permute-start(bf16[8,7168]{1,0:T(8,128)(2,1)S(1)} %bitcast.32), channel_id=1, source_target_pairs={{0,1},{1,0},{2,3},{3,2},{4,5},{5,4},{6,7},{7,6},{8,9},{9,8},{10,11... | collective-permute-start | bytes 344072 | tf_op jit(solution)/shard_map/ppermute | solution.py:309
  2.8 2.6 %collective-permute-start = (bf16[16,1792]{1,0:T(8,128)(2,1)S(1)}, bf16[16,1792]{1,0:T(8,128)(2,1)S(1)}, u32[]{:S(2)}, u32[]{:S(2)}) collective-permute-start(bf16[16,1792]{1,0:T(8,128)(2,1)S(1)} %get-tuple-element.48), channel_id=1, source_target_pairs={{0,2},{1,3},{2,0},{3,1},{4,6},{5,7},{6,4},{7,5},{8,10},{9,11},{10,... | collective-permute-start | bytes 172040 | tf_op jit(solution)/shard_map/ppermute | solution.py:309
  5.4 1.6 %collective-permute-start.1 = (bf16[16,1792]{1,0:T(8,128)(2,1)S(1)}, bf16[16,1792]{1,0:T(8,128)(2,1)S(1)}, u32[]{:S(2)}, u32[]{:S(2)}) collective-permute-start(bf16[16,1792]{1,0:T(8,128)(2,1)S(1)} %get-tuple-element.49), channel_id=1, source_target_pairs={{0,4},{1,5},{2,6},{3,7},{4,0},{5,1},{6,2},{7,3},{8,12},{9,13},{10,... | collective-permute-start | bytes 172040 | tf_op jit(solution)/shard_map/ppermute | solution.py:309
  6.9 3.0 %collective-permute-start.3 = (bf16[16,1792]{1,0:T(8,128)(2,1)S(1)}, bf16[16,1792]{1,0:T(8,128)(2,1)S(1)}, u32[]{:S(2)}, u32[]{:S(2)}) collective-permute-start(bf16[16,1792]{1,0:T(8,128)(2,1)S(1)} %get-tuple-element.51), channel_id=1, source_target_pairs={{0,8},{1,9},{2,10},{3,11},{4,12},{5,13},{6,14},{7,15},{8,0},{9,1},... | collective-permute-start | bytes 172040 | tf_op jit(solution)/shard_map/ppermute | solution.py:309
  9.9 1.7 %collective-permute-start.4 = (bf16[16,1792]{1,0:T(8,128)(2,1)S(1)}, bf16[16,1792]{1,0:T(8,128)(2,1)S(1)}, u32[]{:S(2)}, u32[]{:S(2)}) collective-permute-start(bf16[16,1792]{1,0:T(8,128)(2,1)S(1)} %get-tuple-element.52), channel_id=1, source_target_pairs={{0,10},{1,11},{2,8},{3,9},{4,14},{5,15},{6,12},{7,13},{8,2},{9,3},... | collective-permute-start | bytes 172040 | tf_op jit(solution)/shard_map/ppermute | solution.py:309
  11.7 3.2 %collective-permute-start.5 = (bf16[16,1792]{1,0:T(8,128)(2,1)S(1)}, bf16[16,1792]{1,0:T(8,128)(2,1)S(1)}, u32[]{:S(2)}, u32[]{:S(2)}) collective-permute-start(bf16[16,1792]{1,0:T(8,128)(2,1)S(1)} %get-tuple-element.53), channel_id=1, source_target_pairs={{0,12},{1,13},{2,14},{3,15},{4,8},{5,9},{6,10},{7,11},{8,4},{9,5},... | collective-permute-start | bytes 172040 | tf_op jit(solution)/shard_map/ppermute | solution.py:309
  14.8 0.6 %collective-permute-start.6 = (bf16[16,1792]{1,0:T(8,128)(2,1)S(1)}, bf16[16,1792]{1,0:T(8,128)(2,1)S(1)}, u32[]{:S(2)}, u32[]{:S(2)}) collective-permute-start(bf16[16,1792]{1,0:T(8,128)(2,1)S(1)} %get-tuple-element.54), channel_id=1, source_target_pairs={{0,14},{1,15},{2,12},{3,13},{4,10},{5,11},{6,8},{7,9},{8,6},{9,7},... | collective-permute-start | bytes 172040 | tf_op jit(solution)/shard_map/ppermute | solution.py:309
  15.4 0.8 %outlier.1 = (bf16[7168,128]{1,0:T(8,128)(2,1)S(1)}, f32[8,7168]{1,0:T(8,128)S(1)}) custom-call(s32[1,128]{1,0:T(1,128)S(1)} %constant_dynamic-slice_fusion.cols, bf16[7168,512]{1,0:T(8,128)(2,1)S(1)} %bitcast.24, bf16[7168,512]{1,0:T(8,128)(2,1)S(1)} %bitcast.26, bf16[7168,512]{1,0:T(8,128)(2,1)S(1)} %bitcast.20, bf16[7168,512]{1,0:T(8,128)(2,1)S(1)} %bitcast.22), custom_call_target="tpu_custom_call" | custom-call | flops 100000000 | bytes 1000000 | tf_op jit(solution)/shard_map/outlier/pallas_call | solution.py:350
  16.2 2.0 %shared_up.1.hidden = bf16[16,512]{1,0:T(8,128)(2,1)S(1)} custom-call(bf16[7168,512]{1,0:T(8,128)(2,1)S(1)} %bitcast.21, bf16[7168,512]{1,0:T(8,128)(2,1)S(1)} %bitcast.23, bf16[8,7168]{1,0:T(8,128)(2,1)S(1)} %bitcast.33, bf16[8,7168]{1,0:T(8,128)(2,1)S(1)} %collective-permute-done.7.refs_1_), custom_call_target="tpu_custom_call" | custom-call | flops 234881024 | bytes 14680064 | tf_op jit(solution)/shard_map/shared_up/pallas_call | solution.py:363
  18.3 0.3 collective-permute-done.4.refs_5_
  18.6 3.2 %collective-permute-done.6.refs_7_ = bf16[16,1792]{1,0:T(8,128)(2,1)S(1)} collective-permute-done((bf16[16,1792]{1,0:T(8,128)(2,1)S(1)}, bf16[16,1792]{1,0:T(8,128)(2,1)S(1)}, u32[]{:S(2)}, u32[]{:S(2)}) %collective-permute-start.6) | collective-permute-done | bytes 57376 | tf_op jit(solution)/shard_map/ppermute | solution.py:309
  21.8 0.3 unpack.1.refs_0_
  22.3 1.1 %shared_down.1 = (f32[8,7168]{1,0:T(8,128)S(1)}, bf16[8,7168]{1,0:T(8,128)(2,1)S(1)}) custom-call(bf16[16,512]{1,0:T(8,128)(2,1)S(1)} %shared_up.1.hidden, bf16[512,7168]{1,0:T(8,128)(2,1)S(1)} %bitcast.28), custom_call_target="tpu_custom_call" | custom-call | flops 117440512 | bytes 7340032 | tf_op jit(solution)/shard_map/shared_down/pallas_call | solution.py:392
  23.4 0.5 %collective-permute-done.8.refs_1_ = bf16[32,7168]{1,0:T(8,128)(2,1)S(1)} collective-permute-done((bf16[32,7168]{1,0:T(8,128)(2,1)S(1)}, bf16[32,7168]{1,0:T(8,128)(2,1)S(1)}, u32[]{:S(2)}, u32[]{:S(2)}) %collective-permute-start.8) | collective-permute-done | bytes 458784 | tf_op jit(solution)/shard_map/ppermute | solution.py:309
  24.0 4.5 %expert.1 = (bf16[32,7168]{1,0:T(8,128)(2,1)S(1)}, bf16[32,7168]{1,0:T(8,128)(2,1)S(1)}) custom-call(bf16[7168,512]{1,0:T(8,128)(2,1)S(1)} %bitcast.25, bf16[7168,512]{1,0:T(8,128)(2,1)S(1)} %bitcast.27, bf16[512,7168]{1,0:T(8,128)(2,1)} %bitcast.37, bf16[7168,128]{1,0:T(8,128)(2,1)S(1)} %get-tuple-element.73.onehot, f32[8,7168]{1,0:T(8,128)S(1)} %get-tuple-element.74.keep, ...), custom_call_target="tpu_custom_call" | custom-call | flops 1409286144 | bytes 22020096 | tf_op jit(solution)/shard_map/expert/pallas_call | solution.py:413
  28.5 0.2 collective-permute-start.9
  28.7 0.4 collective-permute-start.17
  29.1 1.3 %collective-permute-done.9.other_ref = bf16[32,7168]{1,0:T(8,128)(2,1)S(1)} collective-permute-done((bf16[32,7168]{1,0:T(8,128)(2,1)S(1)}, bf16[32,7168]{1,0:T(8,128)(2,1)S(1)}, u32[]{:S(2)}, u32[]{:S(2)}) %collective-permute-start.9) | collective-permute-done | bytes 458784 | tf_op jit(solution)/shard_map/ppermute | solution.py:309
  30.4 0.3 pack.1
  30.7 0.6 %collective-permute-start.10 = (bf16[16,1792]{1,0:T(8,128)(2,1)S(1)}, bf16[16,1792]{1,0:T(8,128)(2,1)S(1)}, u32[]{:S(2)}, u32[]{:S(2)}) collective-permute-start(bf16[16,1792]{1,0:T(8,128)(2,1)S(1)} %get-tuple-element.80), channel_id=1, source_target_pairs={{0,2},{1,3},{2,0},{3,1},{4,6},{5,7},{6,4},{7,5},{8,10},{9,11},{10,... | collective-permute-start | bytes 172040 | tf_op jit(solution)/shard_map/ppermute | solution.py:309
  31.3 1.1 %collective-permute-start.11 = (bf16[16,1792]{1,0:T(8,128)(2,1)S(1)}, bf16[16,1792]{1,0:T(8,128)(2,1)S(1)}, u32[]{:S(2)}, u32[]{:S(2)}) collective-permute-start(bf16[16,1792]{1,0:T(8,128)(2,1)S(1)} %get-tuple-element.81), channel_id=1, source_target_pairs={{0,4},{1,5},{2,6},{3,7},{4,0},{5,1},{6,2},{7,3},{8,12},{9,13},{10,... | collective-permute-start | bytes 172040 | tf_op jit(solution)/shard_map/ppermute | solution.py:309
  32.4 1.9 %collective-permute-start.12 = (bf16[16,1792]{1,0:T(8,128)(2,1)S(1)}, bf16[16,1792]{1,0:T(8,128)(2,1)S(1)}, u32[]{:S(2)}, u32[]{:S(2)}) collective-permute-start(bf16[16,1792]{1,0:T(8,128)(2,1)S(1)} %get-tuple-element.82), channel_id=1, source_target_pairs={{0,6},{1,7},{2,4},{3,5},{4,2},{5,3},{6,0},{7,1},{8,14},{9,15},{10,... | collective-permute-start | bytes 172040 | tf_op jit(solution)/shard_map/ppermute | solution.py:309
  34.2 2.0 %collective-permute-start.13 = (bf16[16,1792]{1,0:T(8,128)(2,1)S(1)}, bf16[16,1792]{1,0:T(8,128)(2,1)S(1)}, u32[]{:S(2)}, u32[]{:S(2)}) collective-permute-start(bf16[16,1792]{1,0:T(8,128)(2,1)S(1)} %get-tuple-element.83), channel_id=1, source_target_pairs={{0,8},{1,9},{2,10},{3,11},{4,12},{5,13},{6,14},{7,15},{8,0},{9,1},... | collective-permute-start | bytes 172040 | tf_op jit(solution)/shard_map/ppermute | solution.py:309
  36.2 0.9 %collective-permute-start.14 = (bf16[16,1792]{1,0:T(8,128)(2,1)S(1)}, bf16[16,1792]{1,0:T(8,128)(2,1)S(1)}, u32[]{:S(2)}, u32[]{:S(2)}) collective-permute-start(bf16[16,1792]{1,0:T(8,128)(2,1)S(1)} %get-tuple-element.84), channel_id=1, source_target_pairs={{0,10},{1,11},{2,8},{3,9},{4,14},{5,15},{6,12},{7,13},{8,2},{9,3},... | collective-permute-start | bytes 172040 | tf_op jit(solution)/shard_map/ppermute | solution.py:309
  37.1 1.6 %collective-permute-start.15 = (bf16[16,1792]{1,0:T(8,128)(2,1)S(1)}, bf16[16,1792]{1,0:T(8,128)(2,1)S(1)}, u32[]{:S(2)}, u32[]{:S(2)}) collective-permute-start(bf16[16,1792]{1,0:T(8,128)(2,1)S(1)} %get-tuple-element.85), channel_id=1, source_target_pairs={{0,12},{1,13},{2,14},{3,15},{4,8},{5,9},{6,10},{7,11},{8,4},{9,5},... | collective-permute-start | bytes 172040 | tf_op jit(solution)/shard_map/ppermute | solution.py:309
  38.7 3.2 %collective-permute-start.16 = (bf16[16,1792]{1,0:T(8,128)(2,1)S(1)}, bf16[16,1792]{1,0:T(8,128)(2,1)S(1)}, u32[]{:S(2)}, u32[]{:S(2)}) collective-permute-start(bf16[16,1792]{1,0:T(8,128)(2,1)S(1)} %get-tuple-element.86), channel_id=1, source_target_pairs={{0,14},{1,15},{2,12},{3,13},{4,10},{5,11},{6,8},{7,9},{8,6},{9,7},... | collective-permute-start | bytes 172040 | tf_op jit(solution)/shard_map/ppermute | solution.py:309
  41.9 0.3 collective-permute-done.13.refs_4_
  42.2 2.7 %collective-permute-done.14.refs_5_ = bf16[16,1792]{1,0:T(8,128)(2,1)S(1)} collective-permute-done((bf16[16,1792]{1,0:T(8,128)(2,1)S(1)}, bf16[16,1792]{1,0:T(8,128)(2,1)S(1)}, u32[]{:S(2)}, u32[]{:S(2)}) %collective-permute-start.14) | collective-permute-done | bytes 57376 | tf_op jit(solution)/shard_map/ppermute | solution.py:309
  44.9 0.8 %collective-permute-done.16.refs_7_ = bf16[16,1792]{1,0:T(8,128)(2,1)S(1)} collective-permute-done((bf16[16,1792]{1,0:T(8,128)(2,1)S(1)}, bf16[16,1792]{1,0:T(8,128)(2,1)S(1)}, u32[]{:S(2)}, u32[]{:S(2)}) %collective-permute-start.16) | collective-permute-done | bytes 57376 | tf_op jit(solution)/shard_map/ppermute | solution.py:309
  45.7 0.9 %combine.1 = bf16[8,7168]{1,0:T(8,128)(2,1)} custom-call(bf16[96,128]{1,0:T(8,128)(2,1)S(1)} %share.1.share_ref, bf16[16,1792]{1,0:T(8,128)(2,1)S(1)} %get-tuple-element.79.refs_0_, bf16[16,1792]{1,0:T(8,128)(2,1)S(1)} %collective-permute-done.10.refs_1_, bf16[16,1792]{1,0:T(8,128)(2,1)S(1)} %collective-permute-done.11.refs_2_, ...), custom_call_target="tpu_custom_call" | custom-call | flops 100000000 | bytes 1000000 | tf_op jit(solution)/shard_map/combine/pallas_call | solution.py:463
  (38 shorter events, 0.3 us)
Async XLA Ops:
  0.0 0.7 %copy-start = (s32[8,128]{1,0:T(8,128)S(1)}, s32[8,128]{1,0:T(8,128)}, u32[]{:S(2)}) copy-start(s32[8,128]{1,0:T(8,128)} %param.24) | copy-start | bytes 12292
  0.7 1.5 %copy-start.8 = (bf16[1,8,7168]{2,1,0:T(8,128)(2,1)S(1)}, bf16[1,8,7168]{2,1,0:T(8,128)(2,1)}, u32[]{:S(2)}) copy-start(bf16[1,8,7168]{2,1,0:T(8,128)(2,1)} %param.15) | copy-start | bytes 344068
  0.7 14.7 %copy-start.1 = (bf16[1,7168,512]{2,1,0:T(8,128)(2,1)S(1)}, bf16[1,7168,512]{2,1,0:T(8,128)(2,1)}, u32[]{:S(2)}) copy-start(bf16[1,7168,512]{2,1,0:T(8,128)(2,1)} %param.27) | copy-start | bytes 22020100
  0.7 14.7 %copy-start.2 = (bf16[1,7168,512]{2,1,0:T(8,128)(2,1)S(1)}, bf16[1,7168,512]{2,1,0:T(8,128)(2,1)}, u32[]{:S(2)}) copy-start(bf16[1,7168,512]{2,1,0:T(8,128)(2,1)} %param.28) | copy-start | bytes 22020100
  0.7 14.7 %copy-start.3 = (bf16[1,7168,512]{2,1,0:T(8,128)(2,1)S(1)}, bf16[1,7168,512]{2,1,0:T(8,128)(2,1)}, u32[]{:S(2)}) copy-start(bf16[1,7168,512]{2,1,0:T(8,128)(2,1)} %param.18) | copy-start | bytes 22020100
  0.7 14.7 %copy-start.4 = (bf16[1,7168,512]{2,1,0:T(8,128)(2,1)S(1)}, bf16[1,7168,512]{2,1,0:T(8,128)(2,1)}, u32[]{:S(2)}) copy-start(bf16[1,7168,512]{2,1,0:T(8,128)(2,1)} %param.20) | copy-start | bytes 22020100
  2.2 12.6 %collective-permute-start.7 = (bf16[8,7168]{1,0:T(8,128)(2,1)S(1)}, bf16[8,7168]{1,0:T(8,128)(2,1)S(1)}, u32[]{:S(2)}, u32[]{:S(2)}) collective-permute-start(bf16[8,7168]{1,0:T(8,128)(2,1)S(1)} %bitcast.32), channel_id=1, source_target_pairs={{0,1},{1,0},{2,3},{3,2},{4,5},{5,4},{6,7},{7,6},{8,9},{9,8},{10,11... | collective-permute-start | bytes 344072 | tf_op jit(solution)/shard_map/ppermute | solution.py:309
  2.8 7.2 %collective-permute-start = (bf16[16,1792]{1,0:T(8,128)(2,1)S(1)}, bf16[16,1792]{1,0:T(8,128)(2,1)S(1)}, u32[]{:S(2)}, u32[]{:S(2)}) collective-permute-start(bf16[16,1792]{1,0:T(8,128)(2,1)S(1)} %get-tuple-element.48), channel_id=1, source_target_pairs={{0,2},{1,3},{2,0},{3,1},{4,6},{5,7},{6,4},{7,5},{8,10},{9,11},{10,... | collective-permute-start | bytes 172040 | tf_op jit(solution)/shard_map/ppermute | solution.py:309
  5.4 6.3 %collective-permute-start.1 = (bf16[16,1792]{1,0:T(8,128)(2,1)S(1)}, bf16[16,1792]{1,0:T(8,128)(2,1)S(1)}, u32[]{:S(2)}, u32[]{:S(2)}) collective-permute-start(bf16[16,1792]{1,0:T(8,128)(2,1)S(1)} %get-tuple-element.49), channel_id=1, source_target_pairs={{0,4},{1,5},{2,6},{3,7},{4,0},{5,1},{6,2},{7,3},{8,12},{9,13},{10,... | collective-permute-start | bytes 172040 | tf_op jit(solution)/shard_map/ppermute | solution.py:309
  6.9 11.3 %collective-permute-start.2 = (bf16[16,1792]{1,0:T(8,128)(2,1)S(1)}, bf16[16,1792]{1,0:T(8,128)(2,1)S(1)}, u32[]{:S(2)}, u32[]{:S(2)}) collective-permute-start(bf16[16,1792]{1,0:T(8,128)(2,1)S(1)} %get-tuple-element.50), channel_id=1, source_target_pairs={{0,6},{1,7},{2,4},{3,5},{4,2},{5,3},{6,0},{7,1},{8,14},{9,15},{10,... | collective-permute-start | bytes 172040 | tf_op jit(solution)/shard_map/ppermute | solution.py:309
  6.9 11.3 %collective-permute-start.3 = (bf16[16,1792]{1,0:T(8,128)(2,1)S(1)}, bf16[16,1792]{1,0:T(8,128)(2,1)S(1)}, u32[]{:S(2)}, u32[]{:S(2)}) collective-permute-start(bf16[16,1792]{1,0:T(8,128)(2,1)S(1)} %get-tuple-element.51), channel_id=1, source_target_pairs={{0,8},{1,9},{2,10},{3,11},{4,12},{5,13},{6,14},{7,15},{8,0},{9,1},... | collective-permute-start | bytes 172040 | tf_op jit(solution)/shard_map/ppermute | solution.py:309
  9.9 8.7 %collective-permute-start.4 = (bf16[16,1792]{1,0:T(8,128)(2,1)S(1)}, bf16[16,1792]{1,0:T(8,128)(2,1)S(1)}, u32[]{:S(2)}, u32[]{:S(2)}) collective-permute-start(bf16[16,1792]{1,0:T(8,128)(2,1)S(1)} %get-tuple-element.52), channel_id=1, source_target_pairs={{0,10},{1,11},{2,8},{3,9},{4,14},{5,15},{6,12},{7,13},{8,2},{9,3},... | collective-permute-start | bytes 172040 | tf_op jit(solution)/shard_map/ppermute | solution.py:309
  11.7 6.9 %collective-permute-start.5 = (bf16[16,1792]{1,0:T(8,128)(2,1)S(1)}, bf16[16,1792]{1,0:T(8,128)(2,1)S(1)}, u32[]{:S(2)}, u32[]{:S(2)}) collective-permute-start(bf16[16,1792]{1,0:T(8,128)(2,1)S(1)} %get-tuple-element.53), channel_id=1, source_target_pairs={{0,12},{1,13},{2,14},{3,15},{4,8},{5,9},{6,10},{7,11},{8,4},{9,5},... | collective-permute-start | bytes 172040 | tf_op jit(solution)/shard_map/ppermute | solution.py:309
  14.8 7.0 %collective-permute-start.6 = (bf16[16,1792]{1,0:T(8,128)(2,1)S(1)}, bf16[16,1792]{1,0:T(8,128)(2,1)S(1)}, u32[]{:S(2)}, u32[]{:S(2)}) collective-permute-start(bf16[16,1792]{1,0:T(8,128)(2,1)S(1)} %get-tuple-element.54), channel_id=1, source_target_pairs={{0,14},{1,15},{2,12},{3,13},{4,10},{5,11},{6,8},{7,9},{8,6},{9,7},... | collective-permute-start | bytes 172040 | tf_op jit(solution)/shard_map/ppermute | solution.py:309
  16.2 6.1 %copy-start.5 = (bf16[1,512,7168]{2,1,0:T(8,128)(2,1)S(1)}, bf16[1,512,7168]{2,1,0:T(8,128)(2,1)}, u32[]{:S(2)}) copy-start(bf16[1,512,7168]{2,1,0:T(8,128)(2,1)} %param.29) | copy-start | bytes 22020100
  18.2 5.8 %copy-start.6 = (bf16[1,128,512]{2,1,0:T(8,128)(2,1)S(1)}, bf16[1,128,512]{2,1,0:T(8,128)(2,1)}, u32[]{:S(2)}) copy-start(bf16[1,128,512]{2,1,0:T(8,128)(2,1)} %param.25) | copy-start | bytes 393220
  18.2 5.8 %copy-start.7 = (bf16[1,128,512]{2,1,0:T(8,128)(2,1)S(1)}, bf16[1,128,512]{2,1,0:T(8,128)(2,1)}, u32[]{:S(2)}) copy-start(bf16[1,128,512]{2,1,0:T(8,128)(2,1)} %param.26) | copy-start | bytes 393220
  18.2 5.8 %copy-start.9 = (bf16[1,56,512]{2,1,0:T(8,128)(2,1)S(1)}, bf16[1,56,512]{2,1,0:T(8,128)(2,1)}, u32[]{:S(2)}) copy-start(bf16[1,56,512]{2,1,0:T(8,128)(2,1)} %param.19) | copy-start | bytes 172036
  18.2 5.7 %copy-start.10 = (bf16[1,56,512]{2,1,0:T(8,128)(2,1)S(1)}, bf16[1,56,512]{2,1,0:T(8,128)(2,1)}, u32[]{:S(2)}) copy-start(bf16[1,56,512]{2,1,0:T(8,128)(2,1)} %param.21) | copy-start | bytes 172036
  18.2 5.7 %copy-start.11 = (bf16[1,4,7168]{2,1,0:T(4,128)(2,1)S(1)}, bf16[1,4,7168]{2,1,0:T(4,128)(2,1)}, u32[]{:S(2)}) copy-start(bf16[1,4,7168]{2,1,0:T(4,128)(2,1)} %param.23) | copy-start | bytes 172036
  22.1 1.9 %collective-permute-start.8 = (bf16[32,7168]{1,0:T(8,128)(2,1)S(1)}, bf16[32,7168]{1,0:T(8,128)(2,1)S(1)}, u32[]{:S(2)}, u32[]{:S(2)}) collective-permute-start(bf16[32,7168]{1,0:T(8,128)(2,1)S(1)} %unpack.1.refs_0_), channel_id=1, source_target_pairs={{0,1},{1,0},{2,3},{3,2},{4,5},{5,4},{6,7},{7,6},{8,9},{9,8},{10,11... | collective-permute-start | bytes 1376264 | tf_op jit(solution)/shard_map/ppermute | solution.py:309
  28.5 1.9 %collective-permute-start.9 = (bf16[32,7168]{1,0:T(8,128)(2,1)S(1)}, bf16[32,7168]{1,0:T(8,128)(2,1)S(1)}, u32[]{:S(2)}, u32[]{:S(2)}) collective-permute-start(bf16[32,7168]{1,0:T(8,128)(2,1)S(1)} %get-tuple-element.78), channel_id=1, source_target_pairs={{0,1},{1,0},{2,3},{3,2},{4,5},{5,4},{6,7},{7,6},{8,9},{9,8},{10,11... | collective-permute-start | bytes 1376264 | tf_op jit(solution)/shard_map/ppermute | solution.py:309
  28.7 7.6 %collective-permute-start.17 = (bf16[8,7168]{1,0:T(8,128)(2,1)S(1)}, bf16[8,7168]{1,0:T(8,128)(2,1)S(1)}, u32[]{:S(2)}, u32[]{:S(2)}) collective-permute-start(bf16[8,7168]{1,0:T(8,128)(2,1)S(1)} %get-tuple-element.88), channel_id=1, source_target_pairs={{0,1},{1,0},{2,3},{3,2},{4,5},{5,4},{6,7},{7,6},{8,9},{9,8},{10,11... | collective-permute-start | bytes 344072 | tf_op jit(solution)/shard_map/ppermute | solution.py:309
  30.7 6.4 %collective-permute-start.10 = (bf16[16,1792]{1,0:T(8,128)(2,1)S(1)}, bf16[16,1792]{1,0:T(8,128)(2,1)S(1)}, u32[]{:S(2)}, u32[]{:S(2)}) collective-permute-start(bf16[16,1792]{1,0:T(8,128)(2,1)S(1)} %get-tuple-element.80), channel_id=1, source_target_pairs={{0,2},{1,3},{2,0},{3,1},{4,6},{5,7},{6,4},{7,5},{8,10},{9,11},{10,... | collective-permute-start | bytes 172040 | tf_op jit(solution)/shard_map/ppermute | solution.py:309
  31.3 7.4 %collective-permute-start.11 = (bf16[16,1792]{1,0:T(8,128)(2,1)S(1)}, bf16[16,1792]{1,0:T(8,128)(2,1)S(1)}, u32[]{:S(2)}, u32[]{:S(2)}) collective-permute-start(bf16[16,1792]{1,0:T(8,128)(2,1)S(1)} %get-tuple-element.81), channel_id=1, source_target_pairs={{0,4},{1,5},{2,6},{3,7},{4,0},{5,1},{6,2},{7,3},{8,12},{9,13},{10,... | collective-permute-start | bytes 172040 | tf_op jit(solution)/shard_map/ppermute | solution.py:309
  32.4 9.5 %collective-permute-start.12 = (bf16[16,1792]{1,0:T(8,128)(2,1)S(1)}, bf16[16,1792]{1,0:T(8,128)(2,1)S(1)}, u32[]{:S(2)}, u32[]{:S(2)}) collective-permute-start(bf16[16,1792]{1,0:T(8,128)(2,1)S(1)} %get-tuple-element.82), channel_id=1, source_target_pairs={{0,6},{1,7},{2,4},{3,5},{4,2},{5,3},{6,0},{7,1},{8,14},{9,15},{10,... | collective-permute-start | bytes 172040 | tf_op jit(solution)/shard_map/ppermute | solution.py:309
  34.2 8.0 %collective-permute-start.13 = (bf16[16,1792]{1,0:T(8,128)(2,1)S(1)}, bf16[16,1792]{1,0:T(8,128)(2,1)S(1)}, u32[]{:S(2)}, u32[]{:S(2)}) collective-permute-start(bf16[16,1792]{1,0:T(8,128)(2,1)S(1)} %get-tuple-element.83), channel_id=1, source_target_pairs={{0,8},{1,9},{2,10},{3,11},{4,12},{5,13},{6,14},{7,15},{8,0},{9,1},... | collective-permute-start | bytes 172040 | tf_op jit(solution)/shard_map/ppermute | solution.py:309
  36.2 8.7 %collective-permute-start.14 = (bf16[16,1792]{1,0:T(8,128)(2,1)S(1)}, bf16[16,1792]{1,0:T(8,128)(2,1)S(1)}, u32[]{:S(2)}, u32[]{:S(2)}) collective-permute-start(bf16[16,1792]{1,0:T(8,128)(2,1)S(1)} %get-tuple-element.84), channel_id=1, source_target_pairs={{0,10},{1,11},{2,8},{3,9},{4,14},{5,15},{6,12},{7,13},{8,2},{9,3},... | collective-permute-start | bytes 172040 | tf_op jit(solution)/shard_map/ppermute | solution.py:309
  37.1 7.8 %collective-permute-start.15 = (bf16[16,1792]{1,0:T(8,128)(2,1)S(1)}, bf16[16,1792]{1,0:T(8,128)(2,1)S(1)}, u32[]{:S(2)}, u32[]{:S(2)}) collective-permute-start(bf16[16,1792]{1,0:T(8,128)(2,1)S(1)} %get-tuple-element.85), channel_id=1, source_target_pairs={{0,12},{1,13},{2,14},{3,15},{4,8},{5,9},{6,10},{7,11},{8,4},{9,5},... | collective-permute-start | bytes 172040 | tf_op jit(solution)/shard_map/ppermute | solution.py:309
  38.7 7.0 %collective-permute-start.16 = (bf16[16,1792]{1,0:T(8,128)(2,1)S(1)}, bf16[16,1792]{1,0:T(8,128)(2,1)S(1)}, u32[]{:S(2)}, u32[]{:S(2)}) collective-permute-start(bf16[16,1792]{1,0:T(8,128)(2,1)S(1)} %get-tuple-element.86), channel_id=1, source_target_pairs={{0,14},{1,15},{2,12},{3,13},{4,10},{5,11},{6,8},{7,9},{8,6},{9,7},... | collective-permute-start | bytes 172040 | tf_op jit(solution)/shard_map/ppermute | solution.py:309
